TPU v7x, 32 devices: a whole 2x2x4 slice. The times are simulated.
32 devices in a mesh: cuts: 8 (over y, x, core), fsdp: 4 (over z).
Axes of the slice: x: 2, y: 2, z: 4, core: 2. Of those that a mesh axis runs over, the one named last changes fastest.
Arguments:
- source_ids: int32 [64, 512], P(('cuts', 'fsdp')), may hold values from 0 to 32127
- targets: int32 [64, 128], P(('cuts', 'fsdp')), may hold values from 0 to 32127
- source_lengths: int32 [64], P(('cuts', 'fsdp')), may hold values from 1 to 512, as said below
- target_lengths: int32 [64], P(('cuts', 'fsdp')), may hold values from 1 to 128, as said below
- task_ids: int32 [8], replicated, may hold values from 0 to 7
- task_counts: int32 [8], replicated, may hold values from 1 to 999
- blocks: float32 [768, 28, 768], P('cuts', None, 'fsdp'), may hold values from -0.57735027 to 0.57735027
- blocks_momentum: float32 [768, 28, 768], P('cuts', None, 'fsdp'), may hold values from -1.335144e-05 to 1.335144e-05
- embedding: float32 [32128, 768], P('fsdp', 'cuts'), may hold values from -12 to 12
- embed_momentum: float32 [32128, 768], P('fsdp', 'cuts'), may hold values from -2.9802322e-07 to 2.9802322e-07
- gain_rows: float32 [7, 768], replicated, may hold values from 0.4 to 2.4
- gain_momentum: float32 [7, 768], replicated, may hold values from -5.340576e-05 to 5.340576e-05
- position_bias: float32 [2, 32, 12], replicated, may hold values from -4 to 4
- bias_momentum: float32 [2, 32, 12], replicated, may hold values from -5.340576e-05 to 5.340576e-05
- right_blocks: float32 [28, 768, 8], P(None, 'fsdp'), may hold values from -6 to 6
- right_embed: float32 [32128, 8], P('fsdp'), may hold values from -6 to 6
- error_blocks: float32 [8, 768, 28, 768], P('cuts', None, None, 'fsdp'), may hold values from -0.0012207031 to 0.0012207031
- error_embed: float32 [8, 32128, 768], P('cuts', 'fsdp'), may hold values from -0.0012207031 to 0.0012207031
Outputs:
- loss_total: float32 [], replicated
- loss_count: float32 [], replicated
- grad_norm: float32 [], replicated
- blocks_new: float32 [768, 28, 768], P('cuts', None, 'fsdp')
- momentum_blocks: float32 [768, 28, 768], P('cuts', None, 'fsdp')
- embedding_new: float32 [32128, 768], P('fsdp', 'cuts')
- momentum_embed: float32 [32128, 768], P('fsdp', 'cuts')
- gains_new: float32 [7, 768], replicated
- momentum_gains: float32 [7, 768], replicated
- bias_new: float32 [2, 32, 12], replicated
- momentum_bias: float32 [2, 32, 12], replicated
- factors_blocks: float32 [28, 768, 8], P(None, 'fsdp')
- factors_embed: float32 [32128, 8], P('fsdp')
- errors_blocks: float32 [8, 768, 28, 768], P('cuts', None, None, 'fsdp')
- errors_embed: float32 [8, 32128, 768], P('cuts', 'fsdp')
Inputs may be any that keep to these rules, and one draw needn't show every extreme that they name: `source_lengths`: one sequence has all 512 positions real in every draw. `target_lengths`: one sequence has all 128 positions real in every draw.
All inputs are finite; a program needn't handle non-finite values.
Results may differ from a plain program's by a relative error of at most 0.024.
The roundings to bfloat16 on the way count: a program that leaves them out, or rounds other values in their place, can miss the bound.
Values may be sent and summed in bfloat16 or wider, within the bound.
No kernel may reach another device: no remote copies, remote signals or barrier semaphores. Data moves between devices by JAX's collectives and lax.ppermute only.
A program may use at most 384 MiB of HBM per device.

v0:
```python
import math

import jax
import jax.numpy as jnp
from jax import lax
from jax.sharding import PartitionSpec as P

MODEL_WIDTH = 768
H = 12
DH = 64
FEED_UNITS = 3072
NBK = 32
TASKS = 8
PARAMS = 41189376


EPSILON = 1e-06
MASKED = -1000000000.0
CLIP_NORM = 0.05
MOMENTUM_DECAY = 0.9
STEP_RATE = 5.0
EMBED_SHARE = 50.0
SMALL_SHARE = 1.0 / 7.0
TOP_PRECISION = lax.Precision.HIGHEST
ENCODER_EDGES = (12, 16, 23, 32, 46, 64, 91)
DECODER_EDGES = (19, 21, 24, 27, 31, 35, 40, 46, 52, 59, 67, 77, 87, 99, 113)


def merged(part, axis, combine):
    gathered = jax.tree.map(lambda a: lax.all_gather(a, axis), part)

    def take(source):
        return jax.tree.map(lambda a: lax.dynamic_index_in_dim(a, source, 0, False), gathered)

    return lax.fori_loop(
        1, lax.axis_size(axis), lambda source, state: combine(state, take(source)), take(0)
    )


def root_norm(stream, gain_row):
    return (
        stream * lax.rsqrt(jnp.mean(stream * stream, axis=-1, keepdims=True) + EPSILON) * gain_row
    )


def norm_backward(stream, gain_row, grad_normed):
    _, pull_back = jax.vjp(root_norm, stream, gain_row)
    return pull_back(grad_normed)


def bucket_table(length, causal):
    places = jnp.arange(length, dtype=jnp.int32)
    offset = places[None, :] - places[:, None]
    if causal:
        distance = jnp.maximum(-offset, 0)
        farther = 16 + sum(((distance >= boundary).astype(jnp.int32) for boundary in DECODER_EDGES))
        bucket = jnp.where(distance < 16, distance, farther)
    else:
        distance = jnp.abs(offset)
        farther = 8 + sum(((distance >= boundary).astype(jnp.int32) for boundary in ENCODER_EDGES))
        bucket = jnp.where(distance < 8, distance, farther) + jnp.where(offset > 0, 16, 0)
    return (bucket[:, :, None] == jnp.arange(NBK, dtype=jnp.int32)[None, None, :]).astype(
        jnp.float32
    )


def orthonormal(factor):
    gram_matrix = jnp.einsum("...nr,...ns->...rs", factor, factor, precision=TOP_PRECISION)
    cholesky_factor = jnp.linalg.cholesky(gram_matrix)
    return lax.linalg.triangular_solve(
        cholesky_factor, factor, left_side=False, lower=True, transpose_a=True
    )


def split_heads(tensor):
    return tensor.reshape(tensor.shape[0], tensor.shape[1], H, DH)


def keep_rows(key_ok, query_len, causal):
    keep_mask = jnp.broadcast_to(key_ok[None, :], (query_len, key_ok.shape[0]))
    if causal:
        places = jnp.arange(query_len, dtype=jnp.int32)
        keep_mask = keep_mask & (places[None, :] <= places[:, None])
    return keep_mask


def score_probs(queries, key_rows, key_ok, causal, bias_table):
    scores = (
        jnp.einsum("qhd,khd->hqk", queries, key_rows, preferred_element_type=jnp.float32)
        + bias_table
    )
    scores = jnp.where(keep_rows(key_ok, queries.shape[0], causal)[None], scores, MASKED)
    return jax.nn.softmax(scores, axis=-1)


def attend_forward(queries, key_rows, value_rows, key_ok, causal, bias_table):
    weights = score_probs(queries, key_rows, key_ok, causal, bias_table)
    return jnp.einsum(
        "hqk,khd->qhd", weights.astype(jnp.bfloat16), value_rows, preferred_element_type=jnp.float32
    ).astype(jnp.bfloat16)


def attend_backward(queries, key_rows, value_rows, key_ok, grad_out, causal, bias_table, hot_table):
    weights = score_probs(queries, key_rows, key_ok, causal, bias_table)
    grad_weights = jnp.einsum(
        "qhd,khd->hqk", grad_out, value_rows, preferred_element_type=jnp.float32
    )
    grad_scores = (
        weights * (grad_weights - jnp.sum(weights * grad_weights, axis=-1, keepdims=True))
    ).astype(jnp.bfloat16)
    grad_queries = jnp.einsum(
        "hqk,khd->qhd", grad_scores, key_rows, preferred_element_type=jnp.float32
    ).astype(jnp.bfloat16)
    grad_keys = jnp.einsum(
        "hqk,qhd->khd", grad_scores, queries, preferred_element_type=jnp.float32
    ).astype(jnp.bfloat16)
    grad_values = jnp.einsum(
        "hqk,qhd->khd", weights.astype(jnp.bfloat16), grad_out, preferred_element_type=jnp.float32
    ).astype(jnp.bfloat16)
    if hot_table is None:
        grad_bias = jnp.zeros((NBK, H), jnp.float32)
    else:
        grad_bias = jnp.einsum(
            "hqk,qkb->bh", grad_scores, hot_table, preferred_element_type=jnp.float32
        )
    return (grad_queries, grad_keys, grad_values, grad_bias)


def attention_forward(stream, gain_row, source, matrices, key_ok, causal, bias_table):
    norm_output = root_norm(stream, gain_row).astype(jnp.bfloat16)
    context = norm_output if source is None else source
    batch_size, row_count = (stream.shape[0], stream.shape[1])
    queries = split_heads(
        jnp.dot(norm_output, matrices[:, 0], preferred_element_type=jnp.float32).astype(
            jnp.bfloat16
        )
    )
    key_rows = split_heads(
        jnp.dot(context, matrices[:, 1], preferred_element_type=jnp.float32).astype(jnp.bfloat16)
    )
    value_rows = split_heads(
        jnp.dot(context, matrices[:, 2], preferred_element_type=jnp.float32).astype(jnp.bfloat16)
    )
    attended = lax.map(
        lambda members: attend_forward(
            members[0], members[1], members[2], members[3], causal, bias_table
        ),
        (queries, key_rows, value_rows, key_ok),
    )
    attended = attended.reshape(batch_size, row_count, MODEL_WIDTH)
    branch = jnp.dot(attended, matrices[:, 3], preferred_element_type=jnp.float32)
    return (stream + branch, (norm_output, queries, key_rows, value_rows, attended))


def attention_backward(
    grad_stream, stream, gain_row, source, matrices, saved, key_ok, causal, bias_table, hot_table
):
    norm_output, queries, key_rows, value_rows, attended = saved
    batch_size, row_count = (stream.shape[0], stream.shape[1])
    grad_branch = grad_stream.astype(jnp.bfloat16)
    grad_outward = jnp.einsum(
        "sqd,sqe->de", attended, grad_branch, preferred_element_type=jnp.float32
    )
    grad_attended = split_heads(
        jnp.einsum(
            "sqe,de->sqd", grad_branch, matrices[:, 3], preferred_element_type=jnp.float32
        ).astype(jnp.bfloat16)
    )
    grad_queries, grad_keys, grad_values, grad_bias = lax.map(
        lambda members: attend_backward(
            members[0],
            members[1],
            members[2],
            members[3],
            members[4],
            causal,
            bias_table,
            hot_table,
        ),
        (queries, key_rows, value_rows, key_ok, grad_attended),
    )
    grad_queries = grad_queries.reshape(batch_size, row_count, MODEL_WIDTH)
    grad_keys = grad_keys.reshape(batch_size, -1, MODEL_WIDTH)
    grad_values = grad_values.reshape(batch_size, -1, MODEL_WIDTH)
    context = norm_output if source is None else source
    grad_matrices = jnp.stack(
        [
            jnp.einsum(
                "sqd,sqe->de", norm_output, grad_queries, preferred_element_type=jnp.float32
            ),
            jnp.einsum("skd,ske->de", context, grad_keys, preferred_element_type=jnp.float32),
            jnp.einsum("skd,ske->de", context, grad_values, preferred_element_type=jnp.float32),
            grad_outward,
        ],
        axis=1,
    )
    grad_normed = jnp.einsum(
        "sqe,de->sqd", grad_queries, matrices[:, 0], preferred_element_type=jnp.float32
    )
    grad_context = jnp.einsum(
        "ske,de->skd", grad_keys, matrices[:, 1], preferred_element_type=jnp.float32
    ) + jnp.einsum("ske,de->skd", grad_values, matrices[:, 2], preferred_element_type=jnp.float32)
    if source is None:
        grad_normed = grad_normed + grad_context
    grad_input, grad_gain = norm_backward(stream, gain_row, grad_normed)
    return (
        grad_stream + grad_input,
        grad_gain,
        grad_matrices,
        jnp.sum(grad_bias, axis=0),
        grad_context,
    )


def feed_forward(stream, gain_row, nested_layer_blocks, outer_blocks):
    norm_output = root_norm(stream, gain_row).astype(jnp.bfloat16)
    prior_input = jnp.einsum(
        "cxp,pi->cxi",
        norm_output,
        nested_layer_blocks.reshape(MODEL_WIDTH, FEED_UNITS),
        preferred_element_type=jnp.float32,
    )
    hidden = jax.nn.gelu(prior_input).astype(jnp.bfloat16)
    shaped = hidden.reshape(stream.shape[0], stream.shape[1], 4, MODEL_WIDTH)
    branch = jnp.einsum("sljd,dje->sle", shaped, outer_blocks, preferred_element_type=jnp.float32)
    return (stream + branch, (norm_output, prior_input, hidden))


def feed_backward(grad_stream, stream, gain_row, nested_layer_blocks, outer_blocks, saved):
    norm_output, prior_input, hidden = saved
    batch_size, row_count = (stream.shape[0], stream.shape[1])
    grad_branch = grad_stream.astype(jnp.bfloat16)
    shaped = hidden.reshape(batch_size, row_count, 4, MODEL_WIDTH)
    grad_outer = jnp.einsum(
        "sljd,sle->dje", shaped, grad_branch, preferred_element_type=jnp.float32
    )
    grad_hidden = jnp.einsum(
        "sle,dje->sljd", grad_branch, outer_blocks, preferred_element_type=jnp.float32
    ).reshape(batch_size, row_count, FEED_UNITS)
    _, pull_back = jax.vjp(jax.nn.gelu, prior_input)
    prior_input_gradient = pull_back(grad_hidden)[0].astype(jnp.bfloat16)
    grad_inner = jnp.einsum(
        "zbj,zbh->jh", norm_output, prior_input_gradient, preferred_element_type=jnp.float32
    ).reshape(MODEL_WIDTH, 4, MODEL_WIDTH)
    grad_normed = jnp.einsum(
        "mjc,uc->mju",
        prior_input_gradient,
        nested_layer_blocks.reshape(MODEL_WIDTH, FEED_UNITS),
        preferred_element_type=jnp.float32,
    )
    grad_input, grad_gain = norm_backward(stream, gain_row, grad_normed)
    return (grad_stream + grad_input, grad_gain, jnp.concatenate([grad_inner, grad_outer], axis=1))


def encoder_forward(stream, gain_rows, weights, source_ok, bias_source):
    after_attention, saved_attention = attention_forward(
        stream, gain_rows[0], None, weights[:, 0:4], source_ok, False, bias_source
    )
    after_feed, saved_feed = feed_forward(
        after_attention, gain_rows[1], weights[:, 4:8], weights[:, 8:12]
    )
    encoded = root_norm(after_feed, gain_rows[2]).astype(jnp.bfloat16)
    return (encoded, (stream, saved_attention, after_attention, saved_feed, after_feed))


def encoder_backward(grad_encoded, gain_rows, weights, saved, source_ok, bias_source, hot_source):
    stream, saved_attention, after_attention, saved_feed, after_feed = saved
    grad_stream, gain_final = norm_backward(after_feed, gain_rows[2], grad_encoded)
    grad_stream, gain_feed, grad_feed = feed_backward(
        grad_stream, after_attention, gain_rows[1], weights[:, 4:8], weights[:, 8:12], saved_feed
    )
    grad_stream, gain_self, grad_self, grad_table, _ = attention_backward(
        grad_stream,
        stream,
        gain_rows[0],
        None,
        weights[:, 0:4],
        saved_attention,
        source_ok,
        False,
        bias_source,
        hot_source,
    )
    return (
        grad_stream,
        jnp.stack([gain_self, gain_feed, gain_final]),
        jnp.concatenate([grad_self, grad_feed], axis=1),
        grad_table,
    )


def decoder_forward(stream, gain_rows, weights, target_ok, source_ok, bias_target, encoded):
    after_self, saved_self = attention_forward(
        stream, gain_rows[3], None, weights[:, 0:4], target_ok, True, bias_target
    )
    after_cross, saved_cross = attention_forward(
        after_self, gain_rows[4], encoded, weights[:, 4:8], source_ok, False, 0.0
    )
    after_feed, saved_feed = feed_forward(
        after_cross, gain_rows[5], weights[:, 8:12], weights[:, 12:16]
    )
    final_rows = (root_norm(after_feed, gain_rows[6]) * MODEL_WIDTH ** (-0.5)).astype(jnp.bfloat16)
    return (
        final_rows,
        (stream, saved_self, after_self, saved_cross, after_cross, saved_feed, after_feed),
    )


def decoder_backward(
    grad_final, gain_rows, weights, saved, target_ok, source_ok, bias_target, hot_target, encoded
):
    stream, saved_self, after_self, saved_cross, after_cross, saved_feed, after_feed = saved
    grad_stream, gain_final = norm_backward(after_feed, gain_rows[6], grad_final)
    grad_stream, gain_feed, grad_feed = feed_backward(
        grad_stream, after_cross, gain_rows[5], weights[:, 8:12], weights[:, 12:16], saved_feed
    )
    grad_stream, gain_cross, grad_cross, _, grad_encoded = attention_backward(
        grad_stream,
        after_self,
        gain_rows[4],
        encoded,
        weights[:, 4:8],
        saved_cross,
        source_ok,
        False,
        0.0,
        None,
    )
    grad_stream, gain_self, grad_self, grad_table, _ = attention_backward(
        grad_stream,
        stream,
        gain_rows[3],
        None,
        weights[:, 0:4],
        saved_self,
        target_ok,
        True,
        bias_target,
        hot_target,
    )
    gains_grad = jnp.stack([gain_self, gain_cross, gain_feed, gain_final])
    return (
        grad_stream,
        grad_encoded,
        gains_grad,
        jnp.concatenate([grad_self, grad_cross, grad_feed], axis=1),
        grad_table,
    )


def gather_layer(part_weights):
    return lax.all_gather(part_weights, "fsdp", axis=2, tiled=True)


def regather_layer(part_weights):
    return lax.all_gather(part_weights, "fsdp", axis=2, tiled=True)


def reduce_layer(part_grads):
    return lax.psum_scatter(
        part_grads.astype(jnp.bfloat16), "fsdp", scatter_dimension=2, tiled=True
    ).astype(jnp.float32)


def local(
    source_ids,
    targets,
    source_lengths,
    target_lengths,
    task_ids,
    task_counts,
    blocks,
    blocks_momentum,
    embedding,
    embed_momentum,
    gain_rows,
    gain_momentum,
    position_bias,
    bias_momentum,
    right_blocks,
    right_embed,
    error_blocks,
    error_embed,
):
    fsdp_rank = lax.axis_index("fsdp")
    cuts_rank = lax.axis_index("cuts")
    cuts_count = lax.axis_size("cuts")
    seq_count, source_len = source_ids.shape
    target_len = targets.shape[1]
    block_shard, vocab_shard = (
        lax.all_gather(blocks.astype(jnp.bfloat16), "cuts", axis=0, tiled=True),
        lax.all_gather(embedding.astype(jnp.bfloat16), "cuts", axis=1, tiled=True),
    )
    total_count = lax.psum(jnp.sum(target_lengths).astype(jnp.float32), ("cuts", "fsdp"))
    chosen = jnp.sum(
        jnp.where(
            task_ids[:, None] == jnp.arange(TASKS, dtype=jnp.int32)[None, :],
            task_counts[None, :],
            0,
        ),
        axis=1,
    ).astype(jnp.float32)
    slice_weight = jnp.sum(
        jnp.where(
            jnp.arange(cuts_count, dtype=jnp.int32) == cuts_rank,
            cuts_count * chosen / jnp.sum(chosen),
            0.0,
        )
    )
    group_source, group_target, group_lengths = (
        lax.all_gather(source_ids, "fsdp", axis=0, tiled=True),
        lax.all_gather(targets, "fsdp", axis=0, tiled=True),
        lax.all_gather(target_lengths, "fsdp", axis=0, tiled=True),
    )
    group_input = jnp.concatenate(
        [jnp.zeros_like(group_target[:, :1]), group_target[:, :-1]], axis=1
    )
    vocab_rows = vocab_shard.shape[0]
    vocab_start = fsdp_rank * vocab_rows

    def shard_lookup(token_ids):
        local_ids = token_ids - vocab_start
        inside = (local_ids >= 0) & (local_ids < vocab_rows)
        picked_rows = jnp.take(vocab_shard, jnp.clip(local_ids, 0, vocab_rows - 1), axis=0)
        return jnp.where(inside[..., None], picked_rows.astype(jnp.float32), 0.0)

    def scatter_rows(accumulated, token_ids, rows_grad):
        local_ids = token_ids - vocab_start
        inside = (local_ids >= 0) & (local_ids < vocab_rows)
        flattened = jnp.where(inside[..., None], rows_grad, 0.0).reshape(-1, MODEL_WIDTH)
        return accumulated.at[jnp.clip(local_ids, 0, vocab_rows - 1).reshape(-1)].add(flattened)

    source_stream, target_stream = (
        lax.psum_scatter(
            shard_lookup(group_source).astype(jnp.bfloat16), "fsdp", scatter_dimension=0, tiled=True
        ).astype(jnp.float32),
        lax.psum_scatter(
            shard_lookup(group_input).astype(jnp.bfloat16), "fsdp", scatter_dimension=0, tiled=True
        ).astype(jnp.float32),
    )
    source_ok = jnp.arange(source_len, dtype=jnp.int32)[None, :] < source_lengths[:, None]
    target_ok = jnp.arange(target_len, dtype=jnp.int32)[None, :] < target_lengths[:, None]
    hot_source = bucket_table(source_len, False)
    hot_target = bucket_table(target_len, True)
    bias_source = jnp.einsum("ijb,bh->hij", hot_source, position_bias[0], precision=TOP_PRECISION)
    bias_target = jnp.einsum("ijb,bh->hij", hot_target, position_bias[1], precision=TOP_PRECISION)
    encoder_weights = gather_layer(block_shard[:, :12])
    encoded, encoder_saved = encoder_forward(
        source_stream, gain_rows, encoder_weights, source_ok, bias_source
    )
    decoder_weights = gather_layer(block_shard[:, 12:])
    final_rows, decoder_saved = decoder_forward(
        target_stream, gain_rows, decoder_weights, target_ok, source_ok, bias_target, encoded
    )
    head_rows = lax.all_gather(final_rows.reshape(-1, MODEL_WIDTH), "fsdp", axis=0, tiled=True)
    block_rows = math.gcd(512, head_rows.shape[0])
    blocked_rows = head_rows.reshape(-1, block_rows, MODEL_WIDTH)
    blocked_ids = group_target.reshape(-1, block_rows)
    group_mask = (
        (jnp.arange(target_len, dtype=jnp.int32)[None, :] < group_lengths[:, None])
        .reshape(-1)
        .astype(jnp.float32)
    )

    def local_stats(members):
        logits = jnp.einsum(
            "rd,vd->rv", members[0], vocab_shard, preferred_element_type=jnp.float32
        )
        highest = jnp.max(logits, axis=1)
        total_exp = jnp.sum(jnp.exp(logits - highest[:, None]), axis=1)
        picked = jnp.sum(
            jnp.where(
                jnp.arange(vocab_rows, dtype=jnp.int32)[None, :]
                == (members[1] - vocab_start)[:, None],
                logits,
                0.0,
            ),
            axis=1,
        )
        return (highest, total_exp, picked)

    def join_stats(first, second):
        highest = jnp.maximum(first[0], second[0])
        return (
            highest,
            first[1] * jnp.exp(first[0] - highest) + second[1] * jnp.exp(second[0] - highest),
            first[2] + second[2],
        )

    highest, total_exp, picked = lax.map(local_stats, (blocked_rows, blocked_ids))
    highest, total_exp, picked = merged((highest, total_exp, picked), "fsdp", join_stats)
    log_total = highest + jnp.log(total_exp)
    token_loss = (log_total - picked).reshape(-1) * group_mask
    own_loss = lax.dynamic_slice_in_dim(
        token_loss, fsdp_rank * seq_count * target_len, seq_count * target_len
    )
    loss_local = jnp.sum(own_loss) * slice_weight
    token_weight = (group_mask * (slice_weight / total_count)).reshape(-1, block_rows)

    def head_back(grad_vocab, members):
        row_block, ids_block, log_block, weight_block = members
        logits = jnp.einsum("rd,vd->rv", row_block, vocab_shard, preferred_element_type=jnp.float32)
        target_hit = (
            jnp.arange(vocab_rows, dtype=jnp.int32)[None, :] == (ids_block - vocab_start)[:, None]
        ).astype(jnp.float32)
        grad_logits = (
            (jnp.exp(logits - log_block[:, None]) - target_hit) * weight_block[:, None]
        ).astype(jnp.bfloat16)
        grad_rows = jnp.einsum(
            "rv,vd->rd", grad_logits, vocab_shard, preferred_element_type=jnp.float32
        )
        return (
            grad_vocab
            + jnp.einsum("rv,rd->vd", grad_logits, row_block, preferred_element_type=jnp.float32),
            grad_rows,
        )

    grad_vocab, grad_rows = lax.scan(
        head_back,
        jnp.zeros((vocab_rows, MODEL_WIDTH), jnp.float32),
        (blocked_rows, blocked_ids, log_total, token_weight),
    )
    grad_final = lax.psum_scatter(
        grad_rows.reshape(-1, MODEL_WIDTH), "fsdp", scatter_dimension=0, tiled=True
    ).reshape(seq_count, target_len, MODEL_WIDTH) * MODEL_WIDTH ** (-0.5)
    decoder_weights = regather_layer(block_shard[:, 12:])
    input_grad, encoded_grad, decoder_gains, decoder_grads, decoder_table = decoder_backward(
        grad_final,
        gain_rows,
        decoder_weights,
        decoder_saved,
        target_ok,
        source_ok,
        bias_target,
        hot_target.astype(jnp.bfloat16),
        encoded,
    )
    decoder_grads = reduce_layer(decoder_grads)
    encoder_weights = regather_layer(block_shard[:, :12])
    source_grad, encoder_gains, encoder_grads, encoder_table = encoder_backward(
        encoded_grad,
        gain_rows,
        encoder_weights,
        encoder_saved,
        source_ok,
        bias_source,
        hot_source.astype(jnp.bfloat16),
    )
    block_grads = jnp.concatenate([reduce_layer(encoder_grads), decoder_grads], axis=1)
    group_source_grad, group_input_grad = (
        lax.all_gather(source_grad.astype(jnp.bfloat16), "fsdp", axis=0, tiled=True).astype(
            source_grad.dtype
        ),
        lax.all_gather(input_grad.astype(jnp.bfloat16), "fsdp", axis=0, tiled=True).astype(
            input_grad.dtype
        ),
    )
    grad_vocab = scatter_rows(
        scatter_rows(grad_vocab, group_source, group_source_grad), group_input, group_input_grad
    )
    left_blocks = error_blocks[0] + block_grads
    left_embed = error_embed[0] + grad_vocab
    left_factor = jnp.einsum("ikj,kjr->kir", left_blocks, right_blocks, precision=TOP_PRECISION)
    embed_factor = jnp.einsum("vd,vr->dr", left_embed, right_embed, precision=TOP_PRECISION)
    gains_grad = jnp.concatenate([encoder_gains, decoder_gains], axis=0)
    table_grad = jnp.stack([encoder_table, decoder_table])
    left_factor, embed_factor, gains_grad, table_grad, loss_total = lax.psum(
        (left_factor, embed_factor, gains_grad, table_grad, loss_local), ("cuts", "fsdp")
    )
    left_factor = orthonormal(left_factor)
    embed_factor = orthonormal(embed_factor)
    factors_blocks = jnp.einsum("ikj,kir->kjr", left_blocks, left_factor, precision=TOP_PRECISION)
    factors_embed = jnp.einsum("vd,dr->vr", left_embed, embed_factor, precision=TOP_PRECISION)
    factors_blocks, factors_embed = (
        lax.psum(factors_blocks.astype(jnp.bfloat16), "cuts").astype(jnp.float32),
        lax.psum(factors_embed.astype(jnp.bfloat16), "cuts").astype(jnp.float32),
    )
    full_blocks = jnp.einsum("kir,kjr->ikj", left_factor, factors_blocks, precision=TOP_PRECISION)
    full_embed = jnp.einsum("vr,dr->vd", factors_embed, embed_factor, precision=TOP_PRECISION)
    owned_rows = blocks.shape[0]
    owned_columns = embedding.shape[1]
    own_blocks = lax.dynamic_slice_in_dim(full_blocks, cuts_rank * owned_rows, owned_rows, 0)
    own_embed = lax.dynamic_slice_in_dim(full_embed, cuts_rank * owned_columns, owned_columns, 1)
    small_squares = jnp.sum(gains_grad * gains_grad) + jnp.sum(table_grad * table_grad)
    squares = lax.psum(
        jnp.sum(own_blocks * own_blocks) + jnp.sum(own_embed * own_embed), ("cuts", "fsdp")
    )
    grad_norm = jnp.sqrt(squares + small_squares)
    clip_factor = jnp.minimum(1.0, CLIP_NORM / grad_norm)
    step_size = STEP_RATE * math.sqrt(PARAMS / MODEL_WIDTH) / CLIP_NORM
    embed_step = step_size * EMBED_SHARE * math.sqrt(MODEL_WIDTH)
    small_step = step_size * SMALL_SHARE * math.sqrt(MODEL_WIDTH)
    momentum_blocks = MOMENTUM_DECAY * blocks_momentum + (1.0 - MOMENTUM_DECAY) * (
        clip_factor * own_blocks
    )
    momentum_embed = MOMENTUM_DECAY * embed_momentum + (1.0 - MOMENTUM_DECAY) * (
        clip_factor * own_embed
    )
    momentum_gains = MOMENTUM_DECAY * gain_momentum + (1.0 - MOMENTUM_DECAY) * (
        clip_factor * gains_grad
    )
    momentum_bias = MOMENTUM_DECAY * bias_momentum + (1.0 - MOMENTUM_DECAY) * (
        clip_factor * table_grad
    )
    return (
        loss_total,
        total_count,
        grad_norm,
        blocks - step_size * momentum_blocks,
        momentum_blocks,
        embedding - embed_step * momentum_embed,
        momentum_embed,
        gain_rows - small_step * momentum_gains,
        momentum_gains,
        position_bias - small_step * momentum_bias,
        momentum_bias,
        factors_blocks,
        factors_embed,
        (left_blocks - full_blocks)[None],
        (left_embed - full_embed)[None],
    )


def solution(mesh):
    return jax.shard_map(
        local,
        mesh=mesh,
        in_specs=(
            P(("cuts", "fsdp"), None),
            P(("cuts", "fsdp"), None),
            P(("cuts", "fsdp")),
            P(("cuts", "fsdp")),
            P(),
            P(),
            P("cuts", None, "fsdp"),
            P("cuts", None, "fsdp"),
            P("fsdp", "cuts"),
            P("fsdp", "cuts"),
            P(),
            P(),
            P(),
            P(),
            P(None, "fsdp", None),
            P("fsdp", None),
            P("cuts", None, None, "fsdp"),
            P("cuts", "fsdp", None),
        ),
        out_specs=(
            P(),
            P(),
            P(),
            P("cuts", None, "fsdp"),
            P("cuts", None, "fsdp"),
            P("fsdp", "cuts"),
            P("fsdp", "cuts"),
            P(),
            P(),
            P(),
            P(),
            P(None, "fsdp", None),
            P("fsdp", None),
            P("cuts", None, None, "fsdp"),
            P("cuts", "fsdp", None),
        ),
        check_vma=False,
    )
```

profile of v0, /device:TPU:0, one launch (start us, length us, event | category | flops | bytes accessed | tf_op | source)
XLA Modules:
  0.0 2668.0 jit_solution(13977428175561192164)
XLA Ops:
  12.0 12.6 all-gather.3
  25.9 58.8 %all-gather.16.cloned.1.call-done = bf16[8032,768]{0,1:T(8,128)(2,1)} async-done(((bf16[8032,96]{0,1:T(8,128)(2,1)}), bf16[8032,768]{0,1:T(8,128)(2,1)}) %all-gather.16.cloned.1.call-update) | async-done | bytes 12337168 | tf_op jit(solution)/shard_map/all_gather | solution.py:392
  84.8 16.7 copy.757
  113.6 13.1 all-gather.4
  126.9 25.3 gather_fusion.1
  186.2 14.0 fusion.201
  200.3 17.5 copy.780
  223.9 79.0 %reduce-scatter.8.cloned.1.call-done = bf16[2,512,768]{2,1,0:T(8,128)(2,1)} async-done(((bf16[8,512,768]{2,1,0:T(8,128)(2,1)}), bf16[2,512,768]{2,1,0:T(8,128)(2,1)}) %reduce-scatter.8.cloned.1.call-update) | async-done | bytes 1572880 | tf_op jit(solution)/shard_map/reduce_scatter | solution.py:434
  305.3 243.5 %all-gather.22.cloned.1.call-done = bf16[768,12,768]{0,2,1:T(8,128)(2,1)} async-done(((bf16[768,12,192]{0,2,1:T(8,128)(2,1)}), bf16[768,12,768]{0,2,1:T(8,128)(2,1)}) %all-gather.22.cloned.1.call-update) | async-done | bytes 14155792 | tf_op jit(solution)/shard_map/all_gather | solution.py:352
  572.1 64.3 %while.134 = (s32[]{:T(128)}, bf16[2,512,12,64]{1,3,2,0:T(8,128)(2,1)}, bf16[2,512,12,64]{1,3,2,0:T(8,128)(2,1)}, pred[2,512]{1,0:T(4,128)(4,1)S(1)}, bf16[2,512...) while((s32[]{:T(128)}, ...), condition=%wide.region_12.13_spmd.clone, body=%wide.region_9.12_spmd.sunk.clone | while | flops 827726848 | bytes 66113104 | solution.py:144
  592.0 12.6 fusion.637
  664.7 206.3 %all-gather.20.cloned.1.call-done = bf16[768,16,768]{0,1,2:T(8,128)(2,1)} async-done(((bf16[768,16,192]{0,1,2:T(8,128)(2,1)}), bf16[768,16,768]{0,1,2:T(8,128)(2,1)}) %all-gather.20.cloned.1.call-update) | async-done | bytes 18874384 | tf_op jit(solution)/shard_map/all_gather | solution.py:352
  871.0 34.2 %fusion.387 = (bf16[768,1,768]{0,1,2:T(2,128)(2,1)}, bf16[768,1,768]{0,1,2:T(2,128)(2,1)S(1)}, bf16[768,1,768]{0,1,2:T(2,128)(2,1)}, bf16[768,1,768]{0,1,2:T(2,1...) fusion(bf16[768,16,768]{0,1,2:T(8,128)(2,1)} %all-gather.20.clo, ...), kind=kLoop, calls=%fused_computation.586 | loop fusion | bytes 18874368 | tf_op jit(solution)/shard_map/slice | solution.py:151
  1030.3 41.4 %psum.64 = f32[]{:T(128)} all-reduce(f32[]{:T(128)S(6)} %convert_element_type.507), channel_id=1, replica_groups=mesh['cuts'=8,'fsdp'=4] {'cuts','fsdp'}, use_global_device_ids=true, to_apply=%region_34.35 | all-reduce | flops 1 | bytes 8 | tf_op jit(solution)/shard_map/psum | solution.py:394
  1083.0 28.7 %while.136 = (s32[]{:T(128)}, f32[2,512]{1,0:T(2,128)S(1)}, f32[2,512]{1,0:T(2,128)S(1)}, f32[2,512]{1,0:T(2,128)S(1)}, bf16[2,512,768]{2,1,0:T(8,128)(2,1)}, /*...) while((s32[]{:T(128)}, f32[2,512]{1,0:T(2,128)S(1)}, f32[2,512]{1,0:T(2,128)S(1)}, ...), condition=%wide.region_25.26_spmd.clone, body=%wide.region_21.25_spmd.sunk.clone | while | flops 6341295104 | bytes 46049896 | solution.py:490
  1111.7 13.1 all-gather.7
  1124.8 13.1 all-gather.6
  1138.0 13.1 all-gather.5
  1151.8 93.7 %while.141 = (s32[]{:T(128)}, f32[8032,768]{1,0:T(8,128)}, f32[2,512,768]{2,1,0:T(8,128)}, bf16[2,512,768]{2,1,0:T(8,128)(2,1)}, bf16[8032,768]{1,0:T(8,128)(2,1...) while((s32[]{:T(128)}, f32[8032,768]{1,0:T(8,128)}, ...), condition=%wide.region_36.37_spmd.clone.clone, body=%wide.region_35.36_spmd.clone.sunk.clone | while | flops 18986876928 | bytes 108154000 | solution.py:518
  1151.9 14.4 multiply_convert_fusion.28
  1166.3 14.7 select_add_fusion.3
  1180.9 13.5 bitcast_dynamic-update-slice_fusion.3
  1194.5 14.4 multiply_convert_fusion.28
  1209.0 23.0 select_add_fusion.3
  1232.0 13.6 bitcast_dynamic-update-slice_fusion.3
  1246.3 60.1 %reduce-scatter.10.cloned.1.call-done = f32[256,768]{1,0:T(8,128)} async-done(((f32[1024,768]{1,0:T(8,128)}), f32[256,768]{1,0:T(8,128)}) %reduce-scatter.10.cloned.1.call-update) | async-done | bytes 786448 | tf_op jit(solution)/shard_map/reduce_scatter | solution.py:523
  1325.0 16.4 while.138
  1393.1 12.7 fusion.200
  1427.2 135.3 %while.139 = (s32[]{:T(128)}, bf16[2,512,12,64]{1,3,2,0:T(8,128)(2,1)}, bf16[2,512,12,64]{1,3,2,0:T(8,128)(2,1)}, bf16[2,512,12,64]{1,3,2,0:T(8,128)(2,1)}, f32[...) while((s32[]{:T(128)}, ...), condition=%wide.region_51.52_spmd.clone.clone, body=%wide.region_47.51_spmd.clone.sunk.clone | while | flops 2284979200 | bytes 260742032 | solution.py:169
  1436.3 15.2 fusion.671
  1503.7 15.2 fusion.671
  1720.5 25.4 bitcast_add_fusion.1
  1756.3 44.4 %scatter_fusion = f32[8032,768]{1,0:T(8,128)} fusion(f32[8032,768]{1,0:T(8,128)} %bitcast_add_fusion.1, s32[4096]{0:T(1024)S(1)} %bitcast.993, f32[4096,768]{1,0:T(8,128)} %bitcast.936), kind=kCustom, calls=%fused_computation.2 | custom fusion | flops 3145728 | bytes 37765120 | tf_op jit(solution)/shard_map/scatter-add | solution.py:431
  1800.7 24.3 scatter_fusion.1
  1825.0 15.3 fusion.390
  1840.3 49.1 %psum.67 = f32[768,8]{0,1:T(8,128)S(1)} all-reduce(f32[768,8]{0,1:T(8,128)S(1)} %fusion.390), channel_id=1, replica_groups=mesh['cuts'=8,'fsdp'=4] {'cuts','fsdp'}, use_global_device_ids=true, to_apply=%region_69.70 | all-reduce | flops 6144 | bytes 49152 | tf_op jit(solution)/shard_map/psum | solution.py:567
  1892.5 37.3 %reduce-scatter.12.cloned.1.call-done = bf16[768,12,192]{0,2,1:T(8,128)(2,1)} async-done(((bf16[768,12,768]{0,2,1:T(8,128)(2,1)}), bf16[768,12,192]{0,2,1:T(8,128)(2,1)}) %reduce-scatter.12.cloned.1.call-update) | async-done | bytes 3538960 | tf_op jit(solution)/shard_map/reduce_scatter | solution.py:360
  1929.8 317.1 %reduce-scatter.14.cloned.1.call-done = bf16[768,16,192]{0,2,1:T(8,128)(2,1)} async-done(((bf16[768,16,768]{0,2,1:T(8,128)(2,1)}), bf16[768,16,192]{0,2,1:T(8,128)(2,1)}) %reduce-scatter.14.cloned.1.call-update) | async-done | bytes 4718608 | tf_op jit(solution)/shard_map/reduce_scatter | solution.py:360
  2246.9 14.1 fusion.317
  2261.0 25.4 convolution_convert_fusion.8
  2286.5 103.0 %all-reduce.7.cloned.1.call-done = f32[28,768,8]{1,2,0:T(8,128)} async-done(((f32[28,768,8]{1,2,0:T(8,128)}), f32[28,768,8]{1,2,0:T(8,128)}) %all-reduce.7.cloned.1.call-update) | async-done | bytes 688144 | tf_op jit(solution)/shard_map/psum | solution.py:567
  2392.2 20.5 custom-call.13
  2413.1 17.5 custom-call.14
  2432.6 19.3 convolution_convert_fusion.21
  2451.9 54.0 %all-reduce.9.cloned.1.call-done = (bf16[28,192,8]{1,2,0:T(8,128)(2,1)}, bf16[8032,8]{0,1:T(8,128)(2,1)}) async-done(((bf16[28,192,8]{1,2,0:T(8,128)(2,1)}, bf16[8032,8]{0,1:T(8,128)(2,1)}), (bf16[28,192,8]{1,2,0:T(8,128)(2,1)}, bf16[8032,8]{0,1:T(8,128)(2,1)})) %all-reduce.9.cloned.1.call-update) | async-done | bytes 214544 | tf_op jit(solution)/shard_map/psum | solution.py:575
  2517.4 25.4 subtract_bitcast_fusion
  2560.4 40.3 %all-reduce.2 = (f32[]{:T(128)}, f32[]{:T(128)}, f32[7,768]{1,0:T(8,128)S(1)}, f32[2,32,12]{1,2,0:T(8,128)S(1)}) all-reduce(f32[]{:T(128)S(6)} %mul.768, f32[]{:T(128)S(6)} %add.640, f32[7,768]{1,0:T(8,128)S(1)} %copy-done.128, f32[2,32,12]{1,2,0:T(8,128)S(1)} %pad_maximum_fusion), channel_id=1, replica_groups=mesh['cuts'=8,'fsdp'=4] {'cuts','fsdp'}, use_global_device_ids=true, to_apply=%region_32.33 | all-reduce | flops 6146 | bytes 49168 | tf_op jit(solution)/shard_map/psum | solution.py:567
  2639.7 20.4 fusion.193
  (859 shorter events, 799.4 us)
Async XLA Ops:
  7.2 1817.8 %copy-start = (f32[8032,8]{0,1:T(8,128)S(1)}, f32[8032,8]{0,1:T(8,128)}, u32[]{:S(2)}) copy-start(f32[8032,8]{0,1:T(8,128)} %param.51) | copy-start | bytes 771076
  7.2 77.5 %all-gather.16.cloned.1.call-start = ((), (), s32[]{:S(2)}) async-start(), calls=%async_computation.5 | async-start | bytes 13934592 | tf_op jit(solution)/shard_map/all_gather | solution.py:392
  10.6 148.3 %all-gather.18.cloned.1.call-start = ((), (), s32[]{:S(2)}) async-start(), calls=%async_computation.7 | async-start | bytes 12386304 | tf_op jit(solution)/shard_map/all_gather | solution.py:391
  12.0 210.1 %reduce-scatter.6.cloned.1.call-start = ((), (), s32[]{:S(2)}) async-start(), calls=%async_computation.6 | async-start | bytes 1966080 | tf_op jit(solution)/shard_map/reduce_scatter | solution.py:437
  25.3 86.7 %copy-start.182 = (pred[8,128]{1,0:T(8,128)(4,1)}, pred[8,128]{1,0:T(8,128)(4,1)S(1)}, u32[]{:S(2)}) copy-start(pred[8,128]{1,0:T(8,128)(4,1)S(1)} %get-tuple-element.1373) | copy-start | bytes 3076
  113.5 189.3 %reduce-scatter.8.cloned.1.call-start = ((), (), s32[]{:S(2)}) async-start(), calls=%async_computation.9 | async-start | bytes 7864320 | tf_op jit(solution)/shard_map/reduce_scatter | solution.py:434
  126.8 25.5 copy-start.114
  126.9 25.4 copy-start.142
  158.9 389.9 %all-gather.22.cloned.1.call-start = ((), (), s32[]{:S(2)}) async-start(), calls=%async_computation.10 | async-start | bytes 17694720 | tf_op jit(solution)/shard_map/all_gather | solution.py:352
  170.2 700.9 %all-gather.20.cloned.1.call-start = ((), (), s32[]{:S(2)}) async-start(), calls=%async_computation.8 | async-start | bytes 23592960 | tf_op jit(solution)/shard_map/all_gather | solution.py:352
  185.2 897.9 %all-gather.24.cloned.1.call-start = ((), (), s32[]{:S(2)}) async-start(), calls=%async_computation.11 | async-start | bytes 1966080 | tf_op jit(solution)/shard_map/all_gather | solution.py:455
  221.4 338.2 %copy-start.131 = (f32[768]{0:T(1024)}, f32[768]{0:T(1024)S(1)}, u32[]{:S(2)}) copy-start(f32[768]{0:T(1024)S(1)} %get-tuple-element.1168) | copy-start | bytes 9220
  221.4 420.2 %copy-start.159 = (f32[768]{0:T(1024)}, f32[768]{0:T(1024)S(1)}, u32[]{:S(2)}) copy-start(f32[768]{0:T(1024)S(1)} %get-tuple-element.1167) | copy-start | bytes 9220
  223.3 79.6 %copy-start.184 = (f32[2,128]{1,0:T(2,128)}, f32[2,128]{1,0:T(2,128)S(1)}, u32[]{:S(2)}) copy-start(f32[2,128]{1,0:T(2,128)S(1)} %fusion.311) | copy-start | bytes 3076
  305.3 254.3 %copy-start.133 = (f32[2,512]{1,0:T(2,128)}, f32[2,512]{1,0:T(2,128)S(1)}, u32[]{:S(2)}) copy-start(f32[2,512]{1,0:T(2,128)S(1)} %fusion.355) | copy-start | bytes 12292
  971.0 21.5 copy-start.17
  995.8 22.4 copy-start.167
  1024.1 55.2 %copy-start.149 = (s32[4,2,128]{2,1,0:T(2,128)S(1)}, s32[4,2,128]{2,1,0:T(2,128)}, u32[]{:S(2)}) copy-start(s32[4,2,128]{2,1,0:T(2,128)} %copy-done.148) | copy-start | bytes 12292
  1024.1 55.3 %copy-start.199 = (s32[8]{0:T(128)S(1)}, s32[8]{0:T(128)}, u32[]{:S(2)}) copy-start(s32[8]{0:T(128)} %param.41) | copy-start | bytes 100
  1024.1 55.3 %copy-start.200 = (s32[8]{0:T(128)S(1)}, s32[8]{0:T(128)}, u32[]{:S(2)}) copy-start(s32[8]{0:T(128)} %param.40) | copy-start | bytes 100
  1027.5 278.9 %reduce-scatter.10.cloned.1.call-start = ((), (), s32[]{:S(2)}) async-start(), calls=%async_computation.12 | async-start | bytes 3932160 | tf_op jit(solution)/shard_map/reduce_scatter | solution.py:523
  1245.6 60.8 %copy-start.32 = (f32[2,128,768]{2,1,0:T(8,128)S(1)}, f32[2,128,768]{2,1,0:T(8,128)}, u32[]{:S(2)}) copy-start(f32[2,128,768]{2,1,0:T(8,128)} %copy-done.31) | copy-start | bytes 2359300
  1245.6 60.8 %copy-start.153 = (f32[2,128]{1,0:T(2,128)S(1)}, f32[2,128]{1,0:T(2,128)}, u32[]{:S(2)}) copy-start(f32[2,128]{1,0:T(2,128)} %copy-done.152) | copy-start | bytes 3076
  1245.6 63.0 %copy-start.192 = (f32[2,128]{1,0:T(2,128)S(1)}, f32[2,128]{1,0:T(2,128)}, u32[]{:S(2)}) copy-start(f32[2,128]{1,0:T(2,128)} %copy-done.191) | copy-start | bytes 3076
  1245.6 501.1 %all-gather.28.cloned.1.call-start = ((), (), s32[]{:S(2)}) async-start(), calls=%async_computation.17 | async-start | bytes 1966080 | tf_op jit(solution)/shard_map/all_gather | solution.py:554
  1246.3 73.3 %copy-start.126 = (f32[768]{0:T(1024)}, f32[768]{0:T(1024)S(1)}, u32[]{:S(2)}) copy-start(f32[768]{0:T(1024)S(1)} %broadcast_multiply_fusion) | copy-start | bytes 9220
  1325.0 16.5 copy-start.18
  1363.9 384.6 %all-gather.26.cloned.1.call-start = ((), (), s32[]{:S(2)}) async-start(), calls=%async_computation.16 | async-start | bytes 7864320 | tf_op jit(solution)/shard_map/all_gather | solution.py:551
  1370.5 46.0 %copy-start.27 = (f32[2,512,768]{2,1,0:T(8,128)}, f32[2,512,768]{2,1,0:T(8,128)S(1)}, u32[]{:S(2)}) copy-start(f32[2,512,768]{2,1,0:T(8,128)S(1)} %add_add_fusion.2) | copy-start | bytes 9437188
  1574.8 355.0 %reduce-scatter.12.cloned.1.call-start = ((), (), s32[]{:S(2)}) async-start(), calls=%async_computation.13 | async-start | bytes 17694720 | tf_op jit(solution)/shard_map/reduce_scatter | solution.py:360
  1636.4 610.5 %reduce-scatter.14.cloned.1.call-start = ((), (), s32[]{:S(2)}) async-start(), calls=%async_computation.14 | async-start | bytes 23592960 | tf_op jit(solution)/shard_map/reduce_scatter | solution.py:360
  1702.8 686.6 %all-reduce.7.cloned.1.call-start = ((), (), s32[]{:S(2)}) async-start(), calls=%async_computation.15 | async-start | bytes 1376256 | tf_op jit(solution)/shard_map/psum | solution.py:567
  1720.4 25.5 copy-start.178
  1720.5 25.5 copy-start.190
  1720.5 25.5 copy-start.172
  1720.5 25.5 copy-start.171
  1720.5 25.5 copy-start.189
  1720.5 25.6 copy-start.170
  1720.5 25.6 copy-start.136
  1720.5 26.2 copy-start.183
  1825.0 421.9 %copy-start.110 = (f32[28,192,8]{1,2,0:T(8,128)S(1)}, f32[28,192,8]{1,2,0:T(8,128)}, u32[]{:S(2)}) copy-start(f32[28,192,8]{1,2,0:T(8,128)} %param.50) | copy-start | bytes 516100
  2261.0 244.9 %all-reduce.9.cloned.1.call-start = ((), (), s32[]{:S(2)}) async-start(), calls=%async_computation.18 | async-start | bytes 487424 | tf_op jit(solution)/shard_map/psum | solution.py:575
  2516.7 36.0 %copy-start.2 = (f32[8032,768]{1,0:T(8,128)}, f32[8032,768]{1,0:T(8,128)S(1)}, u32[]{:S(2)}) copy-start(f32[8032,768]{1,0:T(8,128)S(1)} %fusion.392) | copy-start | bytes 74022912
  2517.4 25.4 copy-start.104
  2552.7 51.2 %copy-start.138 = (f32[2,32,12]{1,0,2:T(2,128)S(1)}, f32[2,32,12]{1,0,2:T(2,128)}, u32[]{:S(2)}) copy-start(f32[2,32,12]{1,0,2:T(2,128)} %param.48) | copy-start | bytes 9220
  2552.7 51.2 %copy-start.179 = (f32[2,32,12]{1,0,2:T(2,128)S(1)}, f32[2,32,12]{1,0,2:T(2,128)}, u32[]{:S(2)}) copy-start(f32[2,32,12]{1,0,2:T(2,128)} %param.49) | copy-start | bytes 9220
  2552.7 52.5 %copy-start.130 = (f32[7,768]{1,0:T(8,128)S(1)}, f32[7,768]{1,0:T(8,128)}, u32[]{:S(2)}) copy-start(f32[7,768]{1,0:T(8,128)} %param.46) | copy-start | bytes 64516
  2552.7 52.5 %copy-start.158 = (f32[7,768]{1,0:T(8,128)S(1)}, f32[7,768]{1,0:T(8,128)}, u32[]{:S(2)}) copy-start(f32[7,768]{1,0:T(8,128)} %param.47) | copy-start | bytes 64516
  (200 other events, 979.4 us)
Sparse Core Ops, SparseCore 0:
  10.7 73.9 all-gather.15
  87.2 65.4 all-gather.17
  155.6 35.2 reduce-scatter.5
  193.1 109.7 reduce-scatter.7
  304.3 244.4 all-gather.21
  550.2 320.7 all-gather.19
  1027.6 37.0 all-gather.23
  1245.7 60.5 reduce-scatter.9
  1364.0 37.0 all-gather.27
  1574.9 115.3 all-gather.25
  1693.3 236.4 reduce-scatter.11
  1932.0 314.8 reduce-scatter.13
  2261.1 128.3 all-reduce.6
  2452.0 53.8 all-reduce.8
where the time goes:
time: 2680 us; the launch traced here: 2670 us
  waiting for transfers between devices  1160 us (43%)
  matrix products  558 us (21%)
  local copies, waits for them, and re-layouts  376 us (14%)
  other arithmetic  343 us (13%)
  blocking collectives  203 us (8%)
    all_gather x2, waiting for transfers between devices, gather_layer(): return lax.all_gather(part_weights, 'fsdp', axis=2, tiled=True)  450 us
    reduce_scatter x2, waiting for transfers between devices, reduce_layer(): lax.psum_scatter(part_grads.astype(jnp.bfloat16), 'fsdp', scatter_dimensi...  354 us
    unnamed x429, local copies, waits for them, and re-layouts  134 us
    psum x1, waiting for transfers between devices, local(): lax.psum((left_factor, embed_factor, gains_grad, table_grad, loss_local),...  103 us
    psum x2, blocking collectives, local(): lax.psum((left_factor, embed_factor, gains_grad, table_grad, loss_local),...  89.3 us
    reduce_scatter x1, waiting for transfers between devices, local(): lax.psum_scatter(shard_lookup(group_source).astype(jnp.bfloat16), 'fsdp',...  79 us
    scatter-add x2, other arithmetic, scatter_rows(): accumulated.at[jnp.clip(local_ids, 0, vocab_rows - 1).reshape(-1)]  68.7 us
    reduce_scatter x1, waiting for transfers between devices, local(): lax.psum_scatter(grad_rows.reshape(-1, MODEL_WIDTH), 'fsdp', scatter_dime...  60.1 us
  transfers between devices with their start and end apart: 14, of which 9 were waited for; matrix products, arithmetic and copies ran while one was open for 28% of the time, Pallas kernels for 0%

commit v1 on v0

v1 whole, which is shorter than its diff:
```python
import math

import jax
import jax.numpy as jnp
from jax import lax
from jax.experimental import pallas as pl
from jax.experimental.pallas import tpu as pltpu
from jax.sharding import PartitionSpec as P

MODEL_WIDTH = 768
H = 12
DH = 64
FEED_UNITS = 3072
NBK = 32
TASKS = 8
PARAMS = 41189376


EPSILON = 1e-06
MASKED = -1000000000.0
CLIP_NORM = 0.05
MOMENTUM_DECAY = 0.9
STEP_RATE = 5.0
EMBED_SHARE = 50.0
SMALL_SHARE = 1.0 / 7.0
TOP_PRECISION = lax.Precision.HIGHEST
TILE = 128
ROOM_SOURCE = 1280
ROOM_TARGET = 384
ENCODER_EDGES = (12, 16, 23, 32, 46, 64, 91)
DECODER_EDGES = (19, 21, 24, 27, 31, 35, 40, 46, 52, 59, 67, 77, 87, 99, 113)


def root_norm(stream, gain_row):
    return (
        stream * lax.rsqrt(jnp.mean(stream * stream, axis=-1, keepdims=True) + EPSILON) * gain_row
    )


def norm_backward(stream, gain_row, grad_normed):
    _, pull_back = jax.vjp(root_norm, stream, gain_row)
    return pull_back(grad_normed)


def dot(left, right):
    return jnp.dot(left, right, preferred_element_type=jnp.float32)


def dot_nt(left, right):
    return lax.dot_general(left, right, (((1,), (1,)), ((), ())), preferred_element_type=jnp.float32)


def dot_tn(left, right):
    return lax.dot_general(left, right, (((0,), (0,)), ((), ())), preferred_element_type=jnp.float32)


def gather_cuts(part, cuts_rank, cuts_count):
    number, rows, columns = part.shape
    ways = [1 << bit for bit in range(1, cuts_count.bit_length() - 1)]
    if cuts_count & (cuts_count - 1) or number % max(len(ways), 1):
        return lax.all_gather(part, "cuts", axis=1, tiled=True)

    def swap(array, mask):
        return lax.ppermute(array, "cuts", [(i, i ^ mask) for i in range(cuts_count)])

    share = number // max(len(ways), 1)
    joined = []
    for turn in range(max(len(ways), 1)):
        held = [(0, part[turn * share : (turn + 1) * share])]
        for mask in ways[turn:] + ways[:turn] + [1]:
            held = held + [(place ^ mask, swap(array, mask)) for place, array in held]
        whole = jnp.zeros((share, cuts_count, rows, columns), part.dtype)
        for place, array in held:
            whole = lax.dynamic_update_slice(
                whole, array[:, None], (0, jnp.bitwise_xor(cuts_rank, place), 0, 0)
            )
        joined.append(whole.reshape(share, cuts_count * rows, columns))
    return jnp.concatenate(joined, axis=0) if len(joined) > 1 else joined[0]


def offset_buckets(causal):
    places = jnp.arange(TILE, dtype=jnp.int32)
    offset = (
        (jnp.arange(5, dtype=jnp.int32)[:, None, None] - 2) * TILE
        + places[None, :, None]
        - places[None, None, :]
    )
    if causal:
        distance = jnp.maximum(-offset, 0)
        farther = 16 + sum(((distance >= boundary).astype(jnp.int32) for boundary in DECODER_EDGES))
        bucket = jnp.where(distance < 16, distance, farther)
    else:
        distance = jnp.abs(offset)
        farther = 8 + sum(((distance >= boundary).astype(jnp.int32) for boundary in ENCODER_EDGES))
        bucket = jnp.where(distance < 8, distance, farther) + jnp.where(offset > 0, 16, 0)
    return (bucket[..., None] == jnp.arange(NBK, dtype=jnp.int32)).astype(jnp.float32)


def kept(segment_column, segment_row, key_tile, query_tile, causal):
    keep = segment_column == segment_row
    if causal:
        key_place = key_tile * TILE + lax.broadcasted_iota(jnp.int32, (TILE, TILE), 0)
        query_place = query_tile * TILE + lax.broadcasted_iota(jnp.int32, (TILE, TILE), 1)
        keep = keep & (key_place <= query_place)
    return keep


def lane_half(rows, half):
    return (lax.broadcasted_iota(jnp.int32, (rows, TILE), 1) // DH) == half


def tile_scores(keys, queries, keep, bias):
    scores = dot_nt(keys, queries)
    if bias is not None:
        scores = scores + bias
    return jnp.where(keep, scores, MASKED)


def forward_kernel(
    causal, biased, first_ref, last_ref, q_ref, k_ref, v_ref, row_ref, column_ref, *rest
):
    bias_ref = rest[0] if biased else None
    out_ref, level_ref, top_ref, sum_ref, total_ref = rest[1:] if biased else rest
    here = pl.program_id(0)
    top_ref[...] = jnp.full_like(top_ref, -1e30)
    sum_ref[...] = jnp.zeros_like(sum_ref)
    total_ref[...] = jnp.zeros_like(total_ref)
    segment_row = row_ref[...]

    def step(there, carry):
        rows = pl.ds(pl.multiple_of(there * TILE, TILE), TILE)
        keep = kept(column_ref[rows, :], segment_row, there, here, causal)
        offset = jnp.clip(there - here, -2, 2) + 2
        for pair in range(H // 2):
            lanes = slice(pair * TILE, (pair + 1) * TILE)
            keys = k_ref[rows, lanes]
            values = v_ref[rows, lanes].T
            both = q_ref[:, lanes]
            for half in range(2):
                head = 2 * pair + half
                queries = jnp.where(lane_half(TILE, half), both, jnp.zeros_like(both))
                scores = tile_scores(
                    keys, queries, keep, bias_ref[offset, head] if biased else None
                )
                before = top_ref[head : head + 1, :]
                after = jnp.maximum(before, jnp.max(scores, axis=0, keepdims=True))
                weights = jnp.exp(scores - after)
                scale = jnp.exp(before - after)
                top_ref[head : head + 1, :] = after
                sum_ref[head : head + 1, :] = sum_ref[head : head + 1, :] * scale + jnp.sum(
                    weights, axis=0, keepdims=True
                )
                own = slice(head * DH, (head + 1) * DH)
                total_ref[own, :] = total_ref[own, :] * scale + dot(
                    values[half * DH : (half + 1) * DH], weights.astype(jnp.bfloat16)
                )
        return carry

    lax.fori_loop(first_ref[here], last_ref[here], step, 0)
    seen = sum_ref[...] > 0.0
    divisor = jnp.where(seen, sum_ref[...], 1.0)
    level_ref[...] = jnp.where(seen, top_ref[...] + jnp.log(divisor), 0.0)
    for head in range(H):
        own = slice(head * DH, (head + 1) * DH)
        total_ref[own, :] = total_ref[own, :] / divisor[head : head + 1, :]
    for pair in range(H // 2):
        lanes = slice(pair * TILE, (pair + 1) * TILE)
        out_ref[:, lanes] = total_ref[lanes, :].T.astype(jnp.bfloat16)


def backward_kernel(
    causal, biased, first_ref, last_ref, q_ref, o_ref, k_ref, v_ref, level_ref, row_ref, column_ref, *rest
):
    bias_ref = rest[0] if biased else None
    rest = rest[1:] if biased else rest
    gq_ref, gk_ref, gv_ref = rest[:3]
    gb_ref = rest[3] if biased else None
    weight_ref, slope_ref, mean_ref, tq_ref, tk_ref, tv_ref = rest[-6:]
    here = pl.program_id(0)

    @pl.when(here == 0)
    def _():
        tk_ref[...] = jnp.zeros_like(tk_ref)
        tv_ref[...] = jnp.zeros_like(tv_ref)
        if biased:
            gb_ref[...] = jnp.zeros_like(gb_ref)

    mean_ref[...] = jnp.zeros_like(mean_ref)
    tq_ref[...] = jnp.zeros_like(tq_ref)
    segment_row = row_ref[...]
    first = first_ref[here]
    last = last_ref[here]

    def halves(array):
        return [jnp.where(lane_half(TILE, half), array, jnp.zeros_like(array)) for half in range(2)]

    def look(there, carry):
        rows = pl.ds(pl.multiple_of(there * TILE, TILE), TILE)
        keep = kept(column_ref[rows, :], segment_row, there, here, causal)
        offset = jnp.clip(there - here, -2, 2) + 2
        for pair in range(H // 2):
            lanes = slice(pair * TILE, (pair + 1) * TILE)
            keys = k_ref[rows, lanes]
            values = v_ref[rows, lanes]
            queries = halves(q_ref[:, lanes])
            arriving = halves(o_ref[:, lanes])
            rounded = []
            for half in range(2):
                head = 2 * pair + half
                scores = tile_scores(
                    keys, queries[half], keep, bias_ref[offset, head] if biased else None
                )
                weights = jnp.exp(scores - level_ref[head : head + 1, :])
                slopes = dot_nt(values, arriving[half])
                mean_ref[head : head + 1, :] = mean_ref[head : head + 1, :] + jnp.sum(
                    weights * slopes, axis=0, keepdims=True
                )
                weight_ref[there - first, head] = weights
                slope_ref[there - first, head] = slopes
                rounded.append(weights.astype(jnp.bfloat16))
            tv_ref[rows, lanes] = tv_ref[rows, lanes] + dot(
                jnp.concatenate(rounded, axis=1), jnp.concatenate(arriving, axis=0)
            )
        return carry

    def push(there, carry):
        rows = pl.ds(pl.multiple_of(there * TILE, TILE), TILE)
        offset = jnp.clip(there - here, -2, 2) + 2
        for pair in range(H // 2):
            lanes = slice(pair * TILE, (pair + 1) * TILE)
            keys = k_ref[rows, lanes].T
            queries = halves(q_ref[:, lanes])
            rounded = []
            for half in range(2):
                head = 2 * pair + half
                slopes = (
                    weight_ref[there - first, head]
                    * (slope_ref[there - first, head] - mean_ref[head : head + 1, :])
                ).astype(jnp.bfloat16)
                if biased:
                    gb_ref[offset, head] = gb_ref[offset, head] + slopes.astype(jnp.float32)
                own = slice(head * DH, (head + 1) * DH)
                tq_ref[own, :] = tq_ref[own, :] + dot(keys[half * DH : (half + 1) * DH], slopes)
                rounded.append(slopes)
            tk_ref[rows, lanes] = tk_ref[rows, lanes] + dot(
                jnp.concatenate(rounded, axis=1), jnp.concatenate(queries, axis=0)
            )
        return carry

    lax.fori_loop(first, last, look, 0)
    lax.fori_loop(first, last, push, 0)
    for pair in range(H // 2):
        lanes = slice(pair * TILE, (pair + 1) * TILE)
        gq_ref[:, lanes] = tq_ref[lanes, :].T.astype(jnp.bfloat16)

    @pl.when(here == pl.num_programs(0) - 1)
    def _():
        gk_ref[...] = tk_ref[...].astype(jnp.bfloat16)
        gv_ref[...] = tv_ref[...].astype(jnp.bfloat16)


def whole_block(shape):
    return pl.BlockSpec(shape, lambda i, *_: (0,) * len(shape))


def packed_forward(queries, key_rows, value_rows, span, segment_row, segment_column, causal, bias):
    count, other = queries.shape[0], key_rows.shape[0]
    biased = bias is not None
    tile = pl.BlockSpec((TILE, MODEL_WIDTH), lambda i, *_: (i, 0))
    return pl.pallas_call(
        lambda *refs: forward_kernel(causal, biased, *refs),
        grid_spec=pltpu.PrefetchScalarGridSpec(
            num_scalar_prefetch=2,
            grid=(count // TILE,),
            in_specs=[
                tile,
                whole_block((other, MODEL_WIDTH)),
                whole_block((other, MODEL_WIDTH)),
                pl.BlockSpec((1, TILE), lambda i, *_: (0, i)),
                whole_block((other, 1)),
            ]
            + ([whole_block((5, H, TILE, TILE))] if biased else []),
            out_specs=[tile, pl.BlockSpec((16, TILE), lambda i, *_: (0, i))],
            scratch_shapes=[
                pltpu.VMEM((16, TILE), jnp.float32),
                pltpu.VMEM((16, TILE), jnp.float32),
                pltpu.VMEM((MODEL_WIDTH, TILE), jnp.float32),
            ],
        ),
        out_shape=[
            jax.ShapeDtypeStruct((count, MODEL_WIDTH), jnp.bfloat16),
            jax.ShapeDtypeStruct((16, count), jnp.float32),
        ],
        compiler_params=pltpu.CompilerParams(vmem_limit_bytes=40 << 20),
        name="attend",
    )(*span, queries, key_rows, value_rows, segment_row, segment_column, *([bias] if biased else []))


def packed_backward(
    queries, grad_out, key_rows, value_rows, levels, span, segment_row, segment_column, causal, bias
):
    count, other = queries.shape[0], key_rows.shape[0]
    biased = bias is not None
    reach = min(other // TILE, 9) if biased else other // TILE
    tile = pl.BlockSpec((TILE, MODEL_WIDTH), lambda i, *_: (i, 0))
    table = (5, H, TILE, TILE)
    return pl.pallas_call(
        lambda *refs: backward_kernel(causal, biased, *refs),
        grid_spec=pltpu.PrefetchScalarGridSpec(
            num_scalar_prefetch=2,
            grid=(count // TILE,),
            in_specs=[
                tile,
                tile,
                whole_block((other, MODEL_WIDTH)),
                whole_block((other, MODEL_WIDTH)),
                pl.BlockSpec((16, TILE), lambda i, *_: (0, i)),
                pl.BlockSpec((1, TILE), lambda i, *_: (0, i)),
                whole_block((other, 1)),
            ]
            + ([whole_block(table)] if biased else []),
            out_specs=[tile, whole_block((other, MODEL_WIDTH)), whole_block((other, MODEL_WIDTH))]
            + ([whole_block(table)] if biased else []),
            scratch_shapes=[
                pltpu.VMEM((reach, H, TILE, TILE), jnp.float32),
                pltpu.VMEM((reach, H, TILE, TILE), jnp.float32),
                pltpu.VMEM((16, TILE), jnp.float32),
                pltpu.VMEM((MODEL_WIDTH, TILE), jnp.float32),
                pltpu.VMEM((other, MODEL_WIDTH), jnp.float32),
                pltpu.VMEM((other, MODEL_WIDTH), jnp.float32),
            ],
        ),
        out_shape=[
            jax.ShapeDtypeStruct((count, MODEL_WIDTH), jnp.bfloat16),
            jax.ShapeDtypeStruct((other, MODEL_WIDTH), jnp.bfloat16),
            jax.ShapeDtypeStruct((other, MODEL_WIDTH), jnp.bfloat16),
        ]
        + ([jax.ShapeDtypeStruct(table, jnp.float32)] if biased else []),
        compiler_params=pltpu.CompilerParams(vmem_limit_bytes=58 << 20),
        name="attend_back",
    )(
        *span,
        queries,
        grad_out,
        key_rows,
        value_rows,
        levels,
        segment_row,
        segment_column,
        *([bias] if biased else []),
    )


def lookup_kernel(rows_in, blocks_ref, id_ref, vocab_ref, out_ref, total_ref):
    step = pl.program_id(0)
    width = vocab_ref.shape[1]
    chunk = 2 * TILE

    @pl.when(step == 0)
    def _():
        total_ref[...] = jnp.zeros_like(total_ref)

    inside = step * width + lax.broadcasted_iota(jnp.int32, (1, width), 1) < rows_in
    table = jnp.where(inside, vocab_ref[...], jnp.zeros_like(vocab_ref[...]))
    places = step * width + lax.broadcasted_iota(jnp.int32, (chunk, width), 1)

    def one(index, carry):
        rows = pl.ds(pl.multiple_of(index * chunk, chunk), chunk)
        hot = (id_ref[rows, :] == places).astype(jnp.bfloat16)
        total_ref[rows, :] = total_ref[rows, :] + dot_nt(hot, table)
        return carry

    lax.fori_loop(0, blocks_ref[0], one, 0)
    lax.fori_loop(blocks_ref[1], blocks_ref[2], one, 0)

    @pl.when(step == pl.num_programs(0) - 1)
    def _():
        out_ref[...] = total_ref[...].astype(jnp.bfloat16)


def lookup_rows(local_ids, spans, vocab):
    count, width = local_ids.shape[0], 4 * TILE
    rows_in = vocab.shape[1]
    return pl.pallas_call(
        lambda *refs: lookup_kernel(rows_in, *refs),
        grid_spec=pltpu.PrefetchScalarGridSpec(
            num_scalar_prefetch=1,
            grid=(pl.cdiv(rows_in, width),),
            in_specs=[
                whole_block((count, 1)),
                pl.BlockSpec((MODEL_WIDTH, width), lambda i, *_: (0, i)),
            ],
            out_specs=whole_block((count, MODEL_WIDTH)),
            scratch_shapes=[pltpu.VMEM((count, MODEL_WIDTH), jnp.float32)],
        ),
        out_shape=jax.ShapeDtypeStruct((count, MODEL_WIDTH), jnp.bfloat16),
        compiler_params=pltpu.CompilerParams(vmem_limit_bytes=40 << 20),
        name="lookup",
    )(spans, local_ids[:, None], vocab)


def vocab_grad_kernel(blocks_ref, id_ref, grad_ref, logit_ref, final_ref, left_ref, out_ref):
    step = pl.program_id(0)
    width = left_ref.shape[0]
    chunk = 2 * TILE
    out_ref[...] = left_ref[...] + dot_tn(logit_ref[...], final_ref[...])
    places = step * width + lax.broadcasted_iota(jnp.int32, (width, chunk), 0)

    def one(index, carry):
        rows = pl.ds(pl.multiple_of(index * chunk, chunk), chunk)
        hot = (places == id_ref[:, rows]).astype(jnp.bfloat16)
        out_ref[...] = out_ref[...] + dot(hot, grad_ref[rows, :])
        return carry

    lax.fori_loop(0, blocks_ref[0], one, 0)
    lax.fori_loop(blocks_ref[1], blocks_ref[2], one, 0)


def vocab_grad(left, local_ids, spans, lookups, grad_logits, final_rows):
    count, width = local_ids.shape[0], 4 * TILE
    rows_in = left.shape[0]
    block = pl.BlockSpec((width, MODEL_WIDTH), lambda i, *_: (i, 0))
    return pl.pallas_call(
        vocab_grad_kernel,
        grid_spec=pltpu.PrefetchScalarGridSpec(
            num_scalar_prefetch=1,
            grid=(pl.cdiv(rows_in, width),),
            in_specs=[
                whole_block((1, count)),
                whole_block((count, MODEL_WIDTH)),
                pl.BlockSpec((grad_logits.shape[0], width), lambda i, *_: (0, i)),
                whole_block(final_rows.shape),
                block,
            ],
            out_specs=block,
        ),
        out_shape=jax.ShapeDtypeStruct(left.shape, jnp.float32),
        input_output_aliases={5: 0},
        compiler_params=pltpu.CompilerParams(vmem_limit_bytes=40 << 20),
        name="vocab_grad",
    )(spans, local_ids[None, :], lookups, grad_logits, final_rows, left)


def packing(lengths, room):
    ends = jnp.cumsum(lengths)
    starts = ends - lengths
    places = jnp.arange(room, dtype=jnp.int32)
    segment = jnp.sum((places[:, None] >= ends[None, :]).astype(jnp.int32), axis=1)
    inside = segment[:, None] == jnp.arange(lengths.shape[0], dtype=jnp.int32)[None, :]
    position = places - jnp.sum(jnp.where(inside, starts[None, :], 0), axis=1)
    return segment, position, jnp.minimum(starts, room), jnp.minimum(ends, room)


def key_span(query_segment, query_total, key_starts, key_ends):
    number = key_starts.shape[0]
    count = query_segment.shape[0] // TILE
    begins = jnp.arange(count, dtype=jnp.int32) * TILE
    last_real = jnp.clip(query_total - 1, 0, query_segment.shape[0] - 1)
    finals = jnp.minimum(begins + TILE - 1, last_real)

    def pick(table, places):
        chosen = jnp.sum(
            jnp.where(
                jnp.arange(query_segment.shape[0], dtype=jnp.int32)[None, :] == places[:, None],
                query_segment[None, :],
                0,
            ),
            axis=1,
        )
        return jnp.sum(
            jnp.where(
                chosen[:, None] == jnp.arange(number, dtype=jnp.int32)[None, :], table[None, :], 0
            ),
            axis=1,
        )

    some = begins < query_total
    first = jnp.where(some, pick(key_starts, begins) // TILE, 0)
    last = jnp.where(some, (pick(key_ends, finals) + TILE - 1) // TILE, 0)
    return first, jnp.maximum(first, last)


def column_shards(grads, start, width):
    return [lax.dynamic_slice_in_dim(grad, start, width, 1) for grad in grads]


def packed_gradients(
    source_stream, target_stream, gain_rows, position_bias, weights, layout, head, column_start, column_width
):
    enc_attention, enc_feed, dec = weights
    (
        source_span,
        target_span,
        cross_span,
        source_row,
        source_column,
        target_row,
        target_column,
    ) = layout
    hot_source, hot_target = offset_buckets(False), offset_buckets(True)
    bias_source = jnp.einsum("tkqb,bh->thkq", hot_source, position_bias[0], precision=TOP_PRECISION)
    bias_target = jnp.einsum("tkqb,bh->thkq", hot_target, position_bias[1], precision=TOP_PRECISION)

    def shard(grad):
        return lax.dynamic_slice_in_dim(grad, column_start, column_width, 1)

    def attention(stream, gain_row, context, matrices, span, row, column, causal, bias):
        normed = root_norm(stream, gain_row).astype(jnp.bfloat16)
        context = normed if context is None else context
        queries = dot(normed, matrices[0]).astype(jnp.bfloat16)
        key_rows = dot(context, matrices[1]).astype(jnp.bfloat16)
        value_rows = dot(context, matrices[2]).astype(jnp.bfloat16)
        attended, levels = packed_forward(
            queries, key_rows, value_rows, span, row, column, causal, bias
        )
        return stream + dot(attended, matrices[3]), (
            normed,
            context,
            queries,
            key_rows,
            value_rows,
            attended,
            levels,
        )

    def attention_back(grad, stream, gain_row, crossed, matrices, saved, span, row, column, causal, bias):
        normed, context, queries, key_rows, value_rows, attended, levels = saved
        branch = grad.astype(jnp.bfloat16)
        arriving = dot_nt(branch, matrices[3]).astype(jnp.bfloat16)
        grads = packed_backward(
            queries, arriving, key_rows, value_rows, levels, span, row, column, causal, bias
        )
        grad_queries, grad_keys, grad_values = grads[:3]
        shares = [
            dot_tn(normed, shard(grad_queries)),
            dot_tn(context, shard(grad_keys)),
            dot_tn(context, shard(grad_values)),
            dot_tn(attended, shard(branch)),
        ]
        grad_normed = dot_nt(grad_queries, matrices[0])
        grad_context = dot_nt(grad_keys, matrices[1]) + dot_nt(grad_values, matrices[2])
        if not crossed:
            grad_normed = grad_normed + grad_context
        grad_input, grad_gain = norm_backward(stream, gain_row, grad_normed)
        return grad + grad_input, grad_gain, shares, grads[3:], grad_context

    def feed(stream, gain_row, matrices):
        normed = root_norm(stream, gain_row).astype(jnp.bfloat16)
        inner = [dot(normed, matrices[j]) for j in range(4)]
        hidden = [jax.nn.gelu(a).astype(jnp.bfloat16) for a in inner]
        branch = sum(dot(hidden[j], matrices[4 + j]) for j in range(4))
        return stream + branch, (normed, inner, hidden)

    def feed_back(grad, stream, gain_row, matrices, saved):
        normed, inner, hidden = saved
        branch = grad.astype(jnp.bfloat16)
        grad_inner = [
            jax.vjp(jax.nn.gelu, inner[j])[1](dot_nt(branch, matrices[4 + j]))[0].astype(jnp.bfloat16)
            for j in range(4)
        ]
        grad_normed = sum(dot_nt(grad_inner[j], matrices[j]) for j in range(4))
        branch_shard = shard(branch)
        shares = [dot_tn(normed, shard(grad_inner[j])) for j in range(4)] + [
            dot_tn(hidden[j], branch_shard) for j in range(4)
        ]
        grad_input, grad_gain = norm_backward(stream, gain_row, grad_normed)
        return grad + grad_input, grad_gain, shares

    x1, enc_saved = attention(
        source_stream, gain_rows[0], None, enc_attention, source_span, source_row, source_column, False, bias_source
    )
    x2, enc_feed_saved = feed(x1, gain_rows[1], enc_feed)
    encoded = root_norm(x2, gain_rows[2]).astype(jnp.bfloat16)
    y1, self_saved = attention(
        target_stream, gain_rows[3], None, dec[0:4], target_span, target_row, target_column, True, bias_target
    )
    y2, cross_saved = attention(
        y1, gain_rows[4], encoded, dec[4:8], cross_span, target_row, source_column, False, None
    )
    y3, dec_feed_saved = feed(y2, gain_rows[5], dec[8:16])
    final_rows = (root_norm(y3, gain_rows[6]) * MODEL_WIDTH ** (-0.5)).astype(jnp.bfloat16)

    grad_final, grad_logits, token_loss = head(final_rows)

    grad, gain_final = norm_backward(y3, gain_rows[6], grad_final * MODEL_WIDTH ** (-0.5))
    grad, gain_feed, feed_shares = feed_back(grad, y2, gain_rows[5], dec[8:16], dec_feed_saved)
    grad, gain_cross, cross_shares, _, grad_encoded = attention_back(
        grad, y1, gain_rows[4], True, dec[4:8], cross_saved, cross_span, target_row, source_column, False, None
    )
    target_grad, gain_self, self_shares, table_target, _ = attention_back(
        grad, target_stream, gain_rows[3], False, dec[0:4], self_saved, target_span, target_row, target_column, True, bias_target
    )
    grad, gain_encoded = norm_backward(x2, gain_rows[2], grad_encoded)
    grad, gain_enc_feed, enc_feed_shares = feed_back(grad, x1, gain_rows[1], enc_feed, enc_feed_saved)
    source_grad, gain_enc, enc_shares, table_source, _ = attention_back(
        grad, source_stream, gain_rows[0], False, enc_attention, enc_saved, source_span, source_row, source_column, False, bias_source
    )
    gains = jnp.stack(
        [gain_enc, gain_enc_feed, gain_encoded, gain_self, gain_cross, gain_feed, gain_final]
    )
    tables = jnp.stack(
        [
            jnp.einsum("thkq,tkqb->bh", table_source[0], hot_source, precision=TOP_PRECISION),
            jnp.einsum("thkq,tkqb->bh", table_target[0], hot_target, precision=TOP_PRECISION),
        ]
    )
    shares = jnp.stack(enc_shares + enc_feed_shares + self_shares + cross_shares + feed_shares)
    return shares, gains, tables, source_grad, target_grad, final_rows, grad_logits, token_loss


def orthonormal_kernel(factor_ref, out_ref):
    rank = factor_ref.shape[0]
    for r in range(rank):
        out_ref[r] = factor_ref[r]
    for r in range(rank):
        row = out_ref[r]
        row = row * lax.rsqrt(jnp.sum(row * row, axis=-1, keepdims=True))
        out_ref[r] = row
        for s in range(r + 1, rank):
            other = out_ref[s]
            out_ref[s] = other - row * jnp.sum(row * other, axis=-1, keepdims=True)


def orthonormal_rows(factor):
    return pl.pallas_call(
        orthonormal_kernel,
        out_shape=jax.ShapeDtypeStruct(factor.shape, jnp.float32),
        name="orthonormal",
    )(factor)


def local(
    source_ids,
    targets,
    source_lengths,
    target_lengths,
    task_ids,
    task_counts,
    blocks,
    blocks_momentum,
    embedding,
    embed_momentum,
    gain_rows,
    gain_momentum,
    position_bias,
    bias_momentum,
    right_blocks,
    right_embed,
    error_blocks,
    error_embed,
):
    fsdp_rank = lax.axis_index("fsdp")
    cuts_rank = lax.axis_index("cuts")
    cuts_count = lax.axis_size("cuts")
    seq_count, source_len = source_ids.shape
    target_len = targets.shape[1]
    number = seq_count * lax.axis_size("fsdp")
    room_source = min(ROOM_SOURCE, source_len * number)
    room_target = min(ROOM_TARGET, target_len * number)
    fewest = min(room_source // source_len, room_target // target_len)
    shares_of = sorted({number, -(-number // 2), fewest}, reverse=True)
    vocab_rows = embedding.shape[0]
    vocab_start = fsdp_rank * vocab_rows
    once = (fsdp_rank == 0).astype(jnp.float32)

    def one_round(state):
        _, turn, _, _, left_blocks, left_embed, gains_sum, table_sum, loss_sum = state
        group = lax.all_gather(
            jnp.concatenate(
                [source_ids, targets, source_lengths[:, None], target_lengths[:, None]], axis=1
            ),
            "fsdp",
            axis=0,
            tiled=True,
        )
        group_source = group[:, :source_len]
        group_target = group[:, source_len : source_len + target_len]
        lengths = group[:, -2:]

        def fullest(share):
            padded = jnp.pad(lengths, ((0, -number % share), (0, 0)))
            return jnp.max(jnp.sum(padded.reshape(-1, share, 2), axis=1), axis=0)

        needs = lax.all_gather(
            jnp.concatenate([jnp.sum(lengths, axis=0)] + [fullest(share) for share in shares_of]),
            "cuts",
            axis=0,
        )
        total_count = jnp.sum(needs[:, 1]).astype(jnp.float32)
        most = jnp.max(needs[:, 2:], axis=0)
        share = jnp.int32(shares_of[-1])
        for index in range(len(shares_of) - 2, -1, -1):
            fits = (most[2 * index] <= room_source) & (most[2 * index + 1] <= room_target)
            share = jnp.where(fits, shares_of[index], share)
        members = jnp.arange(number, dtype=jnp.int32)
        taken = (members >= turn * share) & (members < (turn + 1) * share)
        source_taken = jnp.where(taken, lengths[:, 0], 0)
        target_taken = jnp.where(taken, lengths[:, 1], 0)
        more = (turn + 1) * share < number

        chosen = jnp.sum(
            jnp.where(
                task_ids[:, None] == jnp.arange(TASKS, dtype=jnp.int32)[None, :],
                task_counts[None, :],
                0,
            ),
            axis=1,
        ).astype(jnp.float32)
        slice_weight = jnp.sum(
            jnp.where(
                jnp.arange(cuts_count, dtype=jnp.int32) == cuts_rank,
                cuts_count * chosen / jnp.sum(chosen),
                0.0,
            )
        )

        stored_vocab = embedding.T.astype(jnp.bfloat16)
        vocab = gather_cuts(stored_vocab.reshape(2, -1, vocab_rows), cuts_rank, cuts_count)
        vocab = vocab.reshape(2, cuts_count, -1, vocab_rows).transpose(1, 0, 2, 3)
        vocab = vocab.reshape(MODEL_WIDTH, vocab_rows)
        stored = jnp.transpose(blocks, (1, 0, 2)).astype(jnp.bfloat16)
        weights = []
        for begin, end in ((0, 4), (4, 12), (12, 28)):
            columns = lax.all_gather(stored[begin:end], "fsdp", axis=2, tiled=True)
            weights.append(gather_cuts(columns, cuts_rank, cuts_count))

        source_segment, source_place, source_starts, source_ends = packing(source_taken, room_source)
        target_segment, target_place, target_starts, target_ends = packing(target_taken, room_target)
        source_real = source_segment < number
        target_real = target_segment < number
        packed_source = jnp.take(
            group_source.reshape(-1),
            jnp.where(source_real, source_segment * source_len + source_place, 0),
        )
        group_input = jnp.concatenate(
            [jnp.zeros_like(group_target[:, :1]), group_target[:, :-1]], axis=1
        )
        target_from = jnp.where(target_real, target_segment * target_len + target_place, 0)
        packed_target = jnp.take(group_target.reshape(-1), target_from)
        packed_input = jnp.take(group_input.reshape(-1), target_from)
        packed_ids = jnp.concatenate([packed_source, packed_input])
        packed_real = jnp.concatenate([source_real, target_real])
        vocab_places = jnp.arange(vocab_rows, dtype=jnp.int32)
        local_ids = jnp.where(packed_real, packed_ids - vocab_start, -1)
        source_total, target_total = jnp.sum(source_taken), jnp.sum(target_taken)
        chunk = 2 * TILE
        local_ids = jnp.pad(local_ids, (0, -local_ids.shape[0] % chunk), constant_values=-1)
        spans = jnp.stack(
            [
                jnp.minimum((source_total + chunk - 1) // chunk, room_source // chunk),
                jnp.int32(room_source // chunk),
                jnp.minimum(
                    (room_source + target_total + chunk - 1) // chunk,
                    local_ids.shape[0] // chunk,
                ),
            ]
        )
        rows = lax.psum(lookup_rows(local_ids, spans, vocab), "fsdp").astype(jnp.float32)
        source_stream, target_stream = (
            rows[:room_source],
            rows[room_source : room_source + room_target],
        )
        layout = (
            key_span(source_segment, source_total, source_starts, source_ends),
            key_span(target_segment, target_total, target_starts, target_ends),
            key_span(target_segment, target_total, source_starts, source_ends),
            source_segment[None, :],
            source_segment[:, None],
            target_segment[None, :],
            target_segment[:, None],
        )

        token_mask = target_real.astype(jnp.float32)
        token_weight = token_mask * (slice_weight / total_count)
        target_hit = vocab_places[None, :] == (packed_target - vocab_start)[:, None]

        def head(final_rows):
            logits = dot(final_rows, vocab)
            highest = jnp.max(logits, axis=1)
            total_exp = jnp.sum(jnp.exp(logits - highest[:, None]), axis=1)
            picked = jnp.sum(jnp.where(target_hit, logits, 0.0), axis=1)
            stats = lax.all_gather(jnp.stack([highest, total_exp, picked]), "fsdp", axis=0)
            top = jnp.max(stats[:, 0], axis=0)
            log_total = top + jnp.log(
                jnp.sum(stats[:, 1] * jnp.exp(stats[:, 0] - top[None, :]), axis=0)
            )
            token_loss = (log_total - jnp.sum(stats[:, 2], axis=0)) * token_mask
            grad_logits = (
                (jnp.exp(logits - log_total[:, None]) - target_hit.astype(jnp.float32))
                * token_weight[:, None]
            ).astype(jnp.bfloat16)
            grad_rows = lax.psum(dot_nt(grad_logits, vocab), "fsdp")
            return grad_rows, grad_logits, token_loss

        shares, gains, table, source_grad, target_grad, final_rows, grad_logits, token_loss = (
            packed_gradients(
                source_stream,
                target_stream,
                gain_rows,
                position_bias,
                (weights[0], weights[1], weights[2]),
                layout,
                head,
                fsdp_rank * blocks.shape[2],
                blocks.shape[2],
            )
        )
        lookups = jnp.concatenate([source_grad, target_grad]).astype(jnp.bfloat16)
        lookups = jnp.pad(lookups, ((0, local_ids.shape[0] - lookups.shape[0]), (0, 0)))
        left_embed = vocab_grad(left_embed, local_ids, spans, lookups, grad_logits, final_rows)
        return (
            more,
            turn + 1,
            total_count,
            slice_weight,
            left_blocks + shares,
            left_embed,
            gains_sum + gains,
            table_sum + table,
            loss_sum + jnp.sum(token_loss),
        )

    zero = jnp.zeros((), jnp.float32)
    _, _, total_count, slice_weight, left_blocks, left_embed, gains_grad, table_grad, loss_local = (
        lax.while_loop(
            lambda state: state[0],
            one_round,
            (
                jnp.ones((), jnp.bool_),
                jnp.zeros((), jnp.int32),
                zero,
                zero,
                jnp.transpose(error_blocks[0], (1, 0, 2)),
                error_embed[0],
                jnp.zeros_like(gain_rows),
                jnp.zeros_like(position_bias),
                zero,
            ),
        )
    )

    left_factor = jnp.einsum("kij,kjr->rki", left_blocks, right_blocks, precision=TOP_PRECISION)
    embed_factor = jnp.einsum("vd,vr->rd", left_embed, right_embed, precision=TOP_PRECISION)
    factor = jnp.concatenate([left_factor, embed_factor[:, None]], axis=1)
    factor, gains_grad, table_grad, loss_total = lax.psum(
        (factor, gains_grad * once, table_grad * once, loss_local * slice_weight * once),
        ("cuts", "fsdp"),
    )
    factor = orthonormal_rows(factor)
    left_factor, embed_factor = factor[:, :-1], factor[:, -1]
    factors_blocks = jnp.einsum("kij,rki->rkj", left_blocks, left_factor, precision=TOP_PRECISION)
    factors_embed = jnp.einsum("vd,rd->rv", left_embed, embed_factor, precision=TOP_PRECISION)
    rank = factors_blocks.shape[0]
    both = jnp.concatenate([factors_blocks.reshape(rank, -1), factors_embed], axis=1)
    both = lax.psum(both.astype(jnp.bfloat16), "cuts").astype(jnp.float32)
    factors_embed = both[:, -vocab_rows:]
    factors_blocks = both[:, :-vocab_rows].reshape(factors_blocks.shape)
    gram_blocks = jnp.einsum("rki,ski->krs", left_factor, left_factor, precision=TOP_PRECISION)
    gram_embed = jnp.einsum("rd,sd->rs", embed_factor, embed_factor, precision=TOP_PRECISION)
    squares = jnp.sum(
        factors_blocks
        * jnp.einsum("krs,skj->rkj", gram_blocks, factors_blocks, precision=TOP_PRECISION)
    ) + jnp.sum(factors_embed * jnp.dot(gram_embed, factors_embed, precision=TOP_PRECISION))
    squares = lax.psum(squares, "fsdp")
    full_blocks = jnp.einsum("rki,rkj->kij", left_factor, factors_blocks, precision=TOP_PRECISION)
    full_embed = jnp.einsum("rv,rd->vd", factors_embed, embed_factor, precision=TOP_PRECISION)
    owned_rows = blocks.shape[0]
    owned_columns = embedding.shape[1]
    own_left = lax.dynamic_slice_in_dim(left_factor, cuts_rank * owned_rows, owned_rows, 2)
    own_right = lax.dynamic_slice_in_dim(embed_factor, cuts_rank * owned_columns, owned_columns, 1)
    own_blocks = jnp.einsum("rki,rkj->ikj", own_left, factors_blocks, precision=TOP_PRECISION)
    own_embed = jnp.einsum("rv,rd->vd", factors_embed, own_right, precision=TOP_PRECISION)
    small_squares = jnp.sum(gains_grad * gains_grad) + jnp.sum(table_grad * table_grad)
    grad_norm = jnp.sqrt(squares + small_squares)
    clip_factor = jnp.minimum(1.0, CLIP_NORM / grad_norm)
    step_size = STEP_RATE * math.sqrt(PARAMS / MODEL_WIDTH) / CLIP_NORM
    embed_step = step_size * EMBED_SHARE * math.sqrt(MODEL_WIDTH)
    small_step = step_size * SMALL_SHARE * math.sqrt(MODEL_WIDTH)
    momentum_blocks = MOMENTUM_DECAY * blocks_momentum + (1.0 - MOMENTUM_DECAY) * (
        clip_factor * own_blocks
    )
    momentum_embed = MOMENTUM_DECAY * embed_momentum + (1.0 - MOMENTUM_DECAY) * (
        clip_factor * own_embed
    )
    momentum_gains = MOMENTUM_DECAY * gain_momentum + (1.0 - MOMENTUM_DECAY) * (
        clip_factor * gains_grad
    )
    momentum_bias = MOMENTUM_DECAY * bias_momentum + (1.0 - MOMENTUM_DECAY) * (
        clip_factor * table_grad
    )
    return (
        loss_total,
        total_count,
        grad_norm,
        blocks - step_size * momentum_blocks,
        momentum_blocks,
        embedding - embed_step * momentum_embed,
        momentum_embed,
        gain_rows - small_step * momentum_gains,
        momentum_gains,
        position_bias - small_step * momentum_bias,
        momentum_bias,
        jnp.transpose(factors_blocks, (1, 2, 0)),
        factors_embed.T,
        jnp.transpose(left_blocks - full_blocks, (1, 0, 2))[None],
        (left_embed - full_embed)[None],
    )


def solution(mesh):
    return jax.shard_map(
        local,
        mesh=mesh,
        in_specs=(
            P(("cuts", "fsdp"), None),
            P(("cuts", "fsdp"), None),
            P(("cuts", "fsdp")),
            P(("cuts", "fsdp")),
            P(),
            P(),
            P("cuts", None, "fsdp"),
            P("cuts", None, "fsdp"),
            P("fsdp", "cuts"),
            P("fsdp", "cuts"),
            P(),
            P(),
            P(),
            P(),
            P(None, "fsdp", None),
            P("fsdp", None),
            P("cuts", None, None, "fsdp"),
            P("cuts", "fsdp", None),
        ),
        out_specs=(
            P(),
            P(),
            P(),
            P("cuts", None, "fsdp"),
            P("cuts", None, "fsdp"),
            P("fsdp", "cuts"),
            P("fsdp", "cuts"),
            P(),
            P(),
            P(),
            P(),
            P(None, "fsdp", None),
            P("fsdp", None),
            P("cuts", None, None, "fsdp"),
            P("cuts", "fsdp", None),
        ),
        check_vma=False,
    )
```

time: 2680 us -> 1430 us (0.53)
  waiting for transfers between devices: 1160 us -> 290 us
  other arithmetic: 343 us -> 91.5 us
  matrix products: 558 us -> 330 us
  Pallas kernels: 0 us -> 142 us
  local copies, waits for them, and re-layouts: 376 us -> 253 us
  starting transfers between devices: 0.79 us -> 115 us
    all_gather x7 -> x2, waiting for transfers between devices: 509 us -> 0.01 us  [one_round(): columns = lax.all_gather(stored[begin:end], 'fsdp', axis=2, tiled=True)]
    reduce_scatter x5 -> x0, waiting for transfers between devices: 494 us -> none  [the longest x2 354 us: reduce_layer(): lax.psum_scatter(part_grads.astype(jnp.bfloat16), 'fsdp', scatter_dimensi...]
    dot_general x112 -> x102, matrix products: 556 us -> 330 us  [the longest x29 73.7 us: dot_nt(): lax.dot_general(left, right, (((1,), (1,)), ((), ())), preferred_element_...]
    pallas_call x0 -> x9, Pallas kernels: none -> 142 us  [the longest x3 46.7 us: packed_backward(): pl.pallas_call(lambda *refs: backward_kernel(causal, biased, *refs), grid...]
    ppermute x0 -> x56, starting transfers between devices: none -> 115 us  [swap(): lax.ppermute(array, 'cuts', [(i, i ^ mask) for i in range(cuts_count)])]
    unnamed x429 -> x56, local copies, waits for them, and re-layouts: 134 us -> 42.6 us
    ppermute x0 -> x56, waiting for transfers between devices: none -> 80.6 us  [swap(): lax.ppermute(array, 'cuts', [(i, i ^ mask) for i in range(cuts_count)])]
    dynamic_update_slice x6 -> x60, local copies, waits for them, and re-layouts: 0.25 us -> 80.3 us  [gather_cuts(): lax.dynamic_update_slice(whole, array[:, None], (0, jnp.bitwise_xor(cuts_...]
  transfers between devices with their start and end apart: 14 -> 62, of which waited for: 9 -> 14; matrix products, arithmetic and copies ran while one was open for 28% -> 16% of each run, Pallas kernels for 0% -> 3%
where the time goes in v1:
time: 1430 us; the launch traced here: 1440 us
  matrix products  330 us (23%)
  waiting for transfers between devices  290 us (20%)
  local copies, waits for them, and re-layouts  253 us (18%)
  blocking collectives  180 us (13%)
  Pallas kernels  142 us (10%)
  starting transfers between devices  115 us (8%)
  other arithmetic  91.5 us (6%)
  between operations  24.8 us (2%)
  loops' own time  15.6 us (1%)
    ppermute x56, starting transfers between devices, swap(): lax.ppermute(array, 'cuts', [(i, i ^ mask) for i in range(cuts_count)])  115 us
    psum x1, blocking collectives, local(): lax.psum((factor, gains_grad * once, table_grad * once, loss_local * slic...  94.5 us
    psum x1, waiting for transfers between devices, local(): lax.psum((factor, gains_grad * once, table_grad * once, loss_local * slic...  85.1 us
    ppermute x56, waiting for transfers between devices, swap(): lax.ppermute(array, 'cuts', [(i, i ^ mask) for i in range(cuts_count)])  80.6 us
    dynamic_update_slice x60, local copies, waits for them, and re-layouts, gather_cuts(): lax.dynamic_update_slice(whole, array[:, None], (0, jnp.bitwise_xor(cuts_...  80.3 us
    psum x1, waiting for transfers between devices, head(): grad_rows = lax.psum(dot_nt(grad_logits, vocab), 'fsdp')  74.7 us
    dot_general x29, matrix products, dot_nt(): lax.dot_general(left, right, (((1,), (1,)), ((), ())), preferred_element_...  73.7 us
    dot_general x28, matrix products, dot_tn(): lax.dot_general(left, right, (((0,), (0,)), ((), ())), preferred_element_...  59.2 us
  transfers between devices with their start and end apart: 62, of which 14 were waited for; matrix products, arithmetic and copies ran while one was open for 16% of the time, Pallas kernels for 3%

profile of v1, /device:TPU:0, one launch (start us, length us, event | category | flops | bytes accessed | tf_op | source)
XLA Modules:
  0.0 1442.2 jit_solution(17114729093444354013)
XLA Ops:
  8.0 18.1 %copy.880 = f32[1,8032,768]{2,1,0:T(8,128)} copy(f32[1,8032,768]{2,1,0:T(8,128)} %param.39) | data formatting | bytes 49348608
  29.9 6.6 copy.879
  42.9 16.2 %collective-permute-done.42 = bf16[1,48,8032]{2,1,0:T(8,128)(2,1)S(1)} collective-permute-done((bf16[1,48,8032]{2,1,0:T(8,128)(2,1)}, bf16[1,48,8032]{2,1,0:T(8,128)(2,1)S(1)}, u32[]{:S(2)}, u32[]{:S(2)}) %collective-permute-start.42) | collective-permute-done | bytes 771104 | tf_op jit(solution)/shard_map/while/body/ppermute | solution.py:64
  62.9 15.1 %collective-permute-done.43 = bf16[1,48,8032]{2,1,0:T(8,128)(2,1)} collective-permute-done((bf16[1,48,8032]{2,1,0:T(8,128)(2,1)}, bf16[1,48,8032]{2,1,0:T(8,128)(2,1)}, u32[]{:S(2)}, u32[]{:S(2)}) %collective-permute-start.43) | collective-permute-done | bytes 771104 | tf_op jit(solution)/shard_map/while/body/ppermute | solution.py:64
  78.3 13.8 all-gather.5
  95.3 7.8 all-reduce.4
  121.0 925.6 %while.30 = (pred[]{:T(512)}, s32[]{:T(128)}, f32[]{:T(128)}, f32[]{:T(128)}, f32[28,768,192]{1,2,0:T(8,128)}, /*index=5*/f32[8032,768]{1,0:T(8,128)}, f32[7,768...) while((pred[]{:T(512)}, s32[]{:T(128)}, f32[]{:T(128)}, ...), condition=%wide.region_60.62_spmd, body=%wide.region_6.61_spmd.sunk | while | flops 73191235584 | bytes 2375784192 | solution.py:825
  122.4 13.8 all-gather.8
  140.8 6.7 all-reduce.7
  190.2 7.1 gather_fusion.2
  197.8 10.5 pad_maximum_fusion.4
  208.3 25.5 %lookup.9 = bf16[1792,768]{1,0:T(8,128)(2,1)} custom-call(s32[3]{0:T(128)S(1)} %pad_add_fusion.3.refs_0_.blocks_ref, s32[1792,1]{1,0:T(8,128)S(1)} %broadcast_in_dim.1429.refs_1_, bf16[768,8032]{1,0:T(8,128)(2,1)} %bitcast.1165), custom_call_target="tpu_custom_call" | custom-call | tf_op jit(solution)/shard_map/while/body/lookup/pallas_call | solution.py:384
  233.9 17.5 %all_gather.103 = bf16[4,96,768]{1,0,2:T(4,128)(2,1)S(1)} all-gather(bf16[4,96,192]{1,0,2:T(4,128)(2,1)S(1)} %slice.1109), channel_id=1, replica_groups=mesh['cuts'=8,'fsdp'=4] {'fsdp'}, dimensions={2}, use_global_device_ids=true | all-gather | bytes 737280 | tf_op jit(solution)/shard_map/while/body/all_gather | solution.py:724
  256.5 12.9 collective-permute-start.3
  323.8 7.6 collective-permute-done.9
  364.6 8.7 collective-permute-done.21
  387.5 20.4 %attend.27 = (bf16[1280,768]{1,0:T(8,128)(2,1)S(1)}, f32[16,1280]{1,0:T(8,128)S(1)}) custom-call(s32[10]{0:T(128)S(1)} %get-tuple-element.2369.refs_0_, s32[10]{0:T(128)S(1)} %get-tuple-element.2370.refs_1_, bf16[1280,768]{1,0:T(8,128)(2,1)S(1)} %convolution_convert_fusion.26.refs_2_, bf16[1280,768]{1,0:T(8,128)(2,1)S(1)} %convolution_convert_fusion.27.refs_3_.refs_4_, ...), custom_call_target="tpu_custom_call" | custom-call | tf_op jit(solution)/shard_map/while/body/attend/pallas_call | solution.py:270
  415.5 22.3 %collective-permute-start.25 = (bf16[4,96,768]{2,1,0:T(8,128)(2,1)S(1)}, bf16[4,96,768]{2,1,0:T(8,128)(2,1)S(1)}, u32[]{:S(2)}, u32[]{:S(2)}) collective-permute-start(bf16[4,96,768]{2,1,0:T(8,128)(2,1)S(1)} %copy-done.168), channel_id=1, source_target_pairs={{0,4},{4,0},{8,12},{12,8},{16,20},{20,16},{24,28},{28,24},{1,5},{5... | collective-permute-start | bytes 1769480 | tf_op jit(solution)/shard_map/while/body/ppermute | solution.py:64
  459.2 46.6 %collective-permute-start.29 = (bf16[8,96,768]{2,1,0:T(8,128)(2,1)}, bf16[8,96,768]{2,1,0:T(8,128)(2,1)}, u32[]{:S(2)}, u32[]{:S(2)}) collective-permute-start(bf16[8,96,768]{2,1,0:T(8,128)(2,1)} %copy.745), channel_id=1, source_target_pairs={{0,8},{4,12},{8,0},{12,4},{16,24},{20,28},{24,16},{28,20},{1,9},{5... | collective-permute-start | bytes 3538952 | tf_op jit(solution)/shard_map/while/body/ppermute | solution.py:64
  551.4 6.8 collective-permute-done.35
  565.0 17.8 %collective-permute-done.30 = bf16[8,96,768]{2,1,0:T(8,128)(2,1)S(1)} collective-permute-done((bf16[8,96,768]{2,1,0:T(8,128)(2,1)}, bf16[8,96,768]{2,1,0:T(8,128)(2,1)S(1)}, u32[]{:S(2)}, u32[]{:S(2)}) %collective-permute-start.30) | collective-permute-done | bytes 1179680 | tf_op jit(solution)/shard_map/while/body/ppermute | solution.py:64
  609.3 8.8 attend.29
  630.1 9.1 fusion.868
  639.2 12.6 copy.748
  651.8 6.4 exponential_reduce_fusion.2
  658.3 6.4 select_reduce_fusion.35
  664.7 13.5 all-gather.9
  683.2 9.2 fusion.871
  695.7 74.7 %all-reduce.19.cloned.1.call-done = f32[384,768]{1,0:T(8,128)} async-done(((f32[384,768]{1,0:T(8,128)}), f32[384,768]{1,0:T(8,128)}) %all-reduce.19.cloned.1.call-update) | async-done | bytes 1179664 | tf_op jit(solution)/shard_map/while/body/psum | solution.py:792
  788.9 12.2 attend_back.27
  834.3 9.8 attend_back.29
  844.1 9.1 fusion.924
  874.7 24.7 %attend_back.28 = (bf16[1280,768]{1,0:T(8,128)(2,1)}, bf16[1280,768]{1,0:T(8,128)(2,1)}, bf16[1280,768]{1,0:T(8,128)(2,1)}, f32[5,12,128,128]{3,2,1,0:T(8,128)}) custom-call(s32[10]{0:T(128)} %copy-done.31, s32[10]{0:T(128)} %copy-done.30, bf16[1280,768]{1,0:T(8,128)(2,1)} %copy-done.7, bf16[1280,768]{1,0:T(8,128)(2,1)} %convolution_convert_fusion.36.refs_3_, ...), custom_call_target="tpu_custom_call" | custom-call | tf_op jit(solution)/shard_map/while/body/attend_back/pallas_call | solution.py:307
  899.5 9.1 fusion.925
  988.8 17.8 %add.2239 = f32[28,768,192]{1,2,0:T(8,128)} add(f32[28,768,192]{1,2,0:T(8,128)} %get-tuple-element.2559, f32[28,768,192]{1,2,0:T(8,128)} %fusion.917) | non-fusion elementwise | flops 4128768 | bytes 49545216 | tf_op jit(solution)/shard_map/while/body/add | solution.py:816
  1006.8 33.1 %vocab_grad.9 = f32[8032,768]{1,0:T(8,128)} custom-call(s32[3]{0:T(128)S(1)} %copy-done.33, s32[1,1792]{1,0:T(1,128)S(1)} %broadcast_in_dim.1433.id_ref, bf16[1792,768]{1,0:T(8,128)(2,1)S(1)} %fusion.923.grad_ref, bf16[384,8032]{1,0:T(8,128)(2,1)S(1)} %bitcast.1157, bf16[384,768]{1,0:T(8,128)(2,1)S(1)} %copy-done.19, ...), custom_call_target="tpu_custom_call", output_to_operand_aliasing={{}: (5, {})} | custom-call | tf_op jit(solution)/shard_map/while/body/vocab_grad/pallas_call | solution.py:423
  1046.6 11.5 fusion.285
  1058.4 15.1 %convolution_bitcast_fusion.29 = f32[8,768]{1,0:T(8,128)S(1)} fusion(f32[8032,768]{1,0:T(8,128)} %get-tuple-element.2861, f32[8032,8]{0,1:T(8,128)S(1)} %copy-done), kind=kOutput, calls=%fused_computation.557 | convolution fusion | flops 592183296 | bytes 24955904 | tf_op jit(solution)/shard_map/vd,vr->rd/dot_general | solution.py:843
  1074.6 94.5 %all-reduce.5 = (f32[]{:T(128)}, f32[7,768]{1,0:T(8,128)S(1)}, f32[2,32,12]{1,0,2:T(2,128)S(1)}) all-reduce(f32[]{:T(128)S(6)} %mul.2704, f32[7,768]{1,0:T(8,128)S(1)} %broadcast_multiply_fusion.1, f32[2,32,12]{1,0,2:T(2,128)S(1)} %copy_multiply_fusion), channel_id=1, replica_groups=mesh['cuts'=8,'fsdp'=4] {'cuts','fsdp'}, use_global_device_ids=true, to_apply=%region_61.63 | all-reduce | flops 6145 | bytes 49160 | tf_op jit(solution)/shard_map/psum | solution.py:845
  1171.6 85.1 %all-reduce.13.cloned.1.call-done.factor_ref = f32[8,29,768]{2,1,0:T(8,128)} async-done(((f32[8,29,768]{2,1,0:T(8,128)}), f32[8,29,768]{2,1,0:T(8,128)}) %all-reduce.13.cloned.1.call-update) | async-done | bytes 712720 | tf_op jit(solution)/shard_map/psum | solution.py:845
  1261.2 23.5 %convolution_convert_fusion.12 = bf16[8,8032]{1,0:T(8,128)(2,1)S(1)} fusion(f32[8032,768]{1,0:T(8,128)} %get-tuple-element.2861, f32[8,1,768]{2,1,0:T(1,128)S(1)} %slice.891), kind=kOutput, calls=%fused_computation.547 | convolution fusion | flops 592247552 | bytes 24827392 | tf_op jit(solution)/shard_map/vd,rd->rv/dot_general | solution.py:852
  1284.9 16.8 %fusion.225 = bf16[8,28,192]{2,0,1:T(8,128)(2,1)S(1)} fusion(f32[28,768,192]{1,2,0:T(8,128)} %get-tuple-element.2860, f32[8,28,768]{2,1,0:T(8,128)S(1)} %bitcast.1228), kind=kOutput, calls=%fused_computation.556 | convolution fusion | flops 396404736 | bytes 17289216 | tf_op jit(solution)/shard_map/kij,rki->rkj/dot_general | solution.py:851
  1305.2 49.9 %all-reduce.15.cloned.1.call-done = bf16[8,13408]{1,0:T(8,128)(2,1)} async-done(((bf16[8,13408]{1,0:T(8,128)(2,1)}), bf16[8,13408]{1,0:T(8,128)(2,1)}) %all-reduce.15.cloned.1.call-update) | async-done | bytes 214544 | tf_op jit(solution)/shard_map/psum | solution.py:855
  1362.3 13.6 subtract_bitcast_fusion.1
  1375.9 12.4 psum.75
  1390.3 6.1 multiply_subtract_fusion.1
  1403.1 22.8 %subtract_bitcast_fusion = f32[1,8032,768]{2,1,0:T(8,128)} fusion(f32[8032,768]{1,0:T(8,128)} %get-tuple-element.2861, bf16[8,13408]{1,0:T(8,128)(2,1)S(1)} %copy-done.174, f32[8,1,768]{2,1,0:T(1,128)S(1)} %slice.891), kind=kOutput, calls=%fused_computation.541 | convolution fusion | flops 598351872 | bytes 49502208 | tf_op jit(solution)/shard_map/rv,rd->vd/dot_general | solution.py:866
  1425.9 6.6 multiply_subtract_fusion
  (979 shorter events, 485.4 us)
Async XLA Ops:
  37.9 21.3 %collective-permute-start.42 = (bf16[1,48,8032]{2,1,0:T(8,128)(2,1)}, bf16[1,48,8032]{2,1,0:T(8,128)(2,1)S(1)}, u32[]{:S(2)}, u32[]{:S(2)}) collective-permute-start(bf16[1,48,8032]{2,1,0:T(8,128)(2,1)} %get-tuple-element.1938), channel_id=1, source_target_pairs={{0,8},{4,12},{8,0},{12,4},{16,24},{20,28},{24,16},{28,20},{1,9},{5... | collective-permute-start | bytes 2313224 | tf_op jit(solution)/shard_map/while/body/ppermute | solution.py:64
  40.8 20.5 %collective-permute-start.49 = (bf16[1,48,8032]{2,1,0:T(8,128)(2,1)}, bf16[1,48,8032]{2,1,0:T(8,128)(2,1)}, u32[]{:S(2)}, u32[]{:S(2)}) collective-permute-start(bf16[1,48,8032]{2,1,0:T(8,128)(2,1)} %get-tuple-element.1937), channel_id=1, source_target_pairs={{0,16},{4,20},{8,24},{12,28},{16,0},{20,4},{24,8},{28,12},{1,17},{... | collective-permute-start | bytes 2313224 | tf_op jit(solution)/shard_map/while/body/ppermute | solution.py:64
  42.4 35.6 %collective-permute-start.43 = (bf16[1,48,8032]{2,1,0:T(8,128)(2,1)}, bf16[1,48,8032]{2,1,0:T(8,128)(2,1)}, u32[]{:S(2)}, u32[]{:S(2)}) collective-permute-start(bf16[1,48,8032]{2,1,0:T(8,128)(2,1)} %get-tuple-element.1938), channel_id=1, source_target_pairs={{0,16},{4,20},{8,24},{12,28},{16,0},{20,4},{24,8},{28,12},{1,17},{... | collective-permute-start | bytes 2313224 | tf_op jit(solution)/shard_map/while/body/ppermute | solution.py:64
  42.9 35.1 %collective-permute-start.50 = (bf16[1,48,8032]{2,1,0:T(8,128)(2,1)}, bf16[1,48,8032]{2,1,0:T(8,128)(2,1)}, u32[]{:S(2)}, u32[]{:S(2)}) collective-permute-start(bf16[1,48,8032]{2,1,0:T(8,128)(2,1)} %get-tuple-element.1937), channel_id=1, source_target_pairs={{0,8},{4,12},{8,0},{12,4},{16,24},{20,28},{24,16},{28,20},{1,9},{5... | collective-permute-start | bytes 2313224 | tf_op jit(solution)/shard_map/while/body/ppermute | solution.py:64
  42.9 50.5 %collective-permute-start.45 = (bf16[1,48,8032]{2,1,0:T(8,128)(2,1)}, bf16[1,48,8032]{2,1,0:T(8,128)(2,1)S(1)}, u32[]{:S(2)}, u32[]{:S(2)}) collective-permute-start(bf16[1,48,8032]{2,1,0:T(8,128)(2,1)} %get-tuple-element.1938), channel_id=1, source_target_pairs={{0,4},{4,0},{8,12},{12,8},{16,20},{20,16},{24,28},{28,24},{1,5},{5... | collective-permute-start | bytes 2313224 | tf_op jit(solution)/shard_map/while/body/ppermute | solution.py:64
  59.2 34.4 %collective-permute-start.52 = (bf16[1,48,8032]{2,1,0:T(8,128)(2,1)}, bf16[1,48,8032]{2,1,0:T(8,128)(2,1)}, u32[]{:S(2)}, u32[]{:S(2)}) collective-permute-start(bf16[1,48,8032]{2,1,0:T(8,128)(2,1)} %get-tuple-element.1937), channel_id=1, source_target_pairs={{0,4},{4,0},{8,12},{12,8},{16,20},{20,16},{24,28},{28,24},{1,5},{5... | collective-permute-start | bytes 2313224 | tf_op jit(solution)/shard_map/while/body/ppermute | solution.py:64
  61.4 32.7 %collective-permute-start.44 = (bf16[1,48,8032]{2,1,0:T(8,128)(2,1)S(1)}, bf16[1,48,8032]{2,1,0:T(8,128)(2,1)}, u32[]{:S(2)}, u32[]{:S(2)}) collective-permute-start(bf16[1,48,8032]{2,1,0:T(8,128)(2,1)S(1)} %collective-permute-done.42), channel_id=1, source_target_pairs={{0,16},{4,20},{8,24},{12,28},{16,0},{20,4},{24,8},{28,12},{1,17},{... | collective-permute-start | bytes 2313224 | tf_op jit(solution)/shard_map/while/body/ppermute | solution.py:64
  77.9 16.7 %collective-permute-start.51 = (bf16[1,48,8032]{2,1,0:T(8,128)(2,1)}, bf16[1,48,8032]{2,1,0:T(8,128)(2,1)}, u32[]{:S(2)}, u32[]{:S(2)}) collective-permute-start(bf16[1,48,8032]{2,1,0:T(8,128)(2,1)} %collective-permute-done.49), channel_id=1, source_target_pairs={{0,8},{4,12},{8,0},{12,4},{16,24},{20,28},{24,16},{28,20},{1,9},{5... | collective-permute-start | bytes 2313224 | tf_op jit(solution)/shard_map/while/body/ppermute | solution.py:64
  78.0 16.7 %collective-permute-start.46 = (bf16[1,48,8032]{2,1,0:T(8,128)(2,1)S(1)}, bf16[1,48,8032]{2,1,0:T(8,128)(2,1)}, u32[]{:S(2)}, u32[]{:S(2)}) collective-permute-start(bf16[1,48,8032]{2,1,0:T(8,128)(2,1)S(1)} %collective-permute-done.42), channel_id=1, source_target_pairs={{0,4},{4,0},{8,12},{12,8},{16,20},{20,16},{24,28},{28,24},{1,5},{5... | collective-permute-start | bytes 2313224 | tf_op jit(solution)/shard_map/while/body/ppermute | solution.py:64
  93.5 26.2 %collective-permute-start.53 = (bf16[1,48,8032]{2,1,0:T(8,128)(2,1)}, bf16[1,48,8032]{2,1,0:T(8,128)(2,1)}, u32[]{:S(2)}, u32[]{:S(2)}) collective-permute-start(bf16[1,48,8032]{2,1,0:T(8,128)(2,1)} %collective-permute-done.49), channel_id=1, source_target_pairs={{0,4},{4,0},{8,12},{12,8},{16,20},{20,16},{24,28},{28,24},{1,5},{5... | collective-permute-start | bytes 2313224 | tf_op jit(solution)/shard_map/while/body/ppermute | solution.py:64
  93.6 26.1 %collective-permute-start.47 = (bf16[1,48,8032]{2,1,0:T(8,128)(2,1)}, bf16[1,48,8032]{2,1,0:T(8,128)(2,1)}, u32[]{:S(2)}, u32[]{:S(2)}) collective-permute-start(bf16[1,48,8032]{2,1,0:T(8,128)(2,1)} %collective-permute-done.43), channel_id=1, source_target_pairs={{0,4},{4,0},{8,12},{12,8},{16,20},{20,16},{24,28},{28,24},{1,5},{5... | collective-permute-start | bytes 2313224 | tf_op jit(solution)/shard_map/while/body/ppermute | solution.py:64
  94.1 25.6 %collective-permute-start.54 = (bf16[1,48,8032]{2,1,0:T(8,128)(2,1)}, bf16[1,48,8032]{2,1,0:T(8,128)(2,1)}, u32[]{:S(2)}, u32[]{:S(2)}) collective-permute-start(bf16[1,48,8032]{2,1,0:T(8,128)(2,1)} %collective-permute-done.50), channel_id=1, source_target_pairs={{0,4},{4,0},{8,12},{12,8},{16,20},{20,16},{24,28},{28,24},{1,5},{5... | collective-permute-start | bytes 2313224 | tf_op jit(solution)/shard_map/while/body/ppermute | solution.py:64
  94.6 25.1 %collective-permute-start.48 = (bf16[1,48,8032]{2,1,0:T(8,128)(2,1)}, bf16[1,48,8032]{2,1,0:T(8,128)(2,1)}, u32[]{:S(2)}, u32[]{:S(2)}) collective-permute-start(bf16[1,48,8032]{2,1,0:T(8,128)(2,1)} %collective-permute-done.44), channel_id=1, source_target_pairs={{0,4},{4,0},{8,12},{12,8},{16,20},{20,16},{24,28},{28,24},{1,5},{5... | collective-permute-start | bytes 2313224 | tf_op jit(solution)/shard_map/while/body/ppermute | solution.py:64
  94.6 25.1 %collective-permute-start.55 = (bf16[1,48,8032]{2,1,0:T(8,128)(2,1)}, bf16[1,48,8032]{2,1,0:T(8,128)(2,1)}, u32[]{:S(2)}, u32[]{:S(2)}) collective-permute-start(bf16[1,48,8032]{2,1,0:T(8,128)(2,1)} %collective-permute-done.51), channel_id=1, source_target_pairs={{0,4},{4,0},{8,12},{12,8},{16,20},{20,16},{24,28},{28,24},{1,5},{5... | collective-permute-start | bytes 2313224 | tf_op jit(solution)/shard_map/while/body/ppermute | solution.py:64
  121.2 216.2 %all-gather.13.cloned.1.call-start = ((), (), s32[]{:S(2)}) async-start(), calls=%async_computation.3 | async-start | bytes 1966080 | tf_op jit(solution)/shard_map/while/body/all_gather | solution.py:724
  122.3 253.7 %all-reduce.17.cloned.1.call-start = ((), (), s32[]{:S(2)}) async-start(), calls=%async_computation.2 | async-start | bytes 5505024 | tf_op jit(solution)/shard_map/while/body/psum | solution.py:758
  233.8 217.1 %all-gather.15.cloned.1.call-start = ((), (), s32[]{:S(2)}) async-start(), calls=%async_computation.4 | async-start | bytes 3932160 | tf_op jit(solution)/shard_map/while/body/all_gather | solution.py:724
  253.0 58.8 %collective-permute-start = (bf16[2,96,768]{2,1,0:T(8,128)(2,1)}, bf16[2,96,768]{2,1,0:T(8,128)(2,1)}, u32[]{:S(2)}, u32[]{:S(2)}) collective-permute-start(bf16[2,96,768]{2,1,0:T(8,128)(2,1)} %copy.739), channel_id=1, source_target_pairs={{0,16},{4,20},{8,24},{12,28},{16,0},{20,4},{24,8},{28,12},{1,17},{... | collective-permute-start | bytes 884744 | tf_op jit(solution)/shard_map/while/body/ppermute | solution.py:64
  253.0 59.8 %collective-permute-start.1 = (bf16[2,96,768]{2,1,0:T(8,128)(2,1)}, bf16[2,96,768]{2,1,0:T(8,128)(2,1)}, u32[]{:S(2)}, u32[]{:S(2)}) collective-permute-start(bf16[2,96,768]{2,1,0:T(8,128)(2,1)} %copy.739), channel_id=1, source_target_pairs={{0,8},{4,12},{8,0},{12,4},{16,24},{20,28},{24,16},{28,20},{1,9},{5... | collective-permute-start | bytes 884744 | tf_op jit(solution)/shard_map/while/body/ppermute | solution.py:64
  256.5 66.2 %collective-permute-start.3 = (bf16[2,96,768]{2,1,0:T(8,128)(2,1)}, bf16[2,96,768]{2,1,0:T(8,128)(2,1)}, u32[]{:S(2)}, u32[]{:S(2)}) collective-permute-start(bf16[2,96,768]{2,1,0:T(8,128)(2,1)} %copy.739), channel_id=1, source_target_pairs={{0,4},{4,0},{8,12},{12,8},{16,20},{20,16},{24,28},{28,24},{1,5},{5... | collective-permute-start | bytes 884744 | tf_op jit(solution)/shard_map/while/body/ppermute | solution.py:64
  270.5 45.0 %collective-permute-start.7 = (bf16[2,96,768]{2,1,0:T(8,128)(2,1)}, bf16[2,96,768]{2,1,0:T(8,128)(2,1)}, u32[]{:S(2)}, u32[]{:S(2)}) collective-permute-start(bf16[2,96,768]{2,1,0:T(8,128)(2,1)} %copy.740), channel_id=1, source_target_pairs={{0,8},{4,12},{8,0},{12,4},{16,24},{20,28},{24,16},{28,20},{1,9},{5... | collective-permute-start | bytes 884744 | tf_op jit(solution)/shard_map/while/body/ppermute | solution.py:64
  270.8 46.7 %collective-permute-start.8 = (bf16[2,96,768]{2,1,0:T(8,128)(2,1)}, bf16[2,96,768]{2,1,0:T(8,128)(2,1)}, u32[]{:S(2)}, u32[]{:S(2)}) collective-permute-start(bf16[2,96,768]{2,1,0:T(8,128)(2,1)} %copy.740), channel_id=1, source_target_pairs={{0,16},{4,20},{8,24},{12,28},{16,0},{20,4},{24,8},{28,12},{1,17},{... | collective-permute-start | bytes 884744 | tf_op jit(solution)/shard_map/while/body/ppermute | solution.py:64
  273.9 496.5 %all-reduce.19.cloned.1.call-start = ((), (), s32[]{:S(2)}) async-start(), calls=%async_computation.5 | async-start | bytes 2359296 | tf_op jit(solution)/shard_map/while/body/psum | solution.py:792
  311.8 21.0 %collective-permute-start.10 = (bf16[2,96,768]{2,1,0:T(8,128)(2,1)}, bf16[2,96,768]{2,1,0:T(8,128)(2,1)S(1)}, u32[]{:S(2)}, u32[]{:S(2)}) collective-permute-start(bf16[2,96,768]{2,1,0:T(8,128)(2,1)} %copy.740), channel_id=1, source_target_pairs={{0,4},{4,0},{8,12},{12,8},{16,20},{20,16},{24,28},{28,24},{1,5},{5... | collective-permute-start | bytes 884744 | tf_op jit(solution)/shard_map/while/body/ppermute | solution.py:64
  341.2 17.8 %collective-permute-start.14 = (bf16[4,96,768]{2,1,0:T(8,128)(2,1)}, bf16[4,96,768]{2,1,0:T(8,128)(2,1)}, u32[]{:S(2)}, u32[]{:S(2)}) collective-permute-start(bf16[4,96,768]{2,1,0:T(8,128)(2,1)} %copy.743), channel_id=1, source_target_pairs={{0,16},{4,20},{8,24},{12,28},{16,0},{20,4},{24,8},{28,12},{1,17},{... | collective-permute-start | bytes 1769480 | tf_op jit(solution)/shard_map/while/body/ppermute | solution.py:64
  344.3 16.6 %collective-permute-start.15 = (bf16[4,96,768]{2,1,0:T(8,128)(2,1)}, bf16[4,96,768]{2,1,0:T(8,128)(2,1)}, u32[]{:S(2)}, u32[]{:S(2)}) collective-permute-start(bf16[4,96,768]{2,1,0:T(8,128)(2,1)} %copy.743), channel_id=1, source_target_pairs={{0,8},{4,12},{8,0},{12,4},{16,24},{20,28},{24,16},{28,20},{1,9},{5... | collective-permute-start | bytes 1769480 | tf_op jit(solution)/shard_map/while/body/ppermute | solution.py:64
  346.0 69.5 %collective-permute-start.17 = (bf16[4,96,768]{2,1,0:T(8,128)(2,1)}, bf16[4,96,768]{2,1,0:T(8,128)(2,1)}, u32[]{:S(2)}, u32[]{:S(2)}) collective-permute-start(bf16[4,96,768]{2,1,0:T(8,128)(2,1)} %copy.743), channel_id=1, source_target_pairs={{0,4},{4,0},{8,12},{12,8},{16,20},{20,16},{24,28},{28,24},{1,5},{5... | collective-permute-start | bytes 1769480 | tf_op jit(solution)/shard_map/while/body/ppermute | solution.py:64
  347.7 25.6 %collective-permute-start.21 = (bf16[4,96,768]{2,1,0:T(8,128)(2,1)}, bf16[4,96,768]{2,1,0:T(8,128)(2,1)S(1)}, u32[]{:S(2)}, u32[]{:S(2)}) collective-permute-start(bf16[4,96,768]{2,1,0:T(8,128)(2,1)} %copy.744), channel_id=1, source_target_pairs={{0,8},{4,12},{8,0},{12,4},{16,24},{20,28},{24,16},{28,20},{1,9},{5... | collective-permute-start | bytes 1769480 | tf_op jit(solution)/shard_map/while/body/ppermute | solution.py:64
  348.0 26.2 %collective-permute-start.22 = (bf16[4,96,768]{2,1,0:T(8,128)(2,1)}, bf16[4,96,768]{2,1,0:T(8,128)(2,1)S(1)}, u32[]{:S(2)}, u32[]{:S(2)}) collective-permute-start(bf16[4,96,768]{2,1,0:T(8,128)(2,1)} %copy.744), channel_id=1, source_target_pairs={{0,16},{4,20},{8,24},{12,28},{16,0},{20,4},{24,8},{28,12},{1,17},{... | collective-permute-start | bytes 1769480 | tf_op jit(solution)/shard_map/while/body/ppermute | solution.py:64
  359.0 88.2 %collective-permute-start.24 = (bf16[4,96,768]{2,1,0:T(8,128)(2,1)}, bf16[4,96,768]{2,1,0:T(8,128)(2,1)}, u32[]{:S(2)}, u32[]{:S(2)}) collective-permute-start(bf16[4,96,768]{2,1,0:T(8,128)(2,1)} %copy.744), channel_id=1, source_target_pairs={{0,4},{4,0},{8,12},{12,8},{16,20},{20,16},{24,28},{28,24},{1,5},{5... | collective-permute-start | bytes 1769480 | tf_op jit(solution)/shard_map/while/body/ppermute | solution.py:64
  360.9 52.4 %collective-permute-start.16 = (bf16[4,96,768]{2,1,0:T(8,128)(2,1)}, bf16[4,96,768]{2,1,0:T(8,128)(2,1)}, u32[]{:S(2)}, u32[]{:S(2)}) collective-permute-start(bf16[4,96,768]{2,1,0:T(8,128)(2,1)} %collective-permute-done.14), channel_id=1, source_target_pairs={{0,8},{4,12},{8,0},{12,4},{16,24},{20,28},{24,16},{28,20},{1,9},{5... | collective-permute-start | bytes 1769480 | tf_op jit(solution)/shard_map/while/body/ppermute | solution.py:64
  373.3 66.5 %collective-permute-start.18 = (bf16[4,96,768]{2,1,0:T(8,128)(2,1)}, bf16[4,96,768]{2,1,0:T(8,128)(2,1)}, u32[]{:S(2)}, u32[]{:S(2)}) collective-permute-start(bf16[4,96,768]{2,1,0:T(8,128)(2,1)} %collective-permute-done.14), channel_id=1, source_target_pairs={{0,4},{4,0},{8,12},{12,8},{16,20},{20,16},{24,28},{28,24},{1,5},{5... | collective-permute-start | bytes 1769480 | tf_op jit(solution)/shard_map/while/body/ppermute | solution.py:64
  374.3 70.9 %collective-permute-start.19 = (bf16[4,96,768]{2,1,0:T(8,128)(2,1)}, bf16[4,96,768]{2,1,0:T(8,128)(2,1)}, u32[]{:S(2)}, u32[]{:S(2)}) collective-permute-start(bf16[4,96,768]{2,1,0:T(8,128)(2,1)} %collective-permute-done.15), channel_id=1, source_target_pairs={{0,4},{4,0},{8,12},{12,8},{16,20},{20,16},{24,28},{28,24},{1,5},{5... | collective-permute-start | bytes 1769480 | tf_op jit(solution)/shard_map/while/body/ppermute | solution.py:64
  413.6 28.3 %collective-permute-start.23 = (bf16[4,96,768]{2,1,0:T(8,128)(2,1)S(1)}, bf16[4,96,768]{2,1,0:T(8,128)(2,1)}, u32[]{:S(2)}, u32[]{:S(2)}) collective-permute-start(bf16[4,96,768]{2,1,0:T(8,128)(2,1)S(1)} %copy-done.168), channel_id=1, source_target_pairs={{0,16},{4,20},{8,24},{12,28},{16,0},{20,4},{24,8},{28,12},{1,17},{... | collective-permute-start | bytes 1769480 | tf_op jit(solution)/shard_map/while/body/ppermute | solution.py:64
  415.5 33.6 %collective-permute-start.25 = (bf16[4,96,768]{2,1,0:T(8,128)(2,1)S(1)}, bf16[4,96,768]{2,1,0:T(8,128)(2,1)S(1)}, u32[]{:S(2)}, u32[]{:S(2)}) collective-permute-start(bf16[4,96,768]{2,1,0:T(8,128)(2,1)S(1)} %copy-done.168), channel_id=1, source_target_pairs={{0,4},{4,0},{8,12},{12,8},{16,20},{20,16},{24,28},{28,24},{1,5},{5... | collective-permute-start | bytes 1769480 | tf_op jit(solution)/shard_map/while/body/ppermute | solution.py:64
  441.9 67.0 %collective-permute-start.20 = (bf16[4,96,768]{2,1,0:T(8,128)(2,1)}, bf16[4,96,768]{2,1,0:T(8,128)(2,1)}, u32[]{:S(2)}, u32[]{:S(2)}) collective-permute-start(bf16[4,96,768]{2,1,0:T(8,128)(2,1)} %collective-permute-done.16), channel_id=1, source_target_pairs={{0,4},{4,0},{8,12},{12,8},{16,20},{20,16},{24,28},{28,24},{1,5},{5... | collective-permute-start | bytes 1769480 | tf_op jit(solution)/shard_map/while/body/ppermute | solution.py:64
  445.3 63.9 %collective-permute-start.27 = (bf16[4,96,768]{2,1,0:T(8,128)(2,1)}, bf16[4,96,768]{2,1,0:T(8,128)(2,1)}, u32[]{:S(2)}, u32[]{:S(2)}) collective-permute-start(bf16[4,96,768]{2,1,0:T(8,128)(2,1)} %collective-permute-done.23), channel_id=1, source_target_pairs={{0,4},{4,0},{8,12},{12,8},{16,20},{20,16},{24,28},{28,24},{1,5},{5... | collective-permute-start | bytes 1769480 | tf_op jit(solution)/shard_map/while/body/ppermute | solution.py:64
  457.5 84.8 %collective-permute-start.28 = (bf16[8,96,768]{2,1,0:T(8,128)(2,1)}, bf16[8,96,768]{2,1,0:T(8,128)(2,1)}, u32[]{:S(2)}, u32[]{:S(2)}) collective-permute-start(bf16[8,96,768]{2,1,0:T(8,128)(2,1)} %copy.745), channel_id=1, source_target_pairs={{0,16},{4,20},{8,24},{12,28},{16,0},{20,4},{24,8},{28,12},{1,17},{... | collective-permute-start | bytes 3538952 | tf_op jit(solution)/shard_map/while/body/ppermute | solution.py:64
  459.2 92.2 %collective-permute-start.29 = (bf16[8,96,768]{2,1,0:T(8,128)(2,1)}, bf16[8,96,768]{2,1,0:T(8,128)(2,1)}, u32[]{:S(2)}, u32[]{:S(2)}) collective-permute-start(bf16[8,96,768]{2,1,0:T(8,128)(2,1)} %copy.745), channel_id=1, source_target_pairs={{0,8},{4,12},{8,0},{12,4},{16,24},{20,28},{24,16},{28,20},{1,9},{5... | collective-permute-start | bytes 3538952 | tf_op jit(solution)/shard_map/while/body/ppermute | solution.py:64
  505.8 78.2 %collective-permute-start.31 = (bf16[8,96,768]{2,1,0:T(8,128)(2,1)}, bf16[8,96,768]{2,1,0:T(8,128)(2,1)}, u32[]{:S(2)}, u32[]{:S(2)}) collective-permute-start(bf16[8,96,768]{2,1,0:T(8,128)(2,1)} %copy.745), channel_id=1, source_target_pairs={{0,4},{4,0},{8,12},{12,8},{16,20},{20,16},{24,28},{28,24},{1,5},{5... | collective-permute-start | bytes 3538952 | tf_op jit(solution)/shard_map/while/body/ppermute | solution.py:64
  508.8 49.3 %collective-permute-start.35 = (bf16[8,96,768]{2,1,0:T(8,128)(2,1)}, bf16[8,96,768]{2,1,0:T(8,128)(2,1)}, u32[]{:S(2)}, u32[]{:S(2)}) collective-permute-start(bf16[8,96,768]{2,1,0:T(8,128)(2,1)} %copy.746), channel_id=1, source_target_pairs={{0,8},{4,12},{8,0},{12,4},{16,24},{20,28},{24,16},{28,20},{1,9},{5... | collective-permute-start | bytes 3538952 | tf_op jit(solution)/shard_map/while/body/ppermute | solution.py:64
  509.1 53.1 %collective-permute-start.36 = (bf16[8,96,768]{2,1,0:T(8,128)(2,1)}, bf16[8,96,768]{2,1,0:T(8,128)(2,1)}, u32[]{:S(2)}, u32[]{:S(2)}) collective-permute-start(bf16[8,96,768]{2,1,0:T(8,128)(2,1)} %copy.746), channel_id=1, source_target_pairs={{0,16},{4,20},{8,24},{12,28},{16,0},{20,4},{24,8},{28,12},{1,17},{... | collective-permute-start | bytes 3538952 | tf_op jit(solution)/shard_map/while/body/ppermute | solution.py:64
  545.8 37.1 %collective-permute-start.30 = (bf16[8,96,768]{2,1,0:T(8,128)(2,1)}, bf16[8,96,768]{2,1,0:T(8,128)(2,1)S(1)}, u32[]{:S(2)}, u32[]{:S(2)}) collective-permute-start(bf16[8,96,768]{2,1,0:T(8,128)(2,1)} %collective-permute-done.28), channel_id=1, source_target_pairs={{0,8},{4,12},{8,0},{12,4},{16,24},{20,28},{24,16},{28,20},{1,9},{5... | collective-permute-start | bytes 3538952 | tf_op jit(solution)/shard_map/while/body/ppermute | solution.py:64
  551.4 35.6 %collective-permute-start.32 = (bf16[8,96,768]{2,1,0:T(8,128)(2,1)}, bf16[8,96,768]{2,1,0:T(8,128)(2,1)S(1)}, u32[]{:S(2)}, u32[]{:S(2)}) collective-permute-start(bf16[8,96,768]{2,1,0:T(8,128)(2,1)} %collective-permute-done.28), channel_id=1, source_target_pairs={{0,4},{4,0},{8,12},{12,8},{16,20},{20,16},{24,28},{28,24},{1,5},{5... | collective-permute-start | bytes 3538952 | tf_op jit(solution)/shard_map/while/body/ppermute | solution.py:64
  558.1 28.7 %collective-permute-start.37 = (bf16[8,96,768]{2,1,0:T(8,128)(2,1)}, bf16[8,96,768]{2,1,0:T(8,128)(2,1)S(1)}, u32[]{:S(2)}, u32[]{:S(2)}) collective-permute-start(bf16[8,96,768]{2,1,0:T(8,128)(2,1)} %collective-permute-done.35), channel_id=1, source_target_pairs={{0,16},{4,20},{8,24},{12,28},{16,0},{20,4},{24,8},{28,12},{1,17},{... | collective-permute-start | bytes 3538952 | tf_op jit(solution)/shard_map/while/body/ppermute | solution.py:64
  562.3 25.3 %collective-permute-start.33 = (bf16[8,96,768]{2,1,0:T(8,128)(2,1)}, bf16[8,96,768]{2,1,0:T(8,128)(2,1)S(1)}, u32[]{:S(2)}, u32[]{:S(2)}) collective-permute-start(bf16[8,96,768]{2,1,0:T(8,128)(2,1)} %collective-permute-done.29), channel_id=1, source_target_pairs={{0,4},{4,0},{8,12},{12,8},{16,20},{20,16},{24,28},{28,24},{1,5},{5... | collective-permute-start | bytes 3538952 | tf_op jit(solution)/shard_map/while/body/ppermute | solution.py:64
  1046.6 210.1 %all-reduce.13.cloned.1.call-start = ((), (), s32[]{:S(2)}) async-start(), calls=%async_computation | async-start | bytes 1572864 | tf_op jit(solution)/shard_map/psum | solution.py:845
  1074.5 280.6 %all-reduce.15.cloned.1.call-start = ((), (), s32[]{:S(2)}) async-start(), calls=%async_computation.1 | async-start | bytes 430080 | tf_op jit(solution)/shard_map/psum | solution.py:855
  (270 other events, 6669.4 us)
Sparse Core Ops, SparseCore 0:
  123.6 37.3 all-gather.12
  233.9 123.3 all-reduce.16
  358.9 62.5 all-gather.14
  695.1 75.2 all-reduce.18
Sparse Core Ops, SparseCore 1:
  1074.6 182.1 all-reduce.12
  1304.5 50.6 all-reduce.14

commit v2 on v1

v2 whole, which is shorter than its diff:
```python
import itertools
import math

import jax
import jax.numpy as jnp
from jax import lax
from jax.experimental import pallas as pl
from jax.experimental.layout import Layout, with_layout_constraint
from jax.experimental.pallas import tpu as pltpu
from jax.sharding import PartitionSpec as P

MODEL_WIDTH = 768
H = 12
DH = 64
FEED_UNITS = 3072
NBK = 32
TASKS = 8
PARAMS = 41189376


EPSILON = 1e-06
MASKED = -1000000000.0
CLIP_NORM = 0.05
MOMENTUM_DECAY = 0.9
STEP_RATE = 5.0
EMBED_SHARE = 50.0
SMALL_SHARE = 1.0 / 7.0
TOP_PRECISION = lax.Precision.HIGHEST
TILE = 128
ROOM_SOURCE = 1280
ROOM_TARGET = 384
ENCODER_EDGES = (12, 16, 23, 32, 46, 64, 91)
DECODER_EDGES = (19, 21, 24, 27, 31, 35, 40, 46, 52, 59, 67, 77, 87, 99, 113)


def root_norm(stream, gain_row):
    return (
        stream * lax.rsqrt(jnp.mean(stream * stream, axis=-1, keepdims=True) + EPSILON) * gain_row
    )


def norm_backward(stream, gain_row, grad_normed):
    _, pull_back = jax.vjp(root_norm, stream, gain_row)
    return pull_back(grad_normed)


def dot(left, right):
    return jnp.dot(left, right, preferred_element_type=jnp.float32)


def dot_nt(left, right):
    return lax.dot_general(left, right, (((1,), (1,)), ((), ())), preferred_element_type=jnp.float32)


def dot_tn(left, right):
    return lax.dot_general(left, right, (((0,), (0,)), ((), ())), preferred_element_type=jnp.float32)


def exchange(array, mask):
    return lax.ppermute(array, "cuts", [(i, i ^ mask) for i in range(lax.axis_size("cuts"))])


def shifted(array, distance):
    count = lax.axis_size("fsdp")
    return lax.ppermute(array, "fsdp", [(i, (i + distance) % count) for i in range(count)])


def in_order(pieces, rank):
    count = len(pieces)
    ordered = []
    for place in range(count):
        chosen = pieces[-place % count]
        for own in range(1, count):
            chosen = jnp.where(rank == own, pieces[(own - place) % count], chosen)
        ordered.append(chosen)
    return ordered


def gather_fsdp(part, rank):
    count = lax.axis_size("fsdp")
    return in_order([part] + [shifted(part, distance) for distance in range(1, count)], rank)


def sum_fsdp(part, rank):
    count = lax.axis_size("fsdp")
    rows = part.shape[0] // count
    low = part.astype(jnp.bfloat16)
    total = lax.dynamic_slice_in_dim(part, rank * rows, rows, 0)
    for distance in range(1, count):
        piece = lax.dynamic_slice_in_dim(low, (rank + distance) % count * rows, rows, 0)
        total = total + shifted(piece, distance).astype(jnp.float32)
    return jnp.concatenate(gather_fsdp(total.astype(jnp.bfloat16), rank), axis=0).astype(jnp.float32)


def sum_everywhere(part, cuts_rank):
    count = lax.axis_size("cuts")
    masks = [1 << bit for bit in range(count.bit_length() - 1)]
    if count & (count - 1) or part.shape[0] % count:
        return lax.psum(part, ("cuts", "fsdp"))
    bits = [(cuts_rank // mask) % 2 for mask in masks]
    for mask, bit in zip(masks, bits):
        half = part.shape[0] // 2
        away = lax.dynamic_slice_in_dim(part, (1 - bit) * half, half, 0)
        part = lax.dynamic_slice_in_dim(part, bit * half, half, 0) + exchange(away, mask)
    part = jnp.sum(lax.all_gather(part, "fsdp", axis=0), axis=0)
    for mask, bit in zip(masks[::-1], bits[::-1]):
        other = exchange(part, mask)
        part = jnp.where(
            bit == 1, jnp.concatenate([other, part], axis=0), jnp.concatenate([part, other], axis=0)
        )
    return part


def sum_cuts(part):
    count = lax.axis_size("cuts")
    if count & (count - 1):
        return lax.psum(part.astype(jnp.bfloat16), "cuts").astype(jnp.float32)
    for bit in range(count.bit_length() - 1):
        low = part.astype(jnp.bfloat16)
        part = low.astype(jnp.float32) + exchange(low, 1 << bit).astype(jnp.float32)
    return part


def spread_ways():
    return [1 << bit for bit in range(1, lax.axis_size("cuts").bit_length() - 1)]


def spread_begin(part):
    number = max(min(len(spread_ways()), part.shape[0]), 1)
    ends = [part.shape[0] * turn // number for turn in range(number + 1)]
    return [([0], part[None, begin:end]) for begin, end in zip(ends, ends[1:])]


def spread_step(shares, step):
    ways = spread_ways()
    after = []
    for turn, (bits, held) in enumerate(shares):
        mask = ways[(turn + step) % len(ways)]
        after.append(
            (bits + [bit ^ mask for bit in bits], jnp.concatenate([held, exchange(held, mask)]))
        )
    return after


def spread_end(shares):
    found, first = [], 0
    for bits, held in shares:
        found.append((first, [(bits, held), ([bit ^ 1 for bit in bits], exchange(held, 1))]))
        first += held.shape[1]
    return found


def spread_tied(shares, *others):
    arrays, others = lax.optimization_barrier(([held for _, held in shares], others))
    return [(bits, held) for (bits, _), held in zip(shares, arrays)], *others


def cost(flops, moved, powers=0):
    return pl.CostEstimate(flops=int(flops), bytes_accessed=int(moved), transcendentals=int(powers))


def place_kernel(moves, number, rank_ref, *refs):
    sources, outs, sem = refs[:number], refs[number:-1], refs[-1]
    rank = rank_ref[0]
    copies = []
    for source, piece, index, bits, (out, pitch, row, column), shape in moves:
        rows = pl.ds(pl.multiple_of((rank ^ bits) * pitch + row, 16), shape[0])
        copies.append(
            pltpu.make_async_copy(
                sources[source].at[piece, index],
                outs[out].at[rows, pl.ds(column, shape[1])],
                sem.at[len(copies)],
            )
        )
    for copy in copies:
        copy.start()
    for copy in copies:
        copy.wait()


def place_pieces(found, groups, rank):
    count = lax.axis_size("cuts")
    height, width = found[0][1][0][1].shape[2:]
    where = {}
    shapes = []
    for out, (members, how) in enumerate(groups):
        for order, matrix in enumerate(members):
            row = {"columns": 0, "rows": order * count * height, "mixed": order * height}[how]
            pitch = height * (len(members) if how == "mixed" else 1)
            where[matrix] = (out, pitch, row, order * width if how == "columns" else 0)
        tall, wide = (1, len(members)) if how == "columns" else (len(members), 1)
        shapes.append((tall * count * height, wide * width))
    sources, moves = [], []
    for first, held in found:
        for bits, array in held:
            for piece, index in itertools.product(range(array.shape[0]), range(array.shape[1])):
                if first + index in where:
                    moves.append(
                        (len(sources), piece, index, bits[piece], where[first + index], (height, width))
                    )
            sources.append(array)
    space = pl.BlockSpec(memory_space=pl.ANY)
    return pl.pallas_call(
        lambda *refs: place_kernel(moves, len(sources), *refs),
        in_specs=[pl.BlockSpec(memory_space=pltpu.SMEM)] + [space] * len(sources),
        out_specs=[pl.BlockSpec(memory_space=pltpu.VMEM)] * len(shapes),
        out_shape=[jax.ShapeDtypeStruct(shape, sources[0].dtype) for shape in shapes],
        scratch_shapes=[pltpu.SemaphoreType.DMA((len(moves),))],
        compiler_params=pltpu.CompilerParams(vmem_limit_bytes=40 << 20),
        cost_estimate=cost(0, 5 * sum(math.prod(shape) for shape in shapes)),
        name="place",
    )(rank[None], *sources)


def unset_kernel(out_ref):
    pass


def unset(shape):
    return pl.pallas_call(
        unset_kernel,
        out_specs=pl.BlockSpec(memory_space=pl.ANY),
        out_shape=jax.ShapeDtypeStruct(shape, jnp.float32),
        name="unset",
    )()


PAIRS = H // 2
WIDE = 2 * TILE


def offset_buckets(causal, offset):
    if causal:
        distance = jnp.maximum(-offset, 0)
        farther = 16 + sum(((distance >= boundary).astype(jnp.int32) for boundary in DECODER_EDGES))
        bucket = jnp.where(distance < 16, distance, farther)
    else:
        distance = jnp.abs(offset)
        farther = 8 + sum(((distance >= boundary).astype(jnp.int32) for boundary in ENCODER_EDGES))
        bucket = jnp.where(distance < 8, distance, farther) + jnp.where(offset > 0, 16, 0)
    return (bucket[..., None] == jnp.arange(NBK, dtype=jnp.int32)).astype(jnp.float32)


def bias_kernel(row_ref, out_ref):
    for head in range(H):
        row = jnp.broadcast_to(row_ref[0, head : head + 1, :], (TILE, WIDE))
        tile = pltpu.roll(row, 0, 1, stride=1, stride_axis=0)[:, :TILE]
        out_ref[0, head // 2, :, (head % 2) * TILE : (head % 2 + 1) * TILE] = tile


def bias_tiles(causal, table):
    lane = jnp.arange(WIDE, dtype=jnp.int32)
    offset = (jnp.arange(5, dtype=jnp.int32)[:, None] - 2) * TILE + jnp.where(
        lane < TILE, -lane, WIDE - lane
    )
    rows = jnp.einsum(
        "tqb,bh->thq", offset_buckets(causal, offset), table, precision=TOP_PRECISION
    )
    return pl.pallas_call(
        bias_kernel,
        grid=(5,),
        in_specs=[pl.BlockSpec((1, 16, WIDE), lambda i: (i, 0, 0))],
        out_specs=pl.BlockSpec((1, PAIRS, TILE, WIDE), lambda i: (i, 0, 0, 0)),
        out_shape=jax.ShapeDtypeStruct((5, PAIRS, TILE, WIDE), jnp.float32),
        name="bias",
    )(jnp.pad(rows, ((0, 0), (0, 16 - H), (0, 0))))


def bias_grad(tiles, causal):
    places = jnp.arange(TILE, dtype=jnp.int32)
    offset = (
        (jnp.arange(5, dtype=jnp.int32)[:, None, None] - 2) * TILE
        + places[None, :, None]
        - places[None, None, :]
    )
    hot = offset_buckets(causal, offset)
    found = [
        jnp.einsum("tpkq,tkqb->bp", tiles[..., half], hot, precision=lax.Precision.HIGH)
        for half in (slice(0, TILE), slice(TILE, WIDE))
    ]
    return jnp.stack(found, axis=-1).reshape(NBK, H)


def stack_heads(pair):
    half = lax.broadcasted_iota(jnp.int32, (TILE, TILE), 1) // DH
    return jnp.concatenate(
        [jnp.where(half == which, pair, jnp.zeros_like(pair)) for which in range(2)], axis=0
    )


def own_features(wide):
    return jnp.concatenate([wide[:DH, :TILE], wide[DH:, TILE:]], axis=0)


def kept(segment_column, segment_row, key_tile, query_tile, causal):
    keep = segment_column == jnp.concatenate([segment_row, segment_row], axis=1)
    if causal:
        key_place = key_tile * TILE + lax.broadcasted_iota(jnp.int32, (TILE, WIDE), 0)
        query_place = query_tile * TILE + lax.broadcasted_iota(jnp.int32, (TILE, WIDE), 1) % TILE
        keep = keep & (key_place <= query_place)
    return keep


def tile_scores(keys, queries, keep, bias):
    scores = dot_nt(keys, queries)
    if bias is not None:
        scores = scores + bias
    return jnp.where(keep, scores, MASKED)


def forward_kernel(
    causal, biased, first_ref, last_ref, q_ref, k_ref, v_ref, row_ref, column_ref, *rest
):
    bias_ref = rest[0] if biased else None
    out_ref, level_ref, stack_ref, top_ref, sum_ref, total_ref = rest[1:] if biased else rest
    here = pl.program_id(0)
    top_ref[...] = jnp.full_like(top_ref, -1e30)
    sum_ref[...] = jnp.zeros_like(sum_ref)
    total_ref[...] = jnp.zeros_like(total_ref)
    segment_row = row_ref[...]
    for pair in range(PAIRS):
        stack_ref[pair] = stack_heads(q_ref[:, pair * TILE : (pair + 1) * TILE])

    def step(there, carry):
        rows = pl.ds(pl.multiple_of(there * TILE, TILE), TILE)
        keep = kept(column_ref[rows, :], segment_row, there, here, causal)
        offset = jnp.clip(there - here, -2, 2) + 2
        before, sums = top_ref[...], sum_ref[...]
        tops, sums_after = [], []
        for pair in range(PAIRS):
            lanes = slice(pair * TILE, (pair + 1) * TILE)
            scores = tile_scores(
                k_ref[rows, lanes], stack_ref[pair], keep, bias_ref[offset, pair] if biased else None
            )
            old = before[pair : pair + 1, :]
            top = jnp.maximum(old, jnp.max(scores, axis=0, keepdims=True))
            weights = jnp.exp(scores - top)
            scale = jnp.exp(old - top)
            tops.append(top)
            sums_after.append(
                sums[pair : pair + 1, :] * scale + jnp.sum(weights, axis=0, keepdims=True)
            )
            total_ref[pair] = total_ref[pair] * scale + dot(
                v_ref[rows, lanes].T, weights.astype(jnp.bfloat16)
            )
        for pair in range(PAIRS):
            top_ref[pair : pair + 1, :] = tops[pair]
            sum_ref[pair : pair + 1, :] = sums_after[pair]
        return carry

    lax.fori_loop(first_ref[here], last_ref[here], step, 0)
    seen = sum_ref[...] > 0.0
    divisor = jnp.where(seen, sum_ref[...], 1.0)
    level_ref[...] = jnp.where(seen, top_ref[...] + jnp.log(divisor), 0.0)
    for pair in range(PAIRS):
        lanes = slice(pair * TILE, (pair + 1) * TILE)
        wide = total_ref[pair] / divisor[pair : pair + 1, :]
        out_ref[:, lanes] = own_features(wide).T.astype(jnp.bfloat16)


def backward_kernel(
    causal, biased, first_ref, last_ref, q_ref, o_ref, k_ref, v_ref, level_ref, row_ref, column_ref, *rest
):
    bias_ref = rest[0] if biased else None
    rest = rest[1:] if biased else rest
    gq_ref, gkv_ref = rest[:2]
    gb_ref = rest[2] if biased else None
    weight_ref, slope_ref, mean_ref, stack_ref, arrive_ref, tq_ref, tk_ref, tv_ref = rest[-8:]
    here = pl.program_id(0)

    @pl.when(here == 0)
    def _():
        tk_ref[...] = jnp.zeros_like(tk_ref)
        tv_ref[...] = jnp.zeros_like(tv_ref)
        if biased:
            gb_ref[...] = jnp.zeros_like(gb_ref)

    mean_ref[...] = jnp.zeros_like(mean_ref)
    tq_ref[...] = jnp.zeros_like(tq_ref)
    segment_row = row_ref[...]
    first = first_ref[here]
    last = last_ref[here]
    for pair in range(PAIRS):
        lanes = slice(pair * TILE, (pair + 1) * TILE)
        stack_ref[pair] = stack_heads(q_ref[:, lanes])
        arrive_ref[pair] = stack_heads(o_ref[:, lanes])

    def look(there, carry):
        rows = pl.ds(pl.multiple_of(there * TILE, TILE), TILE)
        keep = kept(column_ref[rows, :], segment_row, there, here, causal)
        offset = jnp.clip(there - here, -2, 2) + 2
        means = mean_ref[...]
        sums = []
        for pair in range(PAIRS):
            lanes = slice(pair * TILE, (pair + 1) * TILE)
            scores = tile_scores(
                k_ref[rows, lanes], stack_ref[pair], keep, bias_ref[offset, pair] if biased else None
            )
            weights = jnp.exp(scores - level_ref[pair : pair + 1, :])
            slopes = dot_nt(v_ref[rows, lanes], arrive_ref[pair])
            sums.append(
                means[pair : pair + 1, :] + jnp.sum(weights * slopes, axis=0, keepdims=True)
            )
            weight_ref[there - first, pair] = weights
            slope_ref[there - first, pair] = slopes
            tv_ref[rows, lanes] = tv_ref[rows, lanes] + dot(
                weights.astype(jnp.bfloat16), arrive_ref[pair]
            )
        for pair in range(PAIRS):
            mean_ref[pair : pair + 1, :] = sums[pair]
        return carry

    def push(there, carry):
        rows = pl.ds(pl.multiple_of(there * TILE, TILE), TILE)
        offset = jnp.clip(there - here, -2, 2) + 2
        for pair in range(PAIRS):
            lanes = slice(pair * TILE, (pair + 1) * TILE)
            slopes = (
                weight_ref[there - first, pair]
                * (slope_ref[there - first, pair] - mean_ref[pair : pair + 1, :])
            ).astype(jnp.bfloat16)
            if biased:
                gb_ref[offset, pair] = gb_ref[offset, pair] + slopes.astype(jnp.float32)
            tq_ref[pair] = tq_ref[pair] + dot(k_ref[rows, lanes].T, slopes)
            tk_ref[rows, lanes] = tk_ref[rows, lanes] + dot(slopes, stack_ref[pair])
        return carry

    lax.fori_loop(first, last, look, 0)
    lax.fori_loop(first, last, push, 0)
    for pair in range(PAIRS):
        lanes = slice(pair * TILE, (pair + 1) * TILE)
        gq_ref[:, lanes] = own_features(tq_ref[pair]).T.astype(jnp.bfloat16)

    @pl.when(here == pl.num_programs(0) - 1)
    def _():
        gkv_ref[:, :MODEL_WIDTH] = tk_ref[...].astype(jnp.bfloat16)
        gkv_ref[:, MODEL_WIDTH:] = tv_ref[...].astype(jnp.bfloat16)


def whole_block(shape):
    return pl.BlockSpec(shape, lambda i, *_: (0,) * len(shape))


def column_block(rows, index):
    return pl.BlockSpec((rows, MODEL_WIDTH), lambda i, *_: (0, index))


def packed_forward(queries, pair_rows, span, segment_row, segment_column, causal, bias):
    count, other = queries.shape[0], pair_rows.shape[0]
    biased = bias is not None
    tile = pl.BlockSpec((TILE, MODEL_WIDTH), lambda i, *_: (i, 0))
    return pl.pallas_call(
        lambda *refs: forward_kernel(causal, biased, *refs),
        grid_spec=pltpu.PrefetchScalarGridSpec(
            num_scalar_prefetch=2,
            grid=(count // TILE,),
            in_specs=[
                tile,
                column_block(other, 0),
                column_block(other, 1),
                pl.BlockSpec((1, TILE), lambda i, *_: (0, i)),
                whole_block((other, 1)),
            ]
            + ([whole_block((5, PAIRS, TILE, WIDE))] if biased else []),
            out_specs=[tile, pl.BlockSpec((8, WIDE), lambda i, *_: (0, i))],
            scratch_shapes=[
                pltpu.VMEM((PAIRS, WIDE, TILE), jnp.bfloat16),
                pltpu.VMEM((8, WIDE), jnp.float32),
                pltpu.VMEM((8, WIDE), jnp.float32),
                pltpu.VMEM((PAIRS, TILE, WIDE), jnp.float32),
            ],
        ),
        out_shape=[
            jax.ShapeDtypeStruct((count, MODEL_WIDTH), jnp.bfloat16),
            jax.ShapeDtypeStruct((8, 2 * count), jnp.float32),
        ],
        compiler_params=pltpu.CompilerParams(vmem_limit_bytes=40 << 20),
        cost_estimate=cost(8 * count * other * MODEL_WIDTH, 20 << 20),
        name="attend",
    )(*span, queries, pair_rows, pair_rows, segment_row, segment_column, *([bias] if biased else []))


def packed_backward(
    queries, grad_out, pair_rows, levels, span, segment_row, segment_column, causal, bias
):
    count, other = queries.shape[0], pair_rows.shape[0]
    biased = bias is not None
    reach = min(other // TILE, 9) if biased else other // TILE
    tile = pl.BlockSpec((TILE, MODEL_WIDTH), lambda i, *_: (i, 0))
    table = (5, PAIRS, TILE, WIDE)
    return pl.pallas_call(
        lambda *refs: backward_kernel(causal, biased, *refs),
        grid_spec=pltpu.PrefetchScalarGridSpec(
            num_scalar_prefetch=2,
            grid=(count // TILE,),
            in_specs=[
                tile,
                tile,
                column_block(other, 0),
                column_block(other, 1),
                pl.BlockSpec((8, WIDE), lambda i, *_: (0, i)),
                pl.BlockSpec((1, TILE), lambda i, *_: (0, i)),
                whole_block((other, 1)),
            ]
            + ([whole_block(table)] if biased else []),
            out_specs=[tile, whole_block((other, 2 * MODEL_WIDTH))]
            + ([whole_block(table)] if biased else []),
            scratch_shapes=[
                pltpu.VMEM((reach, PAIRS, TILE, WIDE), jnp.float32),
                pltpu.VMEM((reach, PAIRS, TILE, WIDE), jnp.float32),
                pltpu.VMEM((8, WIDE), jnp.float32),
                pltpu.VMEM((PAIRS, WIDE, TILE), jnp.bfloat16),
                pltpu.VMEM((PAIRS, WIDE, TILE), jnp.bfloat16),
                pltpu.VMEM((PAIRS, TILE, WIDE), jnp.float32),
                pltpu.VMEM((other, MODEL_WIDTH), jnp.float32),
                pltpu.VMEM((other, MODEL_WIDTH), jnp.float32),
            ],
        ),
        out_shape=[
            jax.ShapeDtypeStruct((count, MODEL_WIDTH), jnp.bfloat16),
            jax.ShapeDtypeStruct((other, 2 * MODEL_WIDTH), jnp.bfloat16),
        ]
        + ([jax.ShapeDtypeStruct(table, jnp.float32)] if biased else []),
        compiler_params=pltpu.CompilerParams(vmem_limit_bytes=58 << 20),
        cost_estimate=cost(20 * count * other * MODEL_WIDTH, 40 << 20),
        name="attend_back",
    )(
        *span,
        queries,
        grad_out,
        pair_rows,
        pair_rows,
        levels,
        segment_row,
        segment_column,
        *([bias] if biased else []),
    )


def lookup_kernel(rows_in, blocks_ref, id_ref, vocab_ref, out_ref, total_ref):
    step = pl.program_id(0)
    width = vocab_ref.shape[1]
    chunk = 2 * TILE

    @pl.when(step == 0)
    def _():
        total_ref[...] = jnp.zeros_like(total_ref)

    inside = step * width + lax.broadcasted_iota(jnp.int32, (1, width), 1) < rows_in
    table = jnp.where(inside, vocab_ref[...], jnp.zeros_like(vocab_ref[...]))
    places = step * width + lax.broadcasted_iota(jnp.int32, (chunk, width), 1)

    def one(index, carry):
        rows = pl.ds(pl.multiple_of(index * chunk, chunk), chunk)
        hot = (id_ref[rows, :] == places).astype(jnp.bfloat16)
        total_ref[rows, :] = total_ref[rows, :] + dot_nt(hot, table)
        return carry

    lax.fori_loop(0, blocks_ref[0], one, 0)
    lax.fori_loop(blocks_ref[1], blocks_ref[2], one, 0)

    @pl.when(step == pl.num_programs(0) - 1)
    def _():
        out_ref[...] = total_ref[...].astype(jnp.bfloat16)


def lookup_rows(local_ids, spans, vocab):
    count, width = local_ids.shape[0], 4 * TILE
    rows_in = vocab.shape[1]
    return pl.pallas_call(
        lambda *refs: lookup_kernel(rows_in, *refs),
        grid_spec=pltpu.PrefetchScalarGridSpec(
            num_scalar_prefetch=1,
            grid=(pl.cdiv(rows_in, width),),
            in_specs=[
                whole_block((count, 1)),
                pl.BlockSpec((MODEL_WIDTH, width), lambda i, *_: (0, i)),
            ],
            out_specs=whole_block((count, MODEL_WIDTH)),
            scratch_shapes=[pltpu.VMEM((count, MODEL_WIDTH), jnp.float32)],
        ),
        out_shape=jax.ShapeDtypeStruct((count, MODEL_WIDTH), jnp.bfloat16),
        compiler_params=pltpu.CompilerParams(vmem_limit_bytes=40 << 20),
        cost_estimate=cost(2 * count * rows_in * MODEL_WIDTH, 90 << 20),
        name="lookup",
    )(spans, local_ids[:, None], vocab)


def vocab_grad_kernel(blocks_ref, id_ref, grad_ref, logit_ref, final_ref, start_ref, left_ref, out_ref):
    step = pl.program_id(0)
    width = left_ref.shape[0]
    chunk = 2 * TILE
    before = jnp.where(blocks_ref[3] == 0, start_ref[...], left_ref[...])
    out_ref[...] = before + dot_tn(logit_ref[...], final_ref[...])
    places = step * width + lax.broadcasted_iota(jnp.int32, (width, chunk), 0)

    def one(index, carry):
        rows = pl.ds(pl.multiple_of(index * chunk, chunk), chunk)
        hot = (places == id_ref[:, rows]).astype(jnp.bfloat16)
        out_ref[...] = out_ref[...] + dot(hot, grad_ref[rows, :])
        return carry

    lax.fori_loop(0, blocks_ref[0], one, 0)
    lax.fori_loop(blocks_ref[1], blocks_ref[2], one, 0)


def vocab_grad(start, left, turn, local_ids, spans, lookups, grad_logits, final_rows):
    count, width = local_ids.shape[0], 4 * TILE
    rows_in = left.shape[0]
    block = pl.BlockSpec((width, MODEL_WIDTH), lambda i, *_: (i, 0))
    return pl.pallas_call(
        vocab_grad_kernel,
        grid_spec=pltpu.PrefetchScalarGridSpec(
            num_scalar_prefetch=1,
            grid=(pl.cdiv(rows_in, width),),
            in_specs=[
                whole_block((1, count)),
                whole_block((count, MODEL_WIDTH)),
                pl.BlockSpec((grad_logits.shape[0], width), lambda i, *_: (0, i)),
                whole_block(final_rows.shape),
                pl.BlockSpec((width, MODEL_WIDTH), lambda i, s: (jnp.where(s[3] == 0, i, 0), 0)),
                pl.BlockSpec((width, MODEL_WIDTH), lambda i, s: (jnp.where(s[3] == 0, 0, i), 0)),
            ],
            out_specs=block,
        ),
        out_shape=jax.ShapeDtypeStruct(left.shape, jnp.float32),
        input_output_aliases={6: 0},
        compiler_params=pltpu.CompilerParams(vmem_limit_bytes=40 << 20),
        cost_estimate=cost(2 * (count + 384) * rows_in * MODEL_WIDTH, 100 << 20),
        name="vocab_grad",
    )(
        jnp.concatenate([spans, turn[None]]),
        local_ids[None, :],
        lookups,
        grad_logits,
        final_rows,
        start,
        left,
    )


def packing(lengths, room):
    ends = jnp.cumsum(lengths)
    starts = ends - lengths
    places = jnp.arange(room, dtype=jnp.int32)
    segment = jnp.sum((places[:, None] >= ends[None, :]).astype(jnp.int32), axis=1)
    inside = segment[:, None] == jnp.arange(lengths.shape[0], dtype=jnp.int32)[None, :]
    position = places - jnp.sum(jnp.where(inside, starts[None, :], 0), axis=1)
    return segment, position, jnp.minimum(starts, room), jnp.minimum(ends, room)


def key_span(query_segment, query_total, key_starts, key_ends):
    number = key_starts.shape[0]
    count = query_segment.shape[0] // TILE
    begins = jnp.arange(count, dtype=jnp.int32) * TILE
    last_real = jnp.clip(query_total - 1, 0, query_segment.shape[0] - 1)
    finals = jnp.minimum(begins + TILE - 1, last_real)

    def pick(table, places):
        chosen = jnp.sum(
            jnp.where(
                jnp.arange(query_segment.shape[0], dtype=jnp.int32)[None, :] == places[:, None],
                query_segment[None, :],
                0,
            ),
            axis=1,
        )
        return jnp.sum(
            jnp.where(
                chosen[:, None] == jnp.arange(number, dtype=jnp.int32)[None, :], table[None, :], 0
            ),
            axis=1,
        )

    some = begins < query_total
    first = jnp.where(some, pick(key_starts, begins) // TILE, 0)
    last = jnp.where(some, (pick(key_ends, finals) + TILE - 1) // TILE, 0)
    return first, jnp.maximum(first, last)


def packed_gradients(
    source_stream, target_stream, gain_rows, position_bias, weights, layout, head, column_start, column_width
):
    enc_attention, enc_feed, dec_self, dec_cross, dec_feed = weights
    (
        source_span,
        target_span,
        cross_span,
        source_row,
        source_column,
        target_row,
        target_column,
    ) = layout
    bias_source = bias_tiles(False, position_bias[0])
    bias_target = bias_tiles(True, position_bias[1])

    def shard(grad, which=0):
        return lax.dynamic_slice_in_dim(grad, which * MODEL_WIDTH + column_start, column_width, 1)

    def attention(stream, gain_row, context, matrices, span, row, column, causal, bias):
        to_query, to_pair, outward = matrices
        normed = root_norm(stream, gain_row).astype(jnp.bfloat16)
        context = normed if context is None else context
        queries = dot(normed, to_query).astype(jnp.bfloat16)
        pair_rows = dot(context, to_pair).astype(jnp.bfloat16)
        attended, levels = packed_forward(queries, pair_rows, span, row, column, causal, bias)
        return stream + dot(attended, outward), (
            normed,
            context,
            queries,
            pair_rows,
            attended,
            levels,
        )

    def attention_back(grad, stream, gain_row, crossed, matrices, saved, span, row, column, causal, bias):
        to_query, to_pair, outward = matrices
        normed, context, queries, pair_rows, attended, levels = saved
        branch = grad.astype(jnp.bfloat16)
        arriving = dot_nt(branch, outward).astype(jnp.bfloat16)
        grads = packed_backward(
            queries, arriving, pair_rows, levels, span, row, column, causal, bias
        )
        grad_queries, grad_pair = grads[:2]
        pair_shards = [shard(grad_pair), shard(grad_pair, 1)]
        if crossed:
            shares = [
                dot_tn(shard(grad_queries), normed),
                dot_tn(jnp.concatenate(pair_shards, axis=1), context),
                dot_tn(shard(branch), attended),
            ]
        else:
            shares = [
                dot_tn(jnp.concatenate([shard(grad_queries)] + pair_shards, axis=1), normed),
                dot_tn(shard(branch), attended),
            ]
        grad_normed = dot_nt(grad_queries, to_query)
        grad_context = dot_nt(grad_pair, to_pair)
        if not crossed:
            grad_normed = grad_normed + grad_context
        grad_input, grad_gain = norm_backward(stream, gain_row, grad_normed)
        return grad + grad_input, grad_gain, shares, grads[2:], grad_context

    def feed(stream, gain_row, matrices):
        inward, outward = matrices
        normed = root_norm(stream, gain_row).astype(jnp.bfloat16)
        inner = dot(normed, inward)
        hidden = jax.nn.gelu(inner).astype(jnp.bfloat16)
        return stream + dot(hidden, outward), (normed, inner, hidden)

    def feed_back(grad, stream, gain_row, matrices, saved):
        inward, outward = matrices
        normed, inner, hidden = saved
        branch = grad.astype(jnp.bfloat16)
        grad_inner = jax.vjp(jax.nn.gelu, inner)[1](dot_nt(branch, outward))[0].astype(jnp.bfloat16)
        grad_normed = dot_nt(grad_inner, inward)
        inner_shards = jnp.concatenate([shard(grad_inner, j) for j in range(4)], axis=1)
        outward_shares = dot_tn(shard(branch), hidden)
        shares = [dot_tn(inner_shards, normed)] + [
            outward_shares[:, j * MODEL_WIDTH : (j + 1) * MODEL_WIDTH] for j in range(4)
        ]
        grad_input, grad_gain = norm_backward(stream, gain_row, grad_normed)
        return grad + grad_input, grad_gain, shares

    x1, enc_saved = attention(
        source_stream, gain_rows[0], None, enc_attention, source_span, source_row, source_column, False, bias_source
    )
    x2, enc_feed_saved = feed(x1, gain_rows[1], enc_feed)
    encoded = root_norm(x2, gain_rows[2]).astype(jnp.bfloat16)
    encoded, target_stream = lax.optimization_barrier((encoded, target_stream))
    target_stream = target_stream.astype(jnp.float32)
    y1, self_saved = attention(
        target_stream, gain_rows[3], None, dec_self, target_span, target_row, target_column, True, bias_target
    )
    y2, cross_saved = attention(
        y1, gain_rows[4], encoded, dec_cross, cross_span, target_row, source_column, False, None
    )
    y3, dec_feed_saved = feed(y2, gain_rows[5], dec_feed)
    final_rows = (root_norm(y3, gain_rows[6]) * MODEL_WIDTH ** (-0.5)).astype(jnp.bfloat16)

    grad_final, grad_logits, token_loss = head(final_rows)

    grad, gain_final = norm_backward(y3, gain_rows[6], grad_final * MODEL_WIDTH ** (-0.5))
    grad, gain_feed, feed_shares = feed_back(grad, y2, gain_rows[5], dec_feed, dec_feed_saved)
    grad, gain_cross, cross_shares, _, grad_encoded = attention_back(
        grad, y1, gain_rows[4], True, dec_cross, cross_saved, cross_span, target_row, source_column, False, None
    )
    target_grad, gain_self, self_shares, table_target, _ = attention_back(
        grad, target_stream, gain_rows[3], False, dec_self, self_saved, target_span, target_row, target_column, True, bias_target
    )
    grad, gain_encoded = norm_backward(x2, gain_rows[2], grad_encoded)
    grad, gain_enc_feed, enc_feed_shares = feed_back(grad, x1, gain_rows[1], enc_feed, enc_feed_saved)
    source_grad, gain_enc, enc_shares, table_source, _ = attention_back(
        grad, source_stream, gain_rows[0], False, enc_attention, enc_saved, source_span, source_row, source_column, False, bias_source
    )
    gains = jnp.stack(
        [gain_enc, gain_enc_feed, gain_encoded, gain_self, gain_cross, gain_feed, gain_final]
    )
    tables = jnp.stack(
        [
            bias_grad(table_source[0], False),
            bias_grad(table_target[0], True),
        ]
    )
    shares = jnp.concatenate(
        enc_shares + enc_feed_shares + self_shares + cross_shares + feed_shares
    ).reshape(-1, column_width, MODEL_WIDTH)
    return shares, gains, tables, source_grad, target_grad, final_rows, grad_logits, token_loss


def orthonormal_kernel(factor_ref, out_ref):
    rank = factor_ref.shape[0]
    for r in range(rank):
        out_ref[r] = factor_ref[r]
    for r in range(rank):
        row = out_ref[r]
        row = row * lax.rsqrt(jnp.sum(row * row, axis=-1, keepdims=True))
        out_ref[r] = row
        for s in range(r + 1, rank):
            other = out_ref[s]
            out_ref[s] = other - row * jnp.sum(row * other, axis=-1, keepdims=True)


def orthonormal_rows(factor):
    return pl.pallas_call(
        orthonormal_kernel,
        out_shape=jax.ShapeDtypeStruct(factor.shape, jnp.float32),
        name="orthonormal",
    )(factor)


def local(
    source_ids,
    targets,
    source_lengths,
    target_lengths,
    task_ids,
    task_counts,
    blocks,
    blocks_momentum,
    embedding,
    embed_momentum,
    gain_rows,
    gain_momentum,
    position_bias,
    bias_momentum,
    right_blocks,
    right_embed,
    error_blocks,
    error_embed,
):
    fsdp_rank = lax.axis_index("fsdp")
    cuts_rank = lax.axis_index("cuts")
    cuts_count = lax.axis_size("cuts")
    seq_count, source_len = source_ids.shape
    target_len = targets.shape[1]
    number = seq_count * lax.axis_size("fsdp")
    room_source = min(ROOM_SOURCE, source_len * number)
    room_target = min(ROOM_TARGET, target_len * number)
    fewest = min(room_source // source_len, room_target // target_len)
    shares_of = sorted({number, -(-number // 2), fewest}, reverse=True)
    vocab_rows = embedding.shape[0]
    vocab_start = fsdp_rank * vocab_rows
    once = (fsdp_rank == 0).astype(jnp.float32)

    stored_vocab = embedding.T.astype(jnp.bfloat16)
    steps = len(spread_ways())
    bands = max(n for n in range(1, max(steps, 1) + 1) if stored_vocab.shape[0] % (16 * n) == 0 or n == 1)
    vocab_shares = spread_begin(stored_vocab.reshape(bands, -1, vocab_rows))
    stored = jnp.transpose(blocks, (1, 0, 2)).astype(jnp.bfloat16)
    group = lax.all_gather(
        jnp.concatenate(
            [source_ids, targets, source_lengths[:, None], target_lengths[:, None]], axis=1
        ),
        "fsdp",
        axis=0,
        tiled=True,
    )
    group_source = group[:, :source_len]
    group_target = group[:, source_len : source_len + target_len]
    lengths = group[:, -2:]

    def fullest(share):
        padded = jnp.pad(lengths, ((0, -number % share), (0, 0)))
        return jnp.max(jnp.sum(padded.reshape(-1, share, 2), axis=1), axis=0)

    needs = lax.all_gather(
        jnp.concatenate([jnp.sum(lengths, axis=0)] + [fullest(share) for share in shares_of]),
        "cuts",
        axis=0,
    )
    for step in range(steps):
        if step:
            vocab_shares, needs = spread_tied(vocab_shares, needs)
        vocab_shares = spread_step(vocab_shares, step)
    stored, needs = lax.optimization_barrier((stored, needs))
    first_columns = jnp.concatenate(gather_fsdp(stored[:12], fsdp_rank), axis=2)
    errors = jnp.transpose(error_blocks[0], (1, 2, 0))
    vocab_shares, first_columns = spread_tied(vocab_shares, first_columns)
    first_shares = spread_begin(first_columns)
    first_shares = spread_step(first_shares, 0) if steps else first_shares
    vocab_pieces = spread_end(vocab_shares)
    piece_arrays = [[array for _, array in held] for _, held in vocab_pieces]
    first_arrays = [array for _, array in first_shares]
    given = (group, needs, piece_arrays, first_arrays, stored[12:], errors)

    def one_round(state):
        _, turn, _, _, left_blocks, left_embed, gains_sum, table_sum, loss_sum = state
        turn, group, needs, piece_arrays, first_arrays, stored_rest, errors = (
            lax.optimization_barrier((turn, *given))
        )
        group_source = group[:, :source_len]
        group_target = group[:, source_len : source_len + target_len]
        lengths = group[:, -2:]
        total_count = jnp.sum(needs[:, 1]).astype(jnp.float32)
        most = jnp.max(needs[:, 2:], axis=0)
        share = jnp.int32(shares_of[-1])
        for index in range(len(shares_of) - 2, -1, -1):
            fits = (most[2 * index] <= room_source) & (most[2 * index + 1] <= room_target)
            share = jnp.where(fits, shares_of[index], share)
        members = jnp.arange(number, dtype=jnp.int32)
        taken = (members >= turn * share) & (members < (turn + 1) * share)
        source_taken = jnp.where(taken, lengths[:, 0], 0)
        target_taken = jnp.where(taken, lengths[:, 1], 0)
        more = (turn + 1) * share < number

        chosen = jnp.sum(
            jnp.where(
                task_ids[:, None] == jnp.arange(TASKS, dtype=jnp.int32)[None, :],
                task_counts[None, :],
                0,
            ),
            axis=1,
        ).astype(jnp.float32)
        slice_weight = jnp.sum(
            jnp.where(
                jnp.arange(cuts_count, dtype=jnp.int32) == cuts_rank,
                cuts_count * chosen / jnp.sum(chosen),
                0.0,
            )
        )

        pieces = [
            (first, [(bits, array) for (bits, _), array in zip(held, own)])
            for (first, held), own in zip(vocab_pieces, piece_arrays)
        ]
        (vocab,) = place_pieces(pieces, ((tuple(range(bands)), "mixed"),), cuts_rank)
        shares = [(bits, array) for (bits, _), array in zip(first_shares, first_arrays)]
        rest_parts = [stored_rest] + [
            shifted(stored_rest, distance) for distance in range(1, lax.axis_size("fsdp"))
        ]
        for step in range(1, steps):
            shares = spread_step(shares, step)

        def attention_groups(first):
            return (
                ((first,), "columns"),
                ((first + 1, first + 2), "columns"),
                ((first + 3,), "columns"),
            )

        def feed_groups(first):
            return (
                (tuple(range(first, first + 4)), "columns"),
                (tuple(range(first + 4, first + 8)), "rows"),
            )

        source_segment, source_place, source_starts, source_ends = packing(source_taken, room_source)
        target_segment, target_place, target_starts, target_ends = packing(target_taken, room_target)
        source_real = source_segment < number
        target_real = target_segment < number
        packed_source = jnp.take(
            group_source.reshape(-1),
            jnp.where(source_real, source_segment * source_len + source_place, 0),
        )
        group_input = jnp.concatenate(
            [jnp.zeros_like(group_target[:, :1]), group_target[:, :-1]], axis=1
        )
        target_from = jnp.where(target_real, target_segment * target_len + target_place, 0)
        packed_target = jnp.take(group_target.reshape(-1), target_from)
        packed_input = jnp.take(group_input.reshape(-1), target_from)
        packed_ids = jnp.concatenate([packed_source, packed_input])
        packed_real = jnp.concatenate([source_real, target_real])
        vocab_places = jnp.arange(vocab_rows, dtype=jnp.int32)
        local_ids = jnp.where(packed_real, packed_ids - vocab_start, -1)
        source_total, target_total = jnp.sum(source_taken), jnp.sum(target_taken)
        chunk = 2 * TILE
        local_ids = jnp.pad(local_ids, (0, -local_ids.shape[0] % chunk), constant_values=-1)
        spans = jnp.stack(
            [
                jnp.minimum((source_total + chunk - 1) // chunk, room_source // chunk),
                jnp.int32(room_source // chunk),
                jnp.minimum(
                    (room_source + target_total + chunk - 1) // chunk,
                    local_ids.shape[0] // chunk,
                ),
            ]
        )
        rows = lookup_rows(local_ids, spans, vocab)
        shares, rows = spread_tied(shares, rows)
        first_placed = place_pieces(
            spread_end(shares), attention_groups(0) + feed_groups(4), cuts_rank
        )
        sizes = [room_source * part // 5 for part in (2, 3, 4, 5)]
        fullest_source = jnp.int32(room_source)
        for index in range(len(shares_of) - 1, -1, -1):
            fullest_source = jnp.where(share == shares_of[index], most[2 * index], fullest_source)
        source_rows = lax.switch(
            sum((fullest_source > size).astype(jnp.int32) for size in sizes[:-1]),
            [
                lambda table, size=size: jnp.pad(
                    lax.psum(table[:size], "fsdp"), ((0, room_source - size), (0, 0))
                )
                for size in sizes
            ],
            rows[:room_source],
        )
        source_rows, target_rows, table, rest_parts = lax.optimization_barrier(
            (source_rows, rows[room_source : room_source + room_target], position_bias, rest_parts)
        )
        rest_columns = jnp.concatenate(in_order(rest_parts, fsdp_rank), axis=2)
        rest_shares, first_placed = spread_tied(spread_begin(rest_columns), first_placed)
        for step in range(steps):
            rest_shares = spread_step(rest_shares, step)
        rest_pieces = spread_end(rest_shares)
        rest_attention = place_pieces(
            rest_pieces, attention_groups(0) + attention_groups(4), cuts_rank
        )
        rest_feed = place_pieces(rest_pieces, feed_groups(8), cuts_rank)
        weights = (
            first_placed[:3],
            first_placed[3:],
            rest_attention[:3],
            rest_attention[3:],
            rest_feed,
        )
        target_rows = lax.psum(target_rows, "fsdp")
        source_stream = source_rows.astype(jnp.float32)
        target_stream = target_rows
        layout = (
            key_span(source_segment, source_total, source_starts, source_ends),
            key_span(target_segment, target_total, target_starts, target_ends),
            key_span(target_segment, target_total, source_starts, source_ends),
            source_segment[None, :],
            source_segment[:, None],
            target_segment[None, :],
            target_segment[:, None],
        )

        token_mask = target_real.astype(jnp.float32)
        token_weight = token_mask * (slice_weight / total_count)
        target_hit = vocab_places[None, :] == (packed_target - vocab_start)[:, None]

        def head(final_rows):
            logits = dot(final_rows, vocab)
            highest = jnp.max(logits, axis=1)
            total_exp = jnp.sum(jnp.exp(logits - highest[:, None]), axis=1)
            picked = jnp.sum(jnp.where(target_hit, logits, 0.0), axis=1)
            stats = lax.all_gather(jnp.stack([highest, total_exp, picked]), "fsdp", axis=0)
            top = jnp.max(stats[:, 0], axis=0)
            log_total = top + jnp.log(
                jnp.sum(stats[:, 1] * jnp.exp(stats[:, 0] - top[None, :]), axis=0)
            )
            token_loss = (log_total - jnp.sum(stats[:, 2], axis=0)) * token_mask
            grad_logits = (
                (jnp.exp(logits - log_total[:, None]) - target_hit.astype(jnp.float32))
                * token_weight[:, None]
            ).astype(jnp.bfloat16)
            grad_rows = sum_fsdp(dot_nt(grad_logits, vocab), fsdp_rank)
            return grad_rows, grad_logits, token_loss

        shares, gains, table_found, source_grad, target_grad, final_rows, grad_logits, token_loss = (
            packed_gradients(
                source_stream,
                target_stream,
                gain_rows,
                table,
                weights,
                layout,
                head,
                fsdp_rank * blocks.shape[2],
                blocks.shape[2],
            )
        )
        lookups = jnp.concatenate([source_grad, target_grad]).astype(jnp.bfloat16)
        lookups = jnp.pad(lookups, ((0, local_ids.shape[0] - lookups.shape[0]), (0, 0)))
        left_embed = vocab_grad(
            error_embed[0], left_embed, turn, local_ids, spans, lookups, grad_logits, final_rows
        )
        before = jnp.where(turn == 0, errors, left_blocks)
        return (
            more,
            turn + 1,
            total_count,
            slice_weight,
            before + shares,
            left_embed,
            gains_sum + gains,
            table_sum + table_found,
            loss_sum + jnp.sum(token_loss),
        )

    zero = jnp.zeros((), jnp.float32)
    _, _, total_count, slice_weight, left_blocks, left_embed, gains_grad, table_grad, loss_local = (
        lax.while_loop(
            lambda state: state[0],
            one_round,
            (
                jnp.ones((), jnp.bool_),
                jnp.zeros((), jnp.int32),
                zero,
                zero,
                unset((blocks.shape[1], blocks.shape[2], MODEL_WIDTH)),
                unset((vocab_rows, MODEL_WIDTH)),
                jnp.zeros_like(gain_rows),
                jnp.zeros_like(position_bias),
                zero,
            ),
        )
    )

    left_factor = jnp.einsum("kji,kjr->rki", left_blocks, right_blocks, precision=lax.Precision.HIGH)
    embed_factor = jnp.einsum("vd,vr->rd", left_embed, right_embed, precision=lax.Precision.HIGH)
    rank, count = left_factor.shape[:2]
    small = jnp.concatenate(
        [
            gains_grad * once,
            (table_grad * once).reshape(-1, MODEL_WIDTH),
            jnp.full((1, MODEL_WIDTH), loss_local * slice_weight * once),
        ]
    )
    factor = jnp.concatenate([left_factor, embed_factor[:, None]], axis=1)
    packed = jnp.concatenate([factor.reshape(-1, MODEL_WIDTH), small])
    packed = jnp.pad(packed, ((0, -packed.shape[0] % (8 * cuts_count)), (0, 0)))
    packed = sum_everywhere(packed, cuts_rank)
    factor = packed[: rank * (count + 1)].reshape(factor.shape)
    small = packed[rank * (count + 1) :]
    gains_grad = small[: gain_rows.shape[0]]
    table_rows = position_bias.size // MODEL_WIDTH
    table_grad = small[gain_rows.shape[0] :][:table_rows].reshape(position_bias.shape)
    loss_total = small[gain_rows.shape[0] + table_rows, 0]
    factor = orthonormal_rows(factor)
    left_factor, embed_factor = factor[:, :-1], factor[:, -1]
    factors_blocks = jnp.einsum("kji,rki->rkj", left_blocks, left_factor, precision=lax.Precision.HIGH)
    factors_embed = jnp.einsum("vd,rd->rv", left_embed, embed_factor, precision=lax.Precision.HIGH)
    both = sum_cuts(jnp.concatenate([factors_blocks.reshape(rank, -1), factors_embed], axis=1))
    factors_embed = both[:, -vocab_rows:]
    factors_blocks = both[:, :-vocab_rows].reshape(factors_blocks.shape)
    gram_blocks = jnp.einsum("rki,ski->krs", left_factor, left_factor, precision=TOP_PRECISION)
    gram_embed = jnp.einsum("rd,sd->rs", embed_factor, embed_factor, precision=TOP_PRECISION)
    squares = jnp.sum(
        factors_blocks
        * jnp.einsum("krs,skj->rkj", gram_blocks, factors_blocks, precision=lax.Precision.HIGH)
    ) + jnp.sum(factors_embed * jnp.dot(gram_embed, factors_embed, precision=lax.Precision.HIGH))
    squares = lax.psum(squares, "fsdp")
    full_blocks = jnp.einsum("rki,rkj->kji", left_factor, factors_blocks, precision=lax.Precision.HIGH)
    full_embed = jnp.einsum("rv,rd->vd", factors_embed, embed_factor, precision=lax.Precision.HIGH)
    owned_rows = blocks.shape[0]
    owned_columns = embedding.shape[1]
    own_left = lax.dynamic_slice_in_dim(left_factor, cuts_rank * owned_rows, owned_rows, 2)
    own_right = lax.dynamic_slice_in_dim(embed_factor, cuts_rank * owned_columns, owned_columns, 1)
    own_blocks = jnp.einsum("rki,rkj->ikj", own_left, factors_blocks, precision=lax.Precision.HIGH)
    own_embed = jnp.einsum("rv,rd->vd", factors_embed, own_right, precision=lax.Precision.HIGH)
    small_squares = jnp.sum(gains_grad * gains_grad) + jnp.sum(table_grad * table_grad)
    grad_norm = jnp.sqrt(squares + small_squares)
    clip_factor = jnp.minimum(1.0, CLIP_NORM / grad_norm)
    step_size = STEP_RATE * math.sqrt(PARAMS / MODEL_WIDTH) / CLIP_NORM
    embed_step = step_size * EMBED_SHARE * math.sqrt(MODEL_WIDTH)
    small_step = step_size * SMALL_SHARE * math.sqrt(MODEL_WIDTH)
    momentum_blocks = MOMENTUM_DECAY * blocks_momentum + (1.0 - MOMENTUM_DECAY) * (
        clip_factor * own_blocks
    )
    momentum_embed = MOMENTUM_DECAY * embed_momentum + (1.0 - MOMENTUM_DECAY) * (
        clip_factor * own_embed
    )
    momentum_gains = MOMENTUM_DECAY * gain_momentum + (1.0 - MOMENTUM_DECAY) * (
        clip_factor * gains_grad
    )
    momentum_bias = MOMENTUM_DECAY * bias_momentum + (1.0 - MOMENTUM_DECAY) * (
        clip_factor * table_grad
    )
    return (
        loss_total,
        total_count,
        grad_norm,
        blocks - step_size * momentum_blocks,
        momentum_blocks,
        embedding - embed_step * momentum_embed,
        momentum_embed,
        gain_rows - small_step * momentum_gains,
        momentum_gains,
        position_bias - small_step * momentum_bias,
        momentum_bias,
        jnp.transpose(factors_blocks, (1, 2, 0)),
        factors_embed.T,
        jnp.transpose(left_blocks - full_blocks, (2, 0, 1))[None],
        (left_embed - full_embed)[None],
    )


def solution(mesh):
    return jax.shard_map(
        local,
        mesh=mesh,
        in_specs=(
            P(("cuts", "fsdp"), None),
            P(("cuts", "fsdp"), None),
            P(("cuts", "fsdp")),
            P(("cuts", "fsdp")),
            P(),
            P(),
            P("cuts", None, "fsdp"),
            P("cuts", None, "fsdp"),
            P("fsdp", "cuts"),
            P("fsdp", "cuts"),
            P(),
            P(),
            P(),
            P(),
            P(None, "fsdp", None),
            P("fsdp", None),
            P("cuts", None, None, "fsdp"),
            P("cuts", "fsdp", None),
        ),
        out_specs=(
            P(),
            P(),
            P(),
            P("cuts", None, "fsdp"),
            P("cuts", None, "fsdp"),
            P("fsdp", "cuts"),
            P("fsdp", "cuts"),
            P(),
            P(),
            P(),
            P(),
            P(None, "fsdp", None),
            P("fsdp", None),
            P("cuts", None, None, "fsdp"),
            P("cuts", "fsdp", None),
        ),
        check_vma=False,
    )
```

time: 1430 us -> 1100 us (0.77)
  local copies, waits for them, and re-layouts: 253 us -> 127 us
  blocking collectives: 180 us -> 57.1 us
  waiting for transfers between devices: 290 us -> 233 us
  matrix products: 330 us -> 294 us
  other arithmetic: 91.5 us -> 121 us
    psum x4 -> x2, waiting for transfers between devices: 210 us -> 74.4 us  [the longest x1 74.4 us: one_round(): lax.psum(table[:size], 'fsdp')]
    psum x1 -> x0, blocking collectives: 94.5 us -> none  [local(): lax.psum((factor, gains_grad * once, table_grad * once, loss_local * slic...]
    dynamic_update_slice x60 -> x0, local copies, waits for them, and re-layouts: 80.3 us -> none  [gather_cuts(): lax.dynamic_update_slice(whole, array[:, None], (0, jnp.bitwise_xor(cuts_...]
    ppermute x56 -> x39, waiting for transfers between devices: 80.6 us -> 159 us  [the longest x27 90.1 us: exchange(): lax.ppermute(array, 'cuts', [(i, i ^ mask) for i in range(lax.axis_size('...]
    dot_general x14 -> x16, matrix products: 147 us -> 109 us  [the longest x1 22.9 us: local(): jnp.einsum('rv,rd->vd', factors_embed, embed_factor, precision=lax.Precis...]
    pallas_call x0 -> x8, Pallas kernels: none -> 33.7 us  [the longest x4 24 us: place_pieces(): pl.pallas_call(lambda *refs: place_kernel(moves, len(sources), *refs), in...]
    pallas_call x3, Pallas kernels: 32.9 us -> 9.15 us  [packed_forward(): pl.pallas_call(lambda *refs: forward_kernel(causal, biased, *refs), grid_...]
    unnamed x56 -> x68, local copies, waits for them, and re-layouts: 42.6 us -> 19 us
  transfers between devices with their start and end apart: 62 -> 41, of which waited for: 14 -> 18; matrix products, arithmetic and copies ran while one was open for 16% -> 12% of each run, Pallas kernels for 3% -> 4%
where the time goes in v2:
time: 1100 us; the launch traced here: 1110 us
  matrix products  294 us (27%)
  waiting for transfers between devices  233 us (21%)
  Pallas kernels  131 us (12%)
  local copies, waits for them, and re-layouts  127 us (12%)
  other arithmetic  121 us (11%)
  starting transfers between devices  109 us (10%)
  blocking collectives  57.1 us (5%)
  between operations  21.3 us (2%)
  loops' own time  17.2 us (2%)
    ppermute x27, starting transfers between devices, exchange(): lax.ppermute(array, 'cuts', [(i, i ^ mask) for i in range(lax.axis_size('...  91.8 us
    ppermute x27, waiting for transfers between devices, exchange(): lax.ppermute(array, 'cuts', [(i, i ^ mask) for i in range(lax.axis_size('...  90.1 us
    dot_general x14, matrix products, dot_nt(): lax.dot_general(left, right, (((1,), (1,)), ((), ())), preferred_element_...  81 us
    psum x1, waiting for transfers between devices, one_round(): lax.psum(table[:size], 'fsdp')  74.4 us
    ppermute x12, waiting for transfers between devices, shifted(): lax.ppermute(array, 'fsdp', [(i, (i + distance) % count) for i in range(c...  68.7 us
    dot_general x14, matrix products, dot(): return jnp.dot(left, right, preferred_element_type=jnp.float32)  61.2 us
    dot_general x11, matrix products, dot_tn(): lax.dot_general(left, right, (((0,), (0,)), ((), ())), preferred_element_...  41.5 us
    while x351, local copies, waits for them, and re-layouts  36.6 us
  transfers between devices with their start and end apart: 41, of which 18 were waited for; matrix products, arithmetic and copies ran while one was open for 12% of the time, Pallas kernels for 4%

profile of v2, /device:TPU:0, one launch (start us, length us, event | category | flops | bytes accessed | tf_op | source)
XLA Modules:
  0.0 1111.8 jit_solution(4378089859848462187)
XLA Ops:
  14.3 13.3 %all-gather.4 = s32[4,2,642]{2,1,0:T(2,128)S(1)} all-gather(s32[1,2,642]{2,1,0:T(2,128)S(1)} %add_bitcast_fusion), channel_id=1, replica_groups=mesh['cuts'=8,'fsdp'=4] {'fsdp'}, dimensions={0}, use_global_device_ids=true | all-gather | bytes 25680 | tf_op jit(solution)/shard_map/all_gather | solution.py:871
  48.1 12.4 %collective-permute-done.23 = bf16[12,96,192]{2,1,0:T(8,128)(2,1)} collective-permute-done((bf16[12,96,192]{2,1,0:T(8,128)(2,1)}, bf16[12,96,192]{2,1,0:T(8,128)(2,1)}, u32[]{:S(2)}, u32[]{:S(2)}) %collective-permute-start.23) | collective-permute-done | bytes 442400 | tf_op jit(solution)/shard_map/ppermute | solution.py:65
  60.5 34.7 %collective-permute-done.24 = bf16[12,96,192]{2,1,0:T(8,128)(2,1)} collective-permute-done((bf16[12,96,192]{2,1,0:T(8,128)(2,1)}, bf16[12,96,192]{2,1,0:T(8,128)(2,1)}, u32[]{:S(2)}, u32[]{:S(2)}) %collective-permute-start.24) | collective-permute-done | bytes 442400 | tf_op jit(solution)/shard_map/ppermute | solution.py:65
  110.5 17.1 %collective-permute-done.29 = bf16[1,6,96,768]{3,2,1,0:T(8,128)(2,1)} collective-permute-done((bf16[1,6,96,768]{3,2,1,0:T(8,128)(2,1)}, bf16[1,6,96,768]{3,2,1,0:T(8,128)(2,1)}, u32[]{:S(2)}, u32[]{:S(2)}) %collective-permute-start.29) | collective-permute-done | bytes 884768 | tf_op jit(solution)/shard_map/ppermute | solution.py:60
  134.5 712.0 %while.29 = (pred[]{:T(512)}, s32[]{:T(128)}, f32[]{:T(128)}, f32[]{:T(128)}, f32[28,192,768]{2,1,0:T(8,128)}, /*index=5*/f32[8032,768]{1,0:T(8,128)}, f32[7,768...) while((pred[]{:T(512)}, s32[]{:T(128)}, f32[]{:T(128)}, ...), condition=%wide.region_66.68_spmd, body=%wide.region_5.67_spmd.sunk | while | flops 170049552384 | bytes 2179358464 | solution.py:1105
  158.8 7.1 gather_fusion.2
  178.4 18.7 %lookup.8 = bf16[1792,768]{1,0:T(8,128)(2,1)S(1)} custom-call(s32[3]{0:T(128)S(1)} %pad_add_fusion.4.refs_0_, s32[1792,1]{1,0:T(8,128)S(1)} %copy-done.17, bf16[768,8032]{1,0:T(8,128)(2,1)} %copy-done.2), custom_call_target="tpu_custom_call" | custom-call | flops 22108176384 | bytes 94371840 | tf_op jit(solution)/shard_map/while/body/lookup/pallas_call | solution.py:570
  204.4 9.7 collective-permute-start.5
  223.7 79.9 %conditional.2 = (bf16[1280,768]{1,0:T(8,128)(2,1)}) conditional(s32[]{:T(128)} %clamp.20, bf16[1280,768]{1,0:T(8,128)(2,1)} %slice.669, bf16[1280,768]{1,0:T(8,128)(2,1)} %slice.669, bf16[1280,768]{1,0:T(8,128)(2,1)} %slice.669, bf16[1280,768]{1,0:T(8,128)(2,1)} %slice.669), branch_computations={%region_23.25_spmd, %region_25.27_spmd, %region_27.29_spmd, %regio... | conditional | flops 983040 | bytes 16121906 | solution.py:1008
  226.4 74.4 %all-reduce.20.cloned.1.call-done = bf16[1024,768]{1,0:T(8,128)(2,1)} async-done(((bf16[1024,768]{1,0:T(8,128)(2,1)}), bf16[1024,768]{1,0:T(8,128)(2,1)}) %all-reduce.20.cloned.1.call-update) | async-done | bytes 1572880 | tf_op jit(solution)/shard_map/while/body/cond/branch_2_fun/psum | solution.py:1012
  316.8 9.6 place.26
  346.7 8.7 collective-permute-done.10
  382.5 30.3 %collective-permute-done.11 = bf16[2,8,96,768]{3,2,1,0:T(8,128)(2,1)S(1)} collective-permute-done((bf16[2,8,96,768]{3,2,1,0:T(8,128)(2,1)}, bf16[2,8,96,768]{3,2,1,0:T(8,128)(2,1)S(1)}, u32[]{:S(2)}, u32[]{:S(2)}) %collective-permute-start.11) | collective-permute-done | bytes 2359328 | tf_op jit(solution)/shard_map/while/body/ppermute | solution.py:60
  416.5 9.7 fusion.504
  426.3 12.8 %multiply_reduce_fusion.26 = (f32[1280]{0:T(1024)S(1)}, f32[1280,768]{1,0:T(8,128)S(1)}) fusion(f32[1280,768]{1,0:T(8,128)S(1)} %get-tuple-element.2046, bf16[3072,768]{1,0:T(8,128)(2,1)S(1)} %bitcast.376, f32[1280,3072]{1,0:T(8,128)} %fusion.504), kind=kOutput, calls=%fused_computation.65.clone.1 | convolution fusion | flops 6078135296 | bytes 28316672 | tf_op jit(solution)/shard_map/while/body/dot_general | solution.py:48
  483.3 9.2 fusion.512
  492.5 12.8 %copy.347 = f32[384,8032]{1,0:T(8,128)} copy(f32[384,8032]{0,1:T(8,128)} %get-tuple-element.2092) | data formatting | bytes 24674304 | tf_op jit(solution)/shard_map/while/body/dot_general | solution.py:48
  505.3 6.4 exponential_reduce_fusion.2
  511.8 6.4 select_reduce_fusion.35
  518.2 13.4 %all-gather.6 = f32[4,3,384]{2,1,0:T(4,128)S(1)} all-gather(f32[1,3,384]{2,1,0:T(4,128)S(1)} %maximum_bitcast_fusion.2), channel_id=2, replica_groups=mesh['cuts'=8,'fsdp'=4] {'fsdp'}, dimensions={0}, use_global_device_ids=true | all-gather | bytes 23040 | tf_op jit(solution)/shard_map/while/body/all_gather | solution.py:1059
  537.5 13.6 %fusion.515 = (bf16[384,768]{1,0:T(8,128)(2,1)S(1)}, f32[384,768]{1,0:T(8,128)}) fusion(bf16[384,8032]{1,0:T(8,128)(2,1)} %multiply_convert_fusion.39.logit_ref, bf16[768,8032]{1,0:T(8,128)(2,1)} %copy-done.2), kind=kOutput, calls=%fused_computation.550.clone.1 | convolution fusion | flops 4737761280 | bytes 20275200 | tf_op jit(solution)/shard_map/while/body/dot_general | solution.py:52
  557.9 9.6 collective-permute-done.14
  574.3 10.3 collective-permute-done.17
  587.3 8.7 fusion.518
  602.3 9.1 attend_back.24
  624.3 18.9 %fusion.521 = bf16[1280,3072]{1,0:T(8,128)(2,1)S(1)} fusion(f32[1280,3072]{1,0:T(8,128)} %fusion.504, bf16[1280,768]{1,0:T(8,128)(2,1)S(1)} %fusion.520, bf16[3072,768]{1,0:T(8,128)(2,1)} %get-tuple-element.2050), kind=kOutput, calls=%fused_computation.12.clone.1 | convolution fusion | flops 6118440960 | bytes 30277632 | tf_op jit(solution)/shard_map/while/body/dot_general | solution.py:52
  643.3 8.9 multiply_reduce_fusion.32
  652.3 9.5 attend_back.26
  668.2 6.6 constant_dynamic-slice_fusion.30
  674.8 11.1 %fusion.523 = f32[192,3072]{1,0:T(8,128)} fusion(bf16[1280,768]{1,0:T(8,128)(2,1)} %copy-done.80, s32[]{:T(128)} %get-tuple-element.2322, f32[1280,3072]{1,0:T(8,128)} %fusion.504), kind=kOutput, calls=%fused_computation.164.clone.1 | convolution fusion | flops 1545338880 | bytes 18743808 | tf_op jit(solution)/shard_map/while/body/dot_general | solution.py:56
  697.2 8.6 fusion.522
  708.8 17.1 %attend_back.25 = (bf16[1280,768]{1,0:T(8,128)(2,1)}, bf16[1280,1536]{1,0:T(8,128)(2,1)}, f32[5,6,128,256]{3,2,1,0:T(8,128)}) custom-call(s32[10]{0:T(128)} %copy-done.30, s32[10]{0:T(128)} %copy-done.29, bf16[1280,768]{1,0:T(8,128)(2,1)} %copy-done.49, bf16[1280,768]{1,0:T(8,128)(2,1)} %convolution_convert_fusion.27.refs_3_, bf16[1280,1536]{1,0:T(8,128)(2,1)} %copy-done.50, ...), custom_call_target="tpu_custom_call" | custom-call | flops 25165824000 | bytes 41943040 | tf_op jit(solution)/shard_map/while/body/attend_back/pallas_call | solution.py:491
  740.2 7.0 fusion.530
  792.1 18.3 %select_add_fusion.2 = f32[28,192,768]{2,1,0:T(8,128)} fusion(f32[28,192,768]{2,1,0:T(8,128)} %bitcast.348, f32[28,192,768]{2,1,0:T(8,128)} %get-tuple-element.2147, f32[28,192,768]{2,1,0:T(8,128)} %get-tuple-element.2234, pred[]{:T(512)S(6)} %eq.901), kind=kLoop, calls=%fused_computation.5.clone.1 | loop fusion | flops 8257536 | bytes 66060288 | tf_op jit(solution)/shard_map/while/body/add | solution.py:1096
  810.5 30.6 %vocab_grad.8 = f32[8032,768]{1,0:T(8,128)} custom-call(s32[4]{0:T(128)S(1)} %pad_add_fusion.5.blocks_ref, s32[1,1792]{1,0:T(1,128)S(1)} %broadcast_in_dim.760.id_ref, bf16[1792,768]{1,0:T(8,128)(2,1)S(1)} %fusion.532.grad_ref, bf16[384,8032]{1,0:T(8,128)(2,1)S(1)} %bitcast.354, bf16[384,768]{1,0:T(8,128)(2,1)S(1)} %copy-done.23, ...), custom_call_target="tpu_custom_call", output_to_operand_aliasing={{}: (6, {})} | custom-call | flops 26845642752 | bytes 104857600 | tf_op jit(solution)/shard_map/while/body/vocab_grad/pallas_call | solution.py:611
  846.5 7.9 convolution_bitcast_fusion.2
  854.5 10.8 convolution_bitcast_fusion.4
  867.3 47.4 %collective-permute-start.30 = (f32[128,768]{1,0:T(8,128)S(1)}, f32[128,768]{1,0:T(8,128)}, u32[]{:S(2)}, u32[]{:S(2)}) collective-permute-start(f32[128,768]{1,0:T(8,128)S(1)} %pad_dynamic-slice_fusion), channel_id=1, source_target_pairs={{0,4},{4,0},{8,12},{12,8},{16,20},{20,16},{24,28},{28,24},{1,5},{5... | collective-permute-start | bytes 1179656 | tf_op jit(solution)/shard_map/ppermute | solution.py:60
  918.1 7.5 collective-permute-done.31
  927.2 11.9 %collective-permute-start.32 = (f32[32,768]{1,0:T(8,128)S(1)}, f32[32,768]{1,0:T(8,128)S(1)}, u32[]{:S(2)}, u32[]{:S(2)}) collective-permute-start(f32[32,768]{1,0:T(8,128)S(1)} %constant_dynamic-slice_fusion.21), channel_id=1, source_target_pairs={{0,16},{4,20},{8,24},{12,28},{16,0},{20,4},{24,8},{28,12},{1,17},{... | collective-permute-start | bytes 294920 | tf_op jit(solution)/shard_map/ppermute | solution.py:60
  942.7 14.9 %all-gather.2 = f32[128,768]{1,0:T(8,128)S(1)} all-gather(f32[32,768]{1,0:T(8,128)S(1)} %dynamic-slice_add_fusion.1), channel_id=4, replica_groups=mesh['cuts'=8,'fsdp'=4] {'fsdp'}, dimensions={0}, use_global_device_ids=true | all-gather | bytes 491520 | tf_op jit(solution)/shard_map/all_gather | solution.py:105
  985.8 12.4 %fusion.202 = bf16[8,28,192]{2,0,1:T(8,128)(2,1)S(1)} fusion(f32[28,192,768]{2,1,0:T(8,128)} %get-tuple-element.2536, f32[8,28,768]{2,1,0:T(8,128)} %bitcast.361), kind=kOutput, calls=%fused_computation.481 | convolution fusion | flops 198223872 | bytes 17289216 | tf_op jit(solution)/shard_map/kji,rki->rkj/dot_general | solution.py:1144
  998.5 13.7 %convolution_convert_fusion.9 = bf16[8,8032]{1,0:T(8,128)(2,1)S(1)} fusion(f32[8032,768]{1,0:T(8,128)} %get-tuple-element.2537, f32[8,1,768]{2,1,0:T(1,128)S(1)} %slice.528), kind=kOutput, calls=%fused_computation.464 | convolution fusion | flops 296155904 | bytes 24827392 | tf_op jit(solution)/shard_map/vd,rd->rv/dot_general | solution.py:1145
  1028.2 22.9 %subtract_bitcast_fusion = f32[1,8032,768]{2,1,0:T(8,128)} fusion(f32[8032,768]{1,0:T(8,128)} %get-tuple-element.2537, f32[8,13408]{1,0:T(8,128)S(1)} %convert_add_fusion.2, f32[8,1,768]{2,1,0:T(1,128)S(1)} %slice.528), kind=kOutput, calls=%fused_computation.458 | convolution fusion | flops 302260224 | bytes 49631232 | tf_op jit(solution)/shard_map/rv,rd->vd/dot_general | solution.py:1157
  1055.2 13.9 %subtract_bitcast_fusion.1 = f32[1,768,28,192]{1,3,2,0:T(8,128)} fusion(f32[28,192,768]{2,1,0:T(8,128)} %get-tuple-element.2536, f32[8,28,768]{2,1,0:T(8,128)S(1)} %bitcast.364, f32[8,28,192]{2,1,0:T(8,128)S(1)} %reshape.804), kind=kOutput, calls=%fused_computation.459 | convolution fusion | flops 202309632 | bytes 33890304 | tf_op jit(solution)/shard_map/rki,rkj->kji/dot_general | solution.py:1156
  1069.0 9.1 psum.49
  1081.1 6.7 multiply_subtract_fusion.1
  1095.5 6.7 multiply_subtract_fusion
  (754 shorter events, 392.7 us)
Async XLA Ops:
  7.2 847.3 %copy-start = (f32[8032,8]{0,1:T(8,128)S(1)}, f32[8032,8]{0,1:T(8,128)}, u32[]{:S(2)}) copy-start(f32[8032,8]{0,1:T(8,128)} %param.41) | copy-start | bytes 771076
  9.5 26.1 %collective-permute-start.19 = (bf16[1,1,48,8032]{3,2,1,0:T(8,128)(2,1)S(1)}, bf16[1,1,48,8032]{3,2,1,0:T(8,128)(2,1)}, u32[]{:S(2)}, u32[]{:S(2)}) collective-permute-start(bf16[1,1,48,8032]{3,2,1,0:T(8,128)(2,1)S(1)} %get-tuple-element.1566), channel_id=1, source_target_pairs={{0,8},{4,12},{8,0},{12,4},{16,24},{20,28},{24,16},{28,20},{1,9},{5... | collective-permute-start | bytes 2313224 | tf_op jit(solution)/shard_map/ppermute | solution.py:60
  12.5 24.8 %collective-permute-start.20 = (bf16[1,1,48,8032]{3,2,1,0:T(8,128)(2,1)S(1)}, bf16[1,1,48,8032]{3,2,1,0:T(8,128)(2,1)}, u32[]{:S(2)}, u32[]{:S(2)}) collective-permute-start(bf16[1,1,48,8032]{3,2,1,0:T(8,128)(2,1)S(1)} %get-tuple-element.1565), channel_id=1, source_target_pairs={{0,16},{4,20},{8,24},{12,28},{16,0},{20,4},{24,8},{28,12},{1,17},{... | collective-permute-start | bytes 2313224 | tf_op jit(solution)/shard_map/ppermute | solution.py:60
  40.3 57.5 %collective-permute-start.21 = (bf16[2,1,48,8032]{3,2,1,0:T(8,128)(2,1)S(1)}, bf16[2,1,48,8032]{3,2,1,0:T(8,128)(2,1)}, u32[]{:S(2)}, u32[]{:S(2)}) collective-permute-start(bf16[2,1,48,8032]{3,2,1,0:T(8,128)(2,1)S(1)} %pad_maximum_fusion.13), channel_id=1, source_target_pairs={{0,16},{4,20},{8,24},{12,28},{16,0},{20,4},{24,8},{28,12},{1,17},{... | collective-permute-start | bytes 4626440 | tf_op jit(solution)/shard_map/ppermute | solution.py:60
  43.0 17.5 %collective-permute-start.23 = (bf16[12,96,192]{2,1,0:T(8,128)(2,1)}, bf16[12,96,192]{2,1,0:T(8,128)(2,1)}, u32[]{:S(2)}, u32[]{:S(2)}) collective-permute-start(bf16[12,96,192]{2,1,0:T(8,128)(2,1)} %slice.491), channel_id=1, source_target_pairs={{0,3},{1,0},{2,1},{3,2},{4,7},{5,4},{6,5},{7,6},{8,11},{9,8},{10,9... | collective-permute-start | bytes 1327112 | tf_op jit(solution)/shard_map/ppermute | solution.py:65
  46.4 48.8 %collective-permute-start.24 = (bf16[12,96,192]{2,1,0:T(8,128)(2,1)}, bf16[12,96,192]{2,1,0:T(8,128)(2,1)}, u32[]{:S(2)}, u32[]{:S(2)}) collective-permute-start(bf16[12,96,192]{2,1,0:T(8,128)(2,1)} %slice.491), channel_id=1, source_target_pairs={{0,2},{1,3},{2,0},{3,1},{4,6},{5,7},{6,4},{7,5},{8,10},{9,11},{10,... | collective-permute-start | bytes 1327112 | tf_op jit(solution)/shard_map/ppermute | solution.py:65
  46.4 48.8 %collective-permute-start.25 = (bf16[12,96,192]{2,1,0:T(8,128)(2,1)}, bf16[12,96,192]{2,1,0:T(8,128)(2,1)}, u32[]{:S(2)}, u32[]{:S(2)}) collective-permute-start(bf16[12,96,192]{2,1,0:T(8,128)(2,1)} %slice.491), channel_id=1, source_target_pairs={{0,1},{1,2},{2,3},{3,0},{4,5},{5,6},{6,7},{7,4},{8,9},{9,10},{10,1... | collective-permute-start | bytes 1327112 | tf_op jit(solution)/shard_map/ppermute | solution.py:65
  47.0 53.1 %collective-permute-start.22 = (bf16[2,1,48,8032]{3,2,1,0:T(8,128)(2,1)}, bf16[2,1,48,8032]{3,2,1,0:T(8,128)(2,1)}, u32[]{:S(2)}, u32[]{:S(2)}) collective-permute-start(bf16[2,1,48,8032]{3,2,1,0:T(8,128)(2,1)} %pad_maximum_fusion.14), channel_id=1, source_target_pairs={{0,8},{4,12},{8,0},{12,4},{16,24},{20,28},{24,16},{28,20},{1,9},{5... | collective-permute-start | bytes 4626440 | tf_op jit(solution)/shard_map/ppermute | solution.py:60
  103.9 29.4 %collective-permute-start.26 = (bf16[4,1,48,8032]{3,2,1,0:T(8,128)(2,1)S(1)}, bf16[4,1,48,8032]{3,2,1,0:T(8,128)(2,1)}, u32[]{:S(2)}, u32[]{:S(2)}) collective-permute-start(bf16[4,1,48,8032]{3,2,1,0:T(8,128)(2,1)S(1)} %pad_maximum_fusion.8), channel_id=1, source_target_pairs={{0,4},{4,0},{8,12},{12,8},{16,20},{20,16},{24,28},{28,24},{1,5},{5... | collective-permute-start | bytes 9252872 | tf_op jit(solution)/shard_map/ppermute | solution.py:60
  103.9 29.4 %collective-permute-start.27 = (bf16[4,1,48,8032]{3,2,1,0:T(8,128)(2,1)}, bf16[4,1,48,8032]{3,2,1,0:T(8,128)(2,1)}, u32[]{:S(2)}, u32[]{:S(2)}) collective-permute-start(bf16[4,1,48,8032]{3,2,1,0:T(8,128)(2,1)} %pad_maximum_fusion.9), channel_id=1, source_target_pairs={{0,4},{4,0},{8,12},{12,8},{16,20},{20,16},{24,28},{28,24},{1,5},{5... | collective-permute-start | bytes 9252872 | tf_op jit(solution)/shard_map/ppermute | solution.py:60
  105.8 21.9 %collective-permute-start.29 = (bf16[1,6,96,768]{3,2,1,0:T(8,128)(2,1)}, bf16[1,6,96,768]{3,2,1,0:T(8,128)(2,1)}, u32[]{:S(2)}, u32[]{:S(2)}) collective-permute-start(bf16[1,6,96,768]{3,2,1,0:T(8,128)(2,1)} %get-tuple-element.1563), channel_id=1, source_target_pairs={{0,16},{4,20},{8,24},{12,28},{16,0},{20,4},{24,8},{28,12},{1,17},{... | collective-permute-start | bytes 2654216 | tf_op jit(solution)/shard_map/ppermute | solution.py:60
  106.5 24.0 %collective-permute-start.28 = (bf16[1,6,96,768]{3,2,1,0:T(8,128)(2,1)}, bf16[1,6,96,768]{3,2,1,0:T(8,128)(2,1)}, u32[]{:S(2)}, u32[]{:S(2)}) collective-permute-start(bf16[1,6,96,768]{3,2,1,0:T(8,128)(2,1)} %get-tuple-element.1564), channel_id=1, source_target_pairs={{0,8},{4,12},{8,0},{12,4},{16,24},{20,28},{24,16},{28,20},{1,9},{5... | collective-permute-start | bytes 2654216 | tf_op jit(solution)/shard_map/ppermute | solution.py:60
  134.8 169.1 %collective-permute-start.2 = (bf16[16,96,192]{2,1,0:T(8,128)(2,1)}, bf16[16,96,192]{2,1,0:T(8,128)(2,1)}, u32[]{:S(2)}, u32[]{:S(2)}) collective-permute-start(bf16[16,96,192]{2,1,0:T(8,128)(2,1)} %get-tuple-element.2024), channel_id=1, source_target_pairs={{0,1},{1,2},{2,3},{3,0},{4,5},{5,6},{6,7},{7,4},{8,9},{9,10},{10,1... | collective-permute-start | bytes 1769480 | tf_op jit(solution)/shard_map/while/body/ppermute | solution.py:65
  135.3 168.6 %collective-permute-start.3 = (bf16[16,96,192]{2,1,0:T(8,128)(2,1)}, bf16[16,96,192]{2,1,0:T(8,128)(2,1)}, u32[]{:S(2)}, u32[]{:S(2)}) collective-permute-start(bf16[16,96,192]{2,1,0:T(8,128)(2,1)} %get-tuple-element.2024), channel_id=1, source_target_pairs={{0,2},{1,3},{2,0},{3,1},{4,6},{5,7},{6,4},{7,5},{8,10},{9,11},{10,... | collective-permute-start | bytes 1769480 | tf_op jit(solution)/shard_map/while/body/ppermute | solution.py:65
  137.3 166.6 %collective-permute-start.4 = (bf16[16,96,192]{2,1,0:T(8,128)(2,1)}, bf16[16,96,192]{2,1,0:T(8,128)(2,1)}, u32[]{:S(2)}, u32[]{:S(2)}) collective-permute-start(bf16[16,96,192]{2,1,0:T(8,128)(2,1)} %get-tuple-element.2024), channel_id=1, source_target_pairs={{0,3},{1,0},{2,1},{3,2},{4,7},{5,4},{6,5},{7,6},{8,11},{9,8},{10,9... | collective-permute-start | bytes 1769480 | tf_op jit(solution)/shard_map/while/body/ppermute | solution.py:65
  140.2 56.9 %collective-permute-start = (bf16[2,6,96,768]{3,2,1,0:T(8,128)(2,1)}, bf16[2,6,96,768]{3,2,1,0:T(8,128)(2,1)}, u32[]{:S(2)}, u32[]{:S(2)}) collective-permute-start(bf16[2,6,96,768]{3,2,1,0:T(8,128)(2,1)} %get-tuple-element.2006), channel_id=1, source_target_pairs={{0,16},{4,20},{8,24},{12,28},{16,0},{20,4},{24,8},{28,12},{1,17},{... | collective-permute-start | bytes 5308424 | tf_op jit(solution)/shard_map/while/body/ppermute | solution.py:60
  141.1 59.7 %collective-permute-start.1 = (bf16[2,6,96,768]{3,2,1,0:T(8,128)(2,1)}, bf16[2,6,96,768]{3,2,1,0:T(8,128)(2,1)}, u32[]{:S(2)}, u32[]{:S(2)}) collective-permute-start(bf16[2,6,96,768]{3,2,1,0:T(8,128)(2,1)} %get-tuple-element.2007), channel_id=1, source_target_pairs={{0,8},{4,12},{8,0},{12,4},{16,24},{20,28},{24,16},{28,20},{1,9},{5... | collective-permute-start | bytes 5308424 | tf_op jit(solution)/shard_map/while/body/ppermute | solution.py:60
  204.4 112.5 %collective-permute-start.5 = (bf16[4,6,96,768]{3,2,1,0:T(8,128)(2,1)}, bf16[4,6,96,768]{3,2,1,0:T(8,128)(2,1)}, u32[]{:S(2)}, u32[]{:S(2)}) collective-permute-start(bf16[4,6,96,768]{3,2,1,0:T(8,128)(2,1)} %pad_maximum_fusion.24.refs_1_), channel_id=1, source_target_pairs={{0,4},{4,0},{8,12},{12,8},{16,20},{20,16},{24,28},{28,24},{1,5},{5... | collective-permute-start | bytes 10616840 | tf_op jit(solution)/shard_map/while/body/ppermute | solution.py:60
  214.1 102.7 %collective-permute-start.6 = (bf16[4,6,96,768]{3,2,1,0:T(8,128)(2,1)}, bf16[4,6,96,768]{3,2,1,0:T(8,128)(2,1)}, u32[]{:S(2)}, u32[]{:S(2)}) collective-permute-start(bf16[4,6,96,768]{3,2,1,0:T(8,128)(2,1)} %pad_maximum_fusion.25.refs_3_), channel_id=1, source_target_pairs={{0,4},{4,0},{8,12},{12,8},{16,20},{20,16},{24,28},{28,24},{1,5},{5... | collective-permute-start | bytes 10616840 | tf_op jit(solution)/shard_map/while/body/ppermute | solution.py:60
  216.1 234.3 %copy-start.27 = (s32[3]{0:T(128)}, s32[3]{0:T(128)S(1)}, u32[]{:S(2)}) copy-start(s32[3]{0:T(128)S(1)} %get-tuple-element.2068.refs_1_) | copy-start | bytes 40 | tf_op jit(solution)/shard_map/while
  216.1 234.3 %copy-start.28 = (s32[3]{0:T(128)}, s32[3]{0:T(128)S(1)}, u32[]{:S(2)}) copy-start(s32[3]{0:T(128)S(1)} %get-tuple-element.2067.refs_0_) | copy-start | bytes 40 | tf_op jit(solution)/shard_map/while
  216.8 244.9 %copy-start.31 = (s32[3]{0:T(128)}, s32[3]{0:T(128)S(1)}, u32[]{:S(2)}) copy-start(s32[3]{0:T(128)S(1)} %get-tuple-element.2061.refs_1_) | copy-start | bytes 40 | tf_op jit(solution)/shard_map/while
  216.8 244.9 %copy-start.32 = (s32[3]{0:T(128)}, s32[3]{0:T(128)S(1)}, u32[]{:S(2)}) copy-start(s32[3]{0:T(128)S(1)} %get-tuple-element.2060.refs_0_) | copy-start | bytes 40 | tf_op jit(solution)/shard_map/while
  216.9 244.8 %copy-start.25 = (s32[1,384]{1,0:T(1,128)}, s32[1,384]{1,0:T(1,128)S(1)}, u32[]{:S(2)}) copy-start(s32[1,384]{1,0:T(1,128)S(1)} %broadcast_in_dim.758.refs_5_.refs_7_) | copy-start | bytes 4612 | tf_op jit(solution)/shard_map/while
  217.0 233.4 %copy-start.18 = (s32[384,1]{1,0:T(8,128)}, s32[384,1]{1,0:T(8,128)S(1)}, u32[]{:S(2)}) copy-start(s32[384,1]{1,0:T(8,128)S(1)} %broadcast_in_dim.759.refs_6_.refs_8_) | copy-start | bytes 4612 | tf_op jit(solution)/shard_map/while
  223.7 77.1 %all-reduce.20.cloned.1.call-start = ((), (), s32[]{:S(2)}) async-start(), calls=%async_computation.2 | async-start | bytes 3145728 | tf_op jit(solution)/shard_map/while/body/cond/branch_2_fun/psum | solution.py:1012
  303.6 139.1 %all-reduce.24.cloned.1.call-start = ((), (), s32[]{:S(2)}) async-start(), calls=%async_computation.4 | async-start | bytes 1179648 | tf_op jit(solution)/shard_map/while/body/psum | solution.py:1037
  328.6 26.8 %collective-permute-start.10 = (bf16[1,8,96,768]{3,2,1,0:T(8,128)(2,1)}, bf16[1,8,96,768]{3,2,1,0:T(8,128)(2,1)}, u32[]{:S(2)}, u32[]{:S(2)}) collective-permute-start(bf16[1,8,96,768]{3,2,1,0:T(8,128)(2,1)} %get-tuple-element.2063), channel_id=1, source_target_pairs={{0,16},{4,20},{8,24},{12,28},{16,0},{20,4},{24,8},{28,12},{1,17},{... | collective-permute-start | bytes 3538952 | tf_op jit(solution)/shard_map/while/body/ppermute | solution.py:60
  335.7 29.1 %collective-permute-start.7 = (bf16[1,8,96,768]{3,2,1,0:T(8,128)(2,1)}, bf16[1,8,96,768]{3,2,1,0:T(8,128)(2,1)S(1)}, u32[]{:S(2)}, u32[]{:S(2)}) collective-permute-start(bf16[1,8,96,768]{3,2,1,0:T(8,128)(2,1)} %get-tuple-element.2062), channel_id=1, source_target_pairs={{0,8},{4,12},{8,0},{12,4},{16,24},{20,28},{24,16},{28,20},{1,9},{5... | collective-permute-start | bytes 3538952 | tf_op jit(solution)/shard_map/while/body/ppermute | solution.py:60
  358.7 54.1 %collective-permute-start.11 = (bf16[2,8,96,768]{3,2,1,0:T(8,128)(2,1)}, bf16[2,8,96,768]{3,2,1,0:T(8,128)(2,1)S(1)}, u32[]{:S(2)}, u32[]{:S(2)}) collective-permute-start(bf16[2,8,96,768]{3,2,1,0:T(8,128)(2,1)} %pad_maximum_fusion.28), channel_id=1, source_target_pairs={{0,8},{4,12},{8,0},{12,4},{16,24},{20,28},{24,16},{28,20},{1,9},{5... | collective-permute-start | bytes 7077896 | tf_op jit(solution)/shard_map/while/body/ppermute | solution.py:60
  365.1 49.3 %collective-permute-start.8 = (bf16[2,8,96,768]{3,2,1,0:T(8,128)(2,1)S(1)}, bf16[2,8,96,768]{3,2,1,0:T(8,128)(2,1)S(1)}, u32[]{:S(2)}, u32[]{:S(2)}) collective-permute-start(bf16[2,8,96,768]{3,2,1,0:T(8,128)(2,1)S(1)} %pad_maximum_fusion.27), channel_id=1, source_target_pairs={{0,16},{4,20},{8,24},{12,28},{16,0},{20,4},{24,8},{28,12},{1,17},{... | collective-permute-start | bytes 7077896 | tf_op jit(solution)/shard_map/while/body/ppermute | solution.py:60
  414.4 29.6 %collective-permute-start.12 = (bf16[4,8,96,768]{3,2,1,0:T(8,128)(2,1)}, bf16[4,8,96,768]{3,2,1,0:T(8,128)(2,1)}, u32[]{:S(2)}, u32[]{:S(2)}) collective-permute-start(bf16[4,8,96,768]{3,2,1,0:T(8,128)(2,1)} %constant_dynamic-update-slice_fusion.17.refs_3_), channel_id=1, source_target_pairs={{0,4},{4,0},{8,12},{12,8},{16,20},{20,16},{24,28},{28,24},{1,5},{5... | collective-permute-start | bytes 14155784 | tf_op jit(solution)/shard_map/while/body/ppermute | solution.py:60
  416.0 28.0 %collective-permute-start.9 = (bf16[4,8,96,768]{3,2,1,0:T(8,128)(2,1)}, bf16[4,8,96,768]{3,2,1,0:T(8,128)(2,1)}, u32[]{:S(2)}, u32[]{:S(2)}) collective-permute-start(bf16[4,8,96,768]{3,2,1,0:T(8,128)(2,1)} %constant_dynamic-update-slice_fusion.14.refs_1_), channel_id=1, source_target_pairs={{0,4},{4,0},{8,12},{12,8},{16,20},{20,16},{24,28},{28,24},{1,5},{5... | collective-permute-start | bytes 14155784 | tf_op jit(solution)/shard_map/while/body/ppermute | solution.py:60
  551.1 6.8 collective-permute-start.13
  553.7 13.8 %collective-permute-start.14 = (bf16[96,768]{1,0:T(8,128)(2,1)S(1)}, bf16[96,768]{1,0:T(8,128)(2,1)S(1)}, u32[]{:S(2)}, u32[]{:S(2)}) collective-permute-start(bf16[96,768]{1,0:T(8,128)(2,1)S(1)} %get-tuple-element.2103), channel_id=1, source_target_pairs={{0,2},{1,3},{2,0},{3,1},{4,6},{5,7},{6,4},{7,5},{8,10},{9,11},{10,... | collective-permute-start | bytes 442376 | tf_op jit(solution)/shard_map/while/body/ppermute | solution.py:65
  553.7 13.8 %collective-permute-start.15 = (bf16[96,768]{1,0:T(8,128)(2,1)S(1)}, bf16[96,768]{1,0:T(8,128)(2,1)S(1)}, u32[]{:S(2)}, u32[]{:S(2)}) collective-permute-start(bf16[96,768]{1,0:T(8,128)(2,1)S(1)} %get-tuple-element.2104), channel_id=1, source_target_pairs={{0,1},{1,2},{2,3},{3,0},{4,5},{5,6},{6,7},{7,4},{8,9},{9,10},{10,1... | collective-permute-start | bytes 442376 | tf_op jit(solution)/shard_map/while/body/ppermute | solution.py:65
  568.5 5.7 collective-permute-start.16
  568.7 15.9 %collective-permute-start.17 = (bf16[96,768]{1,0:T(8,128)(2,1)S(1)}, bf16[96,768]{1,0:T(8,128)(2,1)S(1)}, u32[]{:S(2)}, u32[]{:S(2)}) collective-permute-start(bf16[96,768]{1,0:T(8,128)(2,1)S(1)} %add_convert_fusion.4), channel_id=1, source_target_pairs={{0,2},{1,3},{2,0},{3,1},{4,6},{5,7},{6,4},{7,5},{8,10},{9,11},{10,... | collective-permute-start | bytes 442376 | tf_op jit(solution)/shard_map/while/body/ppermute | solution.py:65
  571.0 13.5 %collective-permute-start.18 = (bf16[96,768]{1,0:T(8,128)(2,1)S(1)}, bf16[96,768]{1,0:T(8,128)(2,1)S(1)}, u32[]{:S(2)}, u32[]{:S(2)}) collective-permute-start(bf16[96,768]{1,0:T(8,128)(2,1)S(1)} %add_convert_fusion.4), channel_id=1, source_target_pairs={{0,1},{1,2},{2,3},{3,0},{4,5},{5,6},{6,7},{7,4},{8,9},{9,10},{10,1... | collective-permute-start | bytes 442376 | tf_op jit(solution)/shard_map/while/body/ppermute | solution.py:65
  867.3 48.9 %collective-permute-start.30 = (f32[128,768]{1,0:T(8,128)S(1)}, f32[128,768]{1,0:T(8,128)}, u32[]{:S(2)}, u32[]{:S(2)}) collective-permute-start(f32[128,768]{1,0:T(8,128)S(1)} %pad_dynamic-slice_fusion), channel_id=1, source_target_pairs={{0,4},{4,0},{8,12},{12,8},{16,20},{20,16},{24,28},{28,24},{1,5},{5... | collective-permute-start | bytes 1179656 | tf_op jit(solution)/shard_map/ppermute | solution.py:60
  918.0 7.5 collective-permute-start.31
  927.2 14.6 %collective-permute-start.32 = (f32[32,768]{1,0:T(8,128)S(1)}, f32[32,768]{1,0:T(8,128)S(1)}, u32[]{:S(2)}, u32[]{:S(2)}) collective-permute-start(f32[32,768]{1,0:T(8,128)S(1)} %constant_dynamic-slice_fusion.21), channel_id=1, source_target_pairs={{0,16},{4,20},{8,24},{12,28},{16,0},{20,4},{24,8},{28,12},{1,17},{... | collective-permute-start | bytes 294920 | tf_op jit(solution)/shard_map/ppermute | solution.py:60
  958.3 4.8 collective-permute-start.33
  964.1 5.8 collective-permute-start.34
  971.2 6.2 collective-permute-start.35
  1012.2 2.0 collective-permute-start.36
  1014.3 7.3 collective-permute-start.37
  1021.7 6.4 collective-permute-start.38
  (190 other events, 3464.0 us)
Sparse Core Ops, SparseCore 0:
  227.5 73.3 all-reduce.19
  309.8 38.3 all-reduce.23

commit v3 on v2

--- a/solution.py
+++ b/solution.py
@@ -639,6 +639,139 @@
     )
 
 
+def logit_places(step, rows_in, width):
+    return step * width + lax.broadcasted_iota(jnp.int32, (TILE, width), 1)
+
+
+def logit_kernel(rows_in, tiles_ref, row_ref, vocab_ref, id_ref, logit_ref, stat_ref, top_ref, sum_ref, hit_ref):
+    step = pl.program_id(0)
+    width = vocab_ref.shape[1]
+
+    @pl.when(step == 0)
+    def _():
+        top_ref[...] = jnp.full_like(top_ref, -1e30)
+        sum_ref[...] = jnp.zeros_like(sum_ref)
+        hit_ref[...] = jnp.zeros_like(hit_ref)
+
+    places = logit_places(step, rows_in, width)
+
+    def one(index, carry):
+        rows = pl.ds(pl.multiple_of(index * TILE, TILE), TILE)
+        logits = dot(row_ref[rows, :], vocab_ref[...])
+        logit_ref[rows, :] = logits
+        inside = places < rows_in
+        hits = jnp.where(inside & (places == id_ref[rows, :]), logits, 0.0)
+        logits = jnp.where(inside, logits, -1e30)
+        parts = [slice(begin, begin + TILE) for begin in range(0, width, TILE)]
+        before = top_ref[rows, :]
+        top = before
+        for part in parts:
+            top = jnp.maximum(top, logits[:, part])
+        total = sum_ref[rows, :] * jnp.exp(before - top)
+        hit = hit_ref[rows, :]
+        for part in parts:
+            total = total + jnp.exp(logits[:, part] - top)
+            hit = hit + hits[:, part]
+        top_ref[rows, :] = top
+        sum_ref[rows, :] = total
+        hit_ref[rows, :] = hit
+        return carry
+
+    lax.fori_loop(0, tiles_ref[0], one, 0)
+
+    @pl.when(step == pl.num_programs(0) - 1)
+    def _():
+        top = jnp.max(top_ref[...], axis=1, keepdims=True)
+        total = jnp.sum(sum_ref[...] * jnp.exp(top_ref[...] - top), axis=1, keepdims=True)
+        hit = jnp.sum(hit_ref[...], axis=1, keepdims=True)
+        lane = lax.broadcasted_iota(jnp.int32, stat_ref.shape, 1)
+        seen = jnp.where(total > 0.0, total, 1.0)
+        stat_ref[...] = jnp.where(lane == 0, top, jnp.where(lane == 1, seen, hit))
+
+
+def logit_stats(final_rows, vocab, ids, tiles):
+    count, rows_in, width = final_rows.shape[0], vocab.shape[1], 4 * TILE
+    return pl.pallas_call(
+        lambda *refs: logit_kernel(rows_in, *refs),
+        grid_spec=pltpu.PrefetchScalarGridSpec(
+            num_scalar_prefetch=1,
+            grid=(pl.cdiv(rows_in, width),),
+            in_specs=[
+                whole_block((count, MODEL_WIDTH)),
+                pl.BlockSpec((MODEL_WIDTH, width), lambda i, *_: (0, i)),
+                whole_block((count, 1)),
+            ],
+            out_specs=[
+                pl.BlockSpec((count, width), lambda i, *_: (0, i)),
+                whole_block((count, TILE)),
+            ],
+            scratch_shapes=[pltpu.VMEM((count, TILE), jnp.float32)] * 3,
+        ),
+        out_shape=[
+            jax.ShapeDtypeStruct((count, rows_in), jnp.float32),
+            jax.ShapeDtypeStruct((count, TILE), jnp.float32),
+        ],
+        compiler_params=pltpu.CompilerParams(vmem_limit_bytes=40 << 20),
+        cost_estimate=cost(2 * count * rows_in * MODEL_WIDTH, 40 << 20, count * rows_in),
+        name="logits",
+    )(tiles, final_rows, vocab, ids)
+
+
+def logit_grad_kernel(
+    rows_in, tiles_ref, logit_ref, vocab_ref, id_ref, level_ref, weight_ref, grad_ref, row_ref
+):
+    step = pl.program_id(0)
+    width = vocab_ref.shape[1]
+
+    @pl.when(step == 0)
+    def _():
+        row_ref[...] = jnp.zeros_like(row_ref)
+
+    grad_ref[...] = jnp.zeros_like(grad_ref)
+    places = logit_places(step, rows_in, width)
+    inside = step * width + lax.broadcasted_iota(jnp.int32, (1, width), 1) < rows_in
+    table = jnp.where(inside, vocab_ref[...], jnp.zeros_like(vocab_ref[...]))
+
+    def one(index, carry):
+        rows = pl.ds(pl.multiple_of(index * TILE, TILE), TILE)
+        hit = (places == id_ref[rows, :]).astype(jnp.float32)
+        grads = (jnp.exp(logit_ref[rows, :] - level_ref[rows, :]) - hit) * weight_ref[rows, :]
+        grads = jnp.where(places < rows_in, grads, 0.0).astype(jnp.bfloat16)
+        grad_ref[rows, :] = grads
+        row_ref[rows, :] = row_ref[rows, :] + dot_nt(grads, table)
+        return carry
+
+    lax.fori_loop(0, tiles_ref[0], one, 0)
+
+
+def logit_grads(logits, vocab, ids, tiles, levels, weights):
+    count, rows_in = logits.shape
+    width = 4 * TILE
+    block = pl.BlockSpec((count, width), lambda i, *_: (0, i))
+    return pl.pallas_call(
+        lambda *refs: logit_grad_kernel(rows_in, *refs),
+        grid_spec=pltpu.PrefetchScalarGridSpec(
+            num_scalar_prefetch=1,
+            grid=(pl.cdiv(rows_in, width),),
+            in_specs=[
+                block,
+                pl.BlockSpec((MODEL_WIDTH, width), lambda i, *_: (0, i)),
+                whole_block((count, 1)),
+                whole_block((count, 1)),
+                whole_block((count, 1)),
+            ],
+            out_specs=[block, whole_block((count, MODEL_WIDTH))],
+        ),
+        out_shape=[
+            jax.ShapeDtypeStruct((count, rows_in), jnp.bfloat16),
+            jax.ShapeDtypeStruct((count, MODEL_WIDTH), jnp.float32),
+        ],
+        compiler_params=pltpu.CompilerParams(vmem_limit_bytes=40 << 20),
+        cost_estimate=cost(2 * count * rows_in * MODEL_WIDTH, 40 << 20, count * rows_in),
+        name="logit_grads",
+    )(tiles, logits, vocab, ids, levels[:, None], weights[:, None])
+
+
 def packing(lengths, room):
     ends = jnp.cumsum(lengths)
     starts = ends - lengths
@@ -679,7 +812,7 @@
 
 
 def packed_gradients(
-    source_stream, target_stream, gain_rows, position_bias, weights, layout, head, column_start, column_width
+    source_stream, target_stream, gain_rows, biases, weights, layout, head, column_start, column_width
 ):
     enc_attention, enc_feed, dec_self, dec_cross, dec_feed = weights
     (
@@ -691,8 +824,7 @@
         target_row,
         target_column,
     ) = layout
-    bias_source = bias_tiles(False, position_bias[0])
-    bias_target = bias_tiles(True, position_bias[1])
+    bias_source, bias_target = biases
 
     def shard(grad, which=0):
         return lax.dynamic_slice_in_dim(grad, which * MODEL_WIDTH + column_start, column_width, 1)
@@ -896,17 +1028,18 @@
     stored, needs = lax.optimization_barrier((stored, needs))
     first_columns = jnp.concatenate(gather_fsdp(stored[:12], fsdp_rank), axis=2)
     errors = jnp.transpose(error_blocks[0], (1, 2, 0))
-    vocab_shares, first_columns = spread_tied(vocab_shares, first_columns)
+    biases = (bias_tiles(False, position_bias[0]), bias_tiles(True, position_bias[1]))
+    vocab_shares, first_columns, biases = spread_tied(vocab_shares, first_columns, biases)
     first_shares = spread_begin(first_columns)
     first_shares = spread_step(first_shares, 0) if steps else first_shares
     vocab_pieces = spread_end(vocab_shares)
     piece_arrays = [[array for _, array in held] for _, held in vocab_pieces]
     first_arrays = [array for _, array in first_shares]
-    given = (group, needs, piece_arrays, first_arrays, stored[12:], errors)
+    given = (group, needs, piece_arrays, first_arrays, stored[12:], errors, biases)
 
     def one_round(state):
         _, turn, _, _, left_blocks, left_embed, gains_sum, table_sum, loss_sum = state
-        turn, group, needs, piece_arrays, first_arrays, stored_rest, errors = (
+        turn, group, needs, piece_arrays, first_arrays, stored_rest, errors, biases = (
             lax.optimization_barrier((turn, *given))
         )
         group_source = group[:, :source_len]
@@ -981,7 +1114,6 @@
         packed_input = jnp.take(group_input.reshape(-1), target_from)
         packed_ids = jnp.concatenate([packed_source, packed_input])
         packed_real = jnp.concatenate([source_real, target_real])
-        vocab_places = jnp.arange(vocab_rows, dtype=jnp.int32)
         local_ids = jnp.where(packed_real, packed_ids - vocab_start, -1)
         source_total, target_total = jnp.sum(source_taken), jnp.sum(target_taken)
         chunk = 2 * TILE
@@ -1015,8 +1147,8 @@
             ],
             rows[:room_source],
         )
-        source_rows, target_rows, table, rest_parts = lax.optimization_barrier(
-            (source_rows, rows[room_source : room_source + room_target], position_bias, rest_parts)
+        source_rows, target_rows, rest_parts = lax.optimization_barrier(
+            (source_rows, rows[room_source : room_source + room_target], rest_parts)
         )
         rest_columns = jnp.concatenate(in_order(rest_parts, fsdp_rank), axis=2)
         rest_shares, first_placed = spread_tied(spread_begin(rest_columns), first_placed)
@@ -1049,24 +1181,21 @@
 
         token_mask = target_real.astype(jnp.float32)
         token_weight = token_mask * (slice_weight / total_count)
-        target_hit = vocab_places[None, :] == (packed_target - vocab_start)[:, None]
+        target_ids = (packed_target - vocab_start)[:, None]
+        target_tiles = ((target_total + TILE - 1) // TILE)[None]
 
         def head(final_rows):
-            logits = dot(final_rows, vocab)
-            highest = jnp.max(logits, axis=1)
-            total_exp = jnp.sum(jnp.exp(logits - highest[:, None]), axis=1)
-            picked = jnp.sum(jnp.where(target_hit, logits, 0.0), axis=1)
-            stats = lax.all_gather(jnp.stack([highest, total_exp, picked]), "fsdp", axis=0)
+            logits, own_stats = logit_stats(final_rows, vocab, target_ids, target_tiles)
+            stats = lax.all_gather(own_stats[:, :3].T, "fsdp", axis=0)
             top = jnp.max(stats[:, 0], axis=0)
             log_total = top + jnp.log(
                 jnp.sum(stats[:, 1] * jnp.exp(stats[:, 0] - top[None, :]), axis=0)
             )
             token_loss = (log_total - jnp.sum(stats[:, 2], axis=0)) * token_mask
-            grad_logits = (
-                (jnp.exp(logits - log_total[:, None]) - target_hit.astype(jnp.float32))
-                * token_weight[:, None]
-            ).astype(jnp.bfloat16)
-            grad_rows = sum_fsdp(dot_nt(grad_logits, vocab), fsdp_rank)
+            grad_logits, grad_rows = logit_grads(
+                logits, vocab, target_ids, target_tiles, log_total, token_weight
+            )
+            grad_rows = sum_fsdp(grad_rows, fsdp_rank)
             return grad_rows, grad_logits, token_loss
 
         shares, gains, table_found, source_grad, target_grad, final_rows, grad_logits, token_loss = (
@@ -1074,7 +1203,7 @@
                 source_stream,
                 target_stream,
                 gain_rows,
-                table,
+                biases,
                 weights,
                 layout,
                 head,
@@ -1141,8 +1270,8 @@
     loss_total = small[gain_rows.shape[0] + table_rows, 0]
     factor = orthonormal_rows(factor)
     left_factor, embed_factor = factor[:, :-1], factor[:, -1]
-    factors_blocks = jnp.einsum("kji,rki->rkj", left_blocks, left_factor, precision=lax.Precision.HIGH)
-    factors_embed = jnp.einsum("vd,rd->rv", left_embed, embed_factor, precision=lax.Precision.HIGH)
+    factors_blocks = jnp.einsum("kji,rki->rkj", left_blocks, left_factor, precision=lax.Precision.DEFAULT)
+    factors_embed = jnp.einsum("vd,rd->rv", left_embed, embed_factor, precision=lax.Precision.DEFAULT)
     both = sum_cuts(jnp.concatenate([factors_blocks.reshape(rank, -1), factors_embed], axis=1))
     factors_embed = both[:, -vocab_rows:]
     factors_blocks = both[:, :-vocab_rows].reshape(factors_blocks.shape)
@@ -1153,14 +1282,14 @@
         * jnp.einsum("krs,skj->rkj", gram_blocks, factors_blocks, precision=lax.Precision.HIGH)
     ) + jnp.sum(factors_embed * jnp.dot(gram_embed, factors_embed, precision=lax.Precision.HIGH))
     squares = lax.psum(squares, "fsdp")
-    full_blocks = jnp.einsum("rki,rkj->kji", left_factor, factors_blocks, precision=lax.Precision.HIGH)
-    full_embed = jnp.einsum("rv,rd->vd", factors_embed, embed_factor, precision=lax.Precision.HIGH)
+    full_blocks = jnp.einsum("rki,rkj->kji", left_factor, factors_blocks, precision=lax.Precision.DEFAULT)
+    full_embed = jnp.einsum("rv,rd->vd", factors_embed, embed_factor, precision=lax.Precision.DEFAULT)
     owned_rows = blocks.shape[0]
     owned_columns = embedding.shape[1]
     own_left = lax.dynamic_slice_in_dim(left_factor, cuts_rank * owned_rows, owned_rows, 2)
     own_right = lax.dynamic_slice_in_dim(embed_factor, cuts_rank * owned_columns, owned_columns, 1)
-    own_blocks = jnp.einsum("rki,rkj->ikj", own_left, factors_blocks, precision=lax.Precision.HIGH)
-    own_embed = jnp.einsum("rv,rd->vd", factors_embed, own_right, precision=lax.Precision.HIGH)
+    own_blocks = jnp.einsum("rki,rkj->ikj", own_left, factors_blocks, precision=lax.Precision.DEFAULT)
+    own_embed = jnp.einsum("rv,rd->vd", factors_embed, own_right, precision=lax.Precision.DEFAULT)
     small_squares = jnp.sum(gains_grad * gains_grad) + jnp.sum(table_grad * table_grad)
     grad_norm = jnp.sqrt(squares + small_squares)
     clip_factor = jnp.minimum(1.0, CLIP_NORM / grad_norm)

time: 1100 us -> 1050 us (0.955); the launches traced: 1110 us -> 1030 us
  Pallas kernels: 131 us -> 185 us
  matrix products: 294 us -> 254 us
  starting transfers between devices: 109 us -> 69.9 us
  waiting for transfers between devices: 233 us -> 200 us
  other arithmetic: 121 us -> 105 us
    ppermute x27, starting transfers between devices: 91.8 us -> 53.6 us  [exchange(): lax.ppermute(array, 'cuts', [(i, i ^ mask) for i in range(lax.axis_size('...]
    pallas_call x0 -> x2, Pallas kernels: none -> 37.6 us  [the longest x1 20.6 us: logit_grads(): pl.pallas_call(lambda *refs: logit_grad_kernel(rows_in, *refs), grid_spec...]
    psum x1, waiting for transfers between devices: 74.4 us -> 54.7 us  [one_round(): lax.psum(table[:size], 'fsdp')]
    ppermute x12, waiting for transfers between devices: 68.7 us -> 49.7 us  [shifted(): lax.ppermute(array, 'fsdp', [(i, (i + distance) % count) for i in range(c...]
    dot_general x14 -> x13, matrix products: 81 us -> 68.1 us  [dot_nt(): lax.dot_general(left, right, (((1,), (1,)), ((), ())), preferred_element_...]
    reduce_sum x2 -> x0, other arithmetic: 12.9 us -> none  [the longest x1 6.44 us: head(): total_exp = jnp.sum(jnp.exp(logits - highest[:, None]), axis=1)]
    dot_general x1 -> x0, local copies, waits for them, and re-layouts: 12.8 us -> none  [dot(): return jnp.dot(left, right, preferred_element_type=jnp.float32)]
    dot_general x14 -> x13, matrix products: 61.2 us -> 49.9 us  [dot(): return jnp.dot(left, right, preferred_element_type=jnp.float32)]
  transfers between devices with their start and end apart: 41 -> 41, of which waited for: 18 -> 18; matrix products, arithmetic and copies ran while one was open for 12% -> 13% of each run, Pallas kernels for 4% -> 4%
where the time goes in v3:
time: 1050 us; the launch traced here: 1030 us
  matrix products  254 us (24%)
  waiting for transfers between devices  200 us (19%)
  Pallas kernels  185 us (18%)
  local copies, waits for them, and re-layouts  119 us (11%)
  other arithmetic  105 us (10%)
  starting transfers between devices  69.9 us (7%)
  blocking collectives  57.9 us (6%)
  between operations  21.2 us (2%)
  loops' own time  18.1 us (2%)
    ppermute x27, waiting for transfers between devices, exchange(): lax.ppermute(array, 'cuts', [(i, i ^ mask) for i in range(lax.axis_size('...  96 us
    dot_general x13, matrix products, dot_nt(): lax.dot_general(left, right, (((1,), (1,)), ((), ())), preferred_element_...  68.1 us
    psum x1, waiting for transfers between devices, one_round(): lax.psum(table[:size], 'fsdp')  54.7 us
    ppermute x27, starting transfers between devices, exchange(): lax.ppermute(array, 'cuts', [(i, i ^ mask) for i in range(lax.axis_size('...  53.6 us
    dot_general x13, matrix products, dot(): return jnp.dot(left, right, preferred_element_type=jnp.float32)  49.9 us
    ppermute x12, waiting for transfers between devices, shifted(): lax.ppermute(array, 'fsdp', [(i, (i + distance) % count) for i in range(c...  49.7 us
    pallas_call x3, Pallas kernels, packed_backward(): pl.pallas_call(lambda *refs: backward_kernel(causal, biased, *refs), grid...  44.1 us
    while x319, local copies, waits for them, and re-layouts  41.7 us
  transfers between devices with their start and end apart: 41, of which 18 were waited for; matrix products, arithmetic and copies ran while one was open for 13% of the time, Pallas kernels for 4%

profile of v3, /device:TPU:0, one launch (start us, length us, event | category | flops | bytes accessed | tf_op | source)
XLA Modules:
  0.0 1030.5 jit_solution(5116166879678853741)
XLA Ops:
  14.3 13.3 %all-gather.4 = s32[4,2,642]{2,1,0:T(2,128)S(1)} all-gather(s32[1,2,642]{2,1,0:T(2,128)S(1)} %add_bitcast_fusion), channel_id=1, replica_groups=mesh['cuts'=8,'fsdp'=4] {'fsdp'}, dimensions={0}, use_global_device_ids=true | all-gather | bytes 25680 | tf_op jit(solution)/shard_map/all_gather | solution.py:1003
  29.2 6.4 all-reduce.9
  60.6 34.7 %collective-permute-done.24 = bf16[12,96,192]{2,1,0:T(8,128)(2,1)} collective-permute-done((bf16[12,96,192]{2,1,0:T(8,128)(2,1)}, bf16[12,96,192]{2,1,0:T(8,128)(2,1)}, u32[]{:S(2)}, u32[]{:S(2)}) %collective-permute-start.24) | collective-permute-done | bytes 442400 | tf_op jit(solution)/shard_map/ppermute | solution.py:65
  110.0 17.7 %collective-permute-done.29 = bf16[1,6,96,768]{3,2,1,0:T(8,128)(2,1)} collective-permute-done((bf16[1,6,96,768]{3,2,1,0:T(8,128)(2,1)}, bf16[1,6,96,768]{3,2,1,0:T(8,128)(2,1)}, u32[]{:S(2)}, u32[]{:S(2)}) %collective-permute-start.29) | collective-permute-done | bytes 884768 | tf_op jit(solution)/shard_map/ppermute | solution.py:60
  134.7 674.8 %while.29 = (pred[]{:T(512)}, s32[]{:T(128)}, f32[]{:T(128)}, f32[]{:T(128)}, f32[28,192,768]{2,1,0:T(8,128)}, /*index=5*/f32[8032,768]{1,0:T(8,128)}, f32[7,768...) while((pred[]{:T(512)}, s32[]{:T(128)}, f32[]{:T(128)}, ...), condition=%wide.region_63.65_spmd, body=%wide.region_5.64_spmd.sunk | while | flops 170000547840 | bytes 2084893568 | solution.py:1234
  153.9 7.1 gather_fusion.2
  164.5 5.2 place.25.refs_2_
  174.2 18.7 %lookup.8 = bf16[1792,768]{1,0:T(8,128)(2,1)S(1)} custom-call(s32[3]{0:T(128)S(1)} %pad_add_fusion.4.refs_0_, s32[1792,1]{1,0:T(8,128)S(1)} %copy-done.16, bf16[768,8032]{1,0:T(8,128)(2,1)} %copy-done.1), custom_call_target="tpu_custom_call" | custom-call | flops 22108176384 | bytes 94371840 | tf_op jit(solution)/shard_map/while/body/lookup/pallas_call | solution.py:570
  200.2 9.7 collective-permute-start.5
  223.4 59.8 %conditional.2 = (bf16[1280,768]{1,0:T(8,128)(2,1)}) conditional(s32[]{:T(128)} %clamp.20, bf16[1280,768]{1,0:T(8,128)(2,1)} %slice.660, bf16[1280,768]{1,0:T(8,128)(2,1)} %slice.660, bf16[1280,768]{1,0:T(8,128)(2,1)} %slice.660, bf16[1280,768]{1,0:T(8,128)(2,1)} %slice.660), branch_computations={%region_23.25_spmd, %region_25.27_spmd, %region_27.29_spmd, %regio... | conditional | flops 983040 | bytes 16121906 | solution.py:1140
  225.8 54.7 %all-reduce.18.cloned.1.call-done = bf16[768,768]{1,0:T(8,128)(2,1)} async-done(((bf16[768,768]{1,0:T(8,128)(2,1)}), bf16[768,768]{1,0:T(8,128)(2,1)}) %all-reduce.18.cloned.1.call-update) | async-done | bytes 1179664 | tf_op jit(solution)/shard_map/while/body/cond/branch_1_fun/psum | solution.py:1144
  290.5 9.6 place.26
  308.8 5.8 convolution_convert_fusion.21.refs_3_.refs_4_.refs_5_
  314.7 15.7 %collective-permute-done.10 = bf16[1,8,96,768]{3,2,1,0:T(8,128)(2,1)} collective-permute-done((bf16[1,8,96,768]{3,2,1,0:T(8,128)(2,1)}, bf16[1,8,96,768]{3,2,1,0:T(8,128)(2,1)}, u32[]{:S(2)}, u32[]{:S(2)}) %collective-permute-start.10) | collective-permute-done | bytes 1179680 | tf_op jit(solution)/shard_map/while/body/ppermute | solution.py:60
  339.0 8.7 attend.24
  356.5 28.2 %collective-permute-done.11 = bf16[2,8,96,768]{3,2,1,0:T(8,128)(2,1)S(1)} collective-permute-done((bf16[2,8,96,768]{3,2,1,0:T(8,128)(2,1)S(1)}, bf16[2,8,96,768]{3,2,1,0:T(8,128)(2,1)S(1)}, u32[]{:S(2)}, u32[]{:S(2)}) %collective-permute-start.11) | collective-permute-done | bytes 2359328 | tf_op jit(solution)/shard_map/while/body/ppermute | solution.py:60
  388.4 9.3 fusion.478
  397.7 14.5 %multiply_reduce_fusion.26 = (f32[1280]{0:T(1024)S(1)}, f32[1280,768]{1,0:T(8,128)}) fusion(f32[1280,768]{1,0:T(8,128)S(1)} %get-tuple-element.1878, bf16[3072,768]{1,0:T(8,128)(2,1)S(1)} %bitcast.355, f32[1280,3072]{1,0:T(8,128)} %fusion.478), kind=kOutput, calls=%fused_computation.61.clone.1 | convolution fusion | flops 6078135296 | bytes 28316672 | tf_op jit(solution)/shard_map/while/body/dot_general | solution.py:48
  456.4 17.0 %logits.8 = (f32[384,8032]{1,0:T(8,128)S(1)}, f32[384,128]{1,0:T(8,128)S(1)}) custom-call(s32[1]{0:T(128)} %bitcast.330.refs_0_, bf16[384,768]{1,0:T(8,128)(2,1)S(1)} %multiply_convert_fusion.36.refs_1_.final_ref, bf16[768,8032]{1,0:T(8,128)(2,1)} %copy-done.1, s32[384,1]{1,0:T(8,128)S(1)} %broadcast_in_dim.754.refs_3_), custom_call_target="tpu_custom_call" | custom-call | flops 4737466368 | bytes 41943040 | tf_op jit(solution)/shard_map/while/body/logits/pallas_call | solution.py:694
  477.9 13.1 %all-gather.6 = f32[4,3,384]{2,1,0:T(4,128)S(1)} all-gather(f32[1,3,384]{2,1,0:T(4,128)S(1)} %copy.353), channel_id=2, replica_groups=mesh['cuts'=8,'fsdp'=4] {'fsdp'}, dimensions={0}, use_global_device_ids=true | all-gather | bytes 23040 | tf_op jit(solution)/shard_map/while/body/all_gather | solution.py:1189
  491.8 20.6 %logit_grads.8 = (bf16[384,8032]{1,0:T(8,128)(2,1)S(1)}, f32[384,768]{1,0:T(8,128)S(1)}) custom-call(s32[1]{0:T(128)} %bitcast.330.refs_0_, f32[384,8032]{1,0:T(8,128)} %copy-done.2, bf16[768,8032]{1,0:T(8,128)(2,1)} %copy-done.1, s32[384,1]{1,0:T(8,128)S(1)} %broadcast_in_dim.754.refs_3_, f32[384,1]{1,0:T(8,128)S(1)} %add.2169.refs_4_, ...), custom_call_target="tpu_custom_call" | custom-call | flops 4737466368 | bytes 41943040 | tf_op jit(solution)/shard_map/while/body/logit_grads/pallas_call | solution.py:751
  521.2 7.9 collective-permute-done.14
  543.7 8.6 fusion.490
  557.7 10.8 %attend_back.24 = (bf16[384,768]{1,0:T(8,128)(2,1)}, bf16[1280,1536]{1,0:T(8,128)(2,1)}) custom-call(s32[3]{0:T(128)} %copy-done.31, s32[3]{0:T(128)} %copy-done.30, bf16[384,768]{1,0:T(8,128)(2,1)} %copy-done.20, bf16[384,768]{1,0:T(8,128)(2,1)} %convolution_convert_fusion.26.refs_3_, bf16[1280,1536]{1,0:T(8,128)(2,1)} %copy-done.47, ...), custom_call_target="tpu_custom_call" | custom-call | flops 7549747200 | bytes 41943040 | tf_op jit(solution)/shard_map/while/body/attend_back/pallas_call | solution.py:491
  574.5 5.9 multiply_reduce_fusion.31
  585.2 18.5 %fusion.493 = bf16[1280,3072]{1,0:T(8,128)(2,1)S(1)} fusion(f32[1280,3072]{1,0:T(8,128)} %fusion.478, bf16[1280,768]{1,0:T(8,128)(2,1)S(1)} %fusion.492, bf16[3072,768]{1,0:T(8,128)(2,1)} %get-tuple-element.1882), kind=kOutput, calls=%fused_computation.12.clone.1 | convolution fusion | flops 6118440960 | bytes 30277632 | tf_op jit(solution)/shard_map/while/body/dot_general | solution.py:52
  603.8 8.9 multiply_reduce_fusion.32
  612.7 12.7 %attend_back.26 = (bf16[384,768]{1,0:T(8,128)(2,1)}, bf16[384,1536]{1,0:T(8,128)(2,1)}, f32[5,6,128,256]{3,2,1,0:T(8,128)}) custom-call(s32[3]{0:T(128)} %copy-done.27, s32[3]{0:T(128)} %copy-done.26, bf16[384,768]{1,0:T(8,128)(2,1)} %copy-done.23, bf16[384,768]{1,0:T(8,128)(2,1)} %convolution_convert_fusion.28.refs_3_, bf16[384,1536]{1,0:T(8,128)(2,1)} %copy-done.3, ...), custom_call_target="tpu_custom_call" | custom-call | flops 2264924160 | bytes 41943040 | tf_op jit(solution)/shard_map/while/body/attend_back/pallas_call | solution.py:491
  631.6 6.8 constant_dynamic-slice_fusion.30
  638.3 11.1 %fusion.495 = f32[192,3072]{1,0:T(8,128)} fusion(bf16[1280,768]{1,0:T(8,128)(2,1)} %copy-done.79, s32[]{:T(128)} %get-tuple-element.2156, f32[1280,3072]{1,0:T(8,128)} %fusion.478), kind=kOutput, calls=%fused_computation.158.clone.1 | convolution fusion | flops 1545338880 | bytes 18743808 | tf_op jit(solution)/shard_map/while/body/dot_general | solution.py:56
  660.7 8.6 fusion.494
  672.3 20.6 %attend_back.25 = (bf16[1280,768]{1,0:T(8,128)(2,1)}, bf16[1280,1536]{1,0:T(8,128)(2,1)}, f32[5,6,128,256]{3,2,1,0:T(8,128)}) custom-call(s32[10]{0:T(128)} %copy-done.29, s32[10]{0:T(128)} %copy-done.28, bf16[1280,768]{1,0:T(8,128)(2,1)} %copy-done.48, bf16[1280,768]{1,0:T(8,128)(2,1)} %convolution_convert_fusion.27.refs_3_, bf16[1280,1536]{1,0:T(8,128)(2,1)} %copy-done.49, ...), custom_call_target="tpu_custom_call" | custom-call | flops 25165824000 | bytes 41943040 | tf_op jit(solution)/shard_map/while/body/attend_back/pallas_call | solution.py:491
  707.2 6.9 fusion.502
  754.9 18.4 %select_add_fusion.2 = f32[28,192,768]{2,1,0:T(8,128)} fusion(f32[28,192,768]{2,1,0:T(8,128)} %bitcast.331, f32[28,192,768]{2,1,0:T(8,128)} %get-tuple-element.1977, f32[28,192,768]{2,1,0:T(8,128)} %get-tuple-element.2066, pred[]{:T(512)S(6)} %eq.814), kind=kLoop, calls=%fused_computation.5.clone.1 | loop fusion | flops 8257536 | bytes 66060288 | tf_op jit(solution)/shard_map/while/body/add | solution.py:1225
  773.4 30.6 %vocab_grad.8 = f32[8032,768]{1,0:T(8,128)} custom-call(s32[4]{0:T(128)S(1)} %pad_add_fusion.5.blocks_ref, s32[1,1792]{1,0:T(1,128)S(1)} %broadcast_in_dim.755.id_ref, bf16[1792,768]{1,0:T(8,128)(2,1)S(1)} %fusion.504.grad_ref, bf16[384,8032]{1,0:T(8,128)(2,1)S(1)} %bitcast.335, bf16[384,768]{1,0:T(8,128)(2,1)S(1)} %copy-done.22, ...), custom_call_target="tpu_custom_call", output_to_operand_aliasing={{}: (6, {})} | custom-call | flops 26845642752 | bytes 104857600 | tf_op jit(solution)/shard_map/while/body/vocab_grad/pallas_call | solution.py:611
  809.5 7.9 convolution_bitcast_fusion
  817.5 10.8 %convolution_bitcast_fusion.4 = f32[8,1,768]{2,0,1:T(8,128)S(1)} fusion(f32[8032,768]{1,0:T(8,128)} %get-tuple-element.2373, f32[8032,8]{0,1:T(8,128)S(1)} %copy-done), kind=kOutput, calls=%fused_computation.436 | convolution fusion | flops 296091648 | bytes 24955904 | tf_op jit(solution)/shard_map/vd,vr->rd/dot_general | solution.py:1252
  830.3 23.2 %collective-permute-start.30 = (f32[128,768]{1,0:T(8,128)S(1)}, f32[128,768]{1,0:T(8,128)}, u32[]{:S(2)}, u32[]{:S(2)}) collective-permute-start(f32[128,768]{1,0:T(8,128)S(1)} %pad_dynamic-slice_fusion), channel_id=1, source_target_pairs={{0,4},{4,0},{8,12},{12,8},{16,20},{20,16},{24,28},{28,24},{1,5},{5... | collective-permute-start | bytes 1179656 | tf_op jit(solution)/shard_map/ppermute | solution.py:60
  856.9 7.5 collective-permute-done.31
  871.6 15.3 %all-gather.2 = f32[128,768]{1,0:T(8,128)S(1)} all-gather(f32[32,768]{1,0:T(8,128)S(1)} %dynamic-slice_add_fusion.1), channel_id=4, replica_groups=mesh['cuts'=8,'fsdp'=4] {'fsdp'}, dimensions={0}, use_global_device_ids=true | all-gather | bytes 491520 | tf_op jit(solution)/shard_map/all_gather | solution.py:105
  916.4 8.2 fusion.170
  924.8 11.4 %convolution_convert_fusion.9 = bf16[8,8032]{1,0:T(8,128)(2,1)S(1)} fusion(f32[8032,768]{1,0:T(8,128)} %get-tuple-element.2373, f32[8,1,768]{2,1,0:T(1,128)S(1)} %slice.526), kind=kOutput, calls=%fused_computation.416 | convolution fusion | flops 98697216 | bytes 24827392 | tf_op jit(solution)/shard_map/vd,rd->rv/dot_general | solution.py:1274
  946.1 6.0 collective-permute-done.38
  952.2 16.3 %subtract_bitcast_fusion = f32[1,8032,768]{2,1,0:T(8,128)} fusion(f32[8032,768]{1,0:T(8,128)} %get-tuple-element.2373, f32[8,13408]{1,0:T(8,128)S(1)} %convert_add_fusion.2, f32[8,1,768]{2,1,0:T(1,128)S(1)} %slice.526), kind=kOutput, calls=%fused_computation.410 | convolution fusion | flops 104865792 | bytes 49502208 | tf_op jit(solution)/shard_map/rv,rd->vd/dot_general | solution.py:1286
  972.6 14.5 %subtract_bitcast_fusion.1 = f32[1,768,28,192]{1,3,2,0:T(8,128)} fusion(f32[28,192,768]{2,1,0:T(8,128)} %get-tuple-element.2372, f32[8,28,768]{2,1,0:T(8,128)} %bitcast.341, f32[8,28,192]{2,1,0:T(8,128)S(1)} %reshape.832), kind=kOutput, calls=%fused_computation.411 | convolution fusion | flops 70189056 | bytes 33890304 | tf_op jit(solution)/shard_map/rki,rkj->kji/dot_general | solution.py:1285
  987.2 9.7 psum.49
  1001.3 5.2 multiply_subtract_fusion.1
  1015.4 5.8 multiply_subtract_fusion
  (722 shorter events, 363.1 us)
Async XLA Ops:
  7.2 810.3 %copy-start = (f32[8032,8]{0,1:T(8,128)S(1)}, f32[8032,8]{0,1:T(8,128)}, u32[]{:S(2)}) copy-start(f32[8032,8]{0,1:T(8,128)} %param.41) | copy-start | bytes 771076
  9.5 26.2 %collective-permute-start.19 = (bf16[1,1,48,8032]{3,2,1,0:T(8,128)(2,1)S(1)}, bf16[1,1,48,8032]{3,2,1,0:T(8,128)(2,1)}, u32[]{:S(2)}, u32[]{:S(2)}) collective-permute-start(bf16[1,1,48,8032]{3,2,1,0:T(8,128)(2,1)S(1)} %get-tuple-element.1389), channel_id=1, source_target_pairs={{0,8},{4,12},{8,0},{12,4},{16,24},{20,28},{24,16},{28,20},{1,9},{5... | collective-permute-start | bytes 2313224 | tf_op jit(solution)/shard_map/ppermute | solution.py:60
  12.5 24.9 %collective-permute-start.20 = (bf16[1,1,48,8032]{3,2,1,0:T(8,128)(2,1)S(1)}, bf16[1,1,48,8032]{3,2,1,0:T(8,128)(2,1)}, u32[]{:S(2)}, u32[]{:S(2)}) collective-permute-start(bf16[1,1,48,8032]{3,2,1,0:T(8,128)(2,1)S(1)} %get-tuple-element.1388), channel_id=1, source_target_pairs={{0,16},{4,20},{8,24},{12,28},{16,0},{20,4},{24,8},{28,12},{1,17},{... | collective-permute-start | bytes 2313224 | tf_op jit(solution)/shard_map/ppermute | solution.py:60
  40.4 57.6 %collective-permute-start.21 = (bf16[2,1,48,8032]{3,2,1,0:T(8,128)(2,1)S(1)}, bf16[2,1,48,8032]{3,2,1,0:T(8,128)(2,1)}, u32[]{:S(2)}, u32[]{:S(2)}) collective-permute-start(bf16[2,1,48,8032]{3,2,1,0:T(8,128)(2,1)S(1)} %pad_maximum_fusion.13), channel_id=1, source_target_pairs={{0,16},{4,20},{8,24},{12,28},{16,0},{20,4},{24,8},{28,12},{1,17},{... | collective-permute-start | bytes 4626440 | tf_op jit(solution)/shard_map/ppermute | solution.py:60
  43.1 17.5 %collective-permute-start.23 = (bf16[12,96,192]{2,1,0:T(8,128)(2,1)}, bf16[12,96,192]{2,1,0:T(8,128)(2,1)}, u32[]{:S(2)}, u32[]{:S(2)}) collective-permute-start(bf16[12,96,192]{2,1,0:T(8,128)(2,1)} %slice.487), channel_id=1, source_target_pairs={{0,3},{1,0},{2,1},{3,2},{4,7},{5,4},{6,5},{7,6},{8,11},{9,8},{10,9... | collective-permute-start | bytes 1327112 | tf_op jit(solution)/shard_map/ppermute | solution.py:65
  46.5 48.8 %collective-permute-start.24 = (bf16[12,96,192]{2,1,0:T(8,128)(2,1)}, bf16[12,96,192]{2,1,0:T(8,128)(2,1)}, u32[]{:S(2)}, u32[]{:S(2)}) collective-permute-start(bf16[12,96,192]{2,1,0:T(8,128)(2,1)} %slice.487), channel_id=1, source_target_pairs={{0,2},{1,3},{2,0},{3,1},{4,6},{5,7},{6,4},{7,5},{8,10},{9,11},{10,... | collective-permute-start | bytes 1327112 | tf_op jit(solution)/shard_map/ppermute | solution.py:65
  46.5 48.8 %collective-permute-start.25 = (bf16[12,96,192]{2,1,0:T(8,128)(2,1)}, bf16[12,96,192]{2,1,0:T(8,128)(2,1)}, u32[]{:S(2)}, u32[]{:S(2)}) collective-permute-start(bf16[12,96,192]{2,1,0:T(8,128)(2,1)} %slice.487), channel_id=1, source_target_pairs={{0,1},{1,2},{2,3},{3,0},{4,5},{5,6},{6,7},{7,4},{8,9},{9,10},{10,1... | collective-permute-start | bytes 1327112 | tf_op jit(solution)/shard_map/ppermute | solution.py:65
  47.3 52.9 %collective-permute-start.22 = (bf16[2,1,48,8032]{3,2,1,0:T(8,128)(2,1)}, bf16[2,1,48,8032]{3,2,1,0:T(8,128)(2,1)}, u32[]{:S(2)}, u32[]{:S(2)}) collective-permute-start(bf16[2,1,48,8032]{3,2,1,0:T(8,128)(2,1)} %pad_maximum_fusion.14), channel_id=1, source_target_pairs={{0,8},{4,12},{8,0},{12,4},{16,24},{20,28},{24,16},{28,20},{1,9},{5... | collective-permute-start | bytes 4626440 | tf_op jit(solution)/shard_map/ppermute | solution.py:60
  104.1 29.4 %collective-permute-start.26 = (bf16[4,1,48,8032]{3,2,1,0:T(8,128)(2,1)S(1)}, bf16[4,1,48,8032]{3,2,1,0:T(8,128)(2,1)}, u32[]{:S(2)}, u32[]{:S(2)}) collective-permute-start(bf16[4,1,48,8032]{3,2,1,0:T(8,128)(2,1)S(1)} %pad_maximum_fusion.8), channel_id=1, source_target_pairs={{0,4},{4,0},{8,12},{12,8},{16,20},{20,16},{24,28},{28,24},{1,5},{5... | collective-permute-start | bytes 9252872 | tf_op jit(solution)/shard_map/ppermute | solution.py:60
  104.1 29.4 %collective-permute-start.27 = (bf16[4,1,48,8032]{3,2,1,0:T(8,128)(2,1)}, bf16[4,1,48,8032]{3,2,1,0:T(8,128)(2,1)}, u32[]{:S(2)}, u32[]{:S(2)}) collective-permute-start(bf16[4,1,48,8032]{3,2,1,0:T(8,128)(2,1)} %pad_maximum_fusion.9), channel_id=1, source_target_pairs={{0,4},{4,0},{8,12},{12,8},{16,20},{20,16},{24,28},{28,24},{1,5},{5... | collective-permute-start | bytes 9252872 | tf_op jit(solution)/shard_map/ppermute | solution.py:60
  105.9 21.9 %collective-permute-start.29 = (bf16[1,6,96,768]{3,2,1,0:T(8,128)(2,1)}, bf16[1,6,96,768]{3,2,1,0:T(8,128)(2,1)}, u32[]{:S(2)}, u32[]{:S(2)}) collective-permute-start(bf16[1,6,96,768]{3,2,1,0:T(8,128)(2,1)} %get-tuple-element.1386), channel_id=1, source_target_pairs={{0,16},{4,20},{8,24},{12,28},{16,0},{20,4},{24,8},{28,12},{1,17},{... | collective-permute-start | bytes 2654216 | tf_op jit(solution)/shard_map/ppermute | solution.py:60
  106.6 24.0 %collective-permute-start.28 = (bf16[1,6,96,768]{3,2,1,0:T(8,128)(2,1)}, bf16[1,6,96,768]{3,2,1,0:T(8,128)(2,1)}, u32[]{:S(2)}, u32[]{:S(2)}) collective-permute-start(bf16[1,6,96,768]{3,2,1,0:T(8,128)(2,1)} %get-tuple-element.1387), channel_id=1, source_target_pairs={{0,8},{4,12},{8,0},{12,4},{16,24},{20,28},{24,16},{28,20},{1,9},{5... | collective-permute-start | bytes 2654216 | tf_op jit(solution)/shard_map/ppermute | solution.py:60
  135.1 148.3 %collective-permute-start.2 = (bf16[16,96,192]{2,1,0:T(8,128)(2,1)}, bf16[16,96,192]{2,1,0:T(8,128)(2,1)}, u32[]{:S(2)}, u32[]{:S(2)}) collective-permute-start(bf16[16,96,192]{2,1,0:T(8,128)(2,1)} %get-tuple-element.1857), channel_id=1, source_target_pairs={{0,1},{1,2},{2,3},{3,0},{4,5},{5,6},{6,7},{7,4},{8,9},{9,10},{10,1... | collective-permute-start | bytes 1769480 | tf_op jit(solution)/shard_map/while/body/ppermute | solution.py:65
  135.7 147.7 %collective-permute-start.3 = (bf16[16,96,192]{2,1,0:T(8,128)(2,1)}, bf16[16,96,192]{2,1,0:T(8,128)(2,1)}, u32[]{:S(2)}, u32[]{:S(2)}) collective-permute-start(bf16[16,96,192]{2,1,0:T(8,128)(2,1)} %get-tuple-element.1857), channel_id=1, source_target_pairs={{0,2},{1,3},{2,0},{3,1},{4,6},{5,7},{6,4},{7,5},{8,10},{9,11},{10,... | collective-permute-start | bytes 1769480 | tf_op jit(solution)/shard_map/while/body/ppermute | solution.py:65
  137.7 145.8 %collective-permute-start.4 = (bf16[16,96,192]{2,1,0:T(8,128)(2,1)}, bf16[16,96,192]{2,1,0:T(8,128)(2,1)}, u32[]{:S(2)}, u32[]{:S(2)}) collective-permute-start(bf16[16,96,192]{2,1,0:T(8,128)(2,1)} %get-tuple-element.1857), channel_id=1, source_target_pairs={{0,3},{1,0},{2,1},{3,2},{4,7},{5,4},{6,5},{7,6},{8,11},{9,8},{10,9... | collective-permute-start | bytes 1769480 | tf_op jit(solution)/shard_map/while/body/ppermute | solution.py:65
  140.5 52.4 %collective-permute-start = (bf16[2,6,96,768]{3,2,1,0:T(8,128)(2,1)}, bf16[2,6,96,768]{3,2,1,0:T(8,128)(2,1)}, u32[]{:S(2)}, u32[]{:S(2)}) collective-permute-start(bf16[2,6,96,768]{3,2,1,0:T(8,128)(2,1)} %get-tuple-element.1838), channel_id=1, source_target_pairs={{0,16},{4,20},{8,24},{12,28},{16,0},{20,4},{24,8},{28,12},{1,17},{... | collective-permute-start | bytes 5308424 | tf_op jit(solution)/shard_map/while/body/ppermute | solution.py:60
  141.4 55.2 %collective-permute-start.1 = (bf16[2,6,96,768]{3,2,1,0:T(8,128)(2,1)}, bf16[2,6,96,768]{3,2,1,0:T(8,128)(2,1)}, u32[]{:S(2)}, u32[]{:S(2)}) collective-permute-start(bf16[2,6,96,768]{3,2,1,0:T(8,128)(2,1)} %get-tuple-element.1839), channel_id=1, source_target_pairs={{0,8},{4,12},{8,0},{12,4},{16,24},{20,28},{24,16},{28,20},{1,9},{5... | collective-permute-start | bytes 5308424 | tf_op jit(solution)/shard_map/while/body/ppermute | solution.py:60
  200.2 90.3 %collective-permute-start.5 = (bf16[4,6,96,768]{3,2,1,0:T(8,128)(2,1)}, bf16[4,6,96,768]{3,2,1,0:T(8,128)(2,1)}, u32[]{:S(2)}, u32[]{:S(2)}) collective-permute-start(bf16[4,6,96,768]{3,2,1,0:T(8,128)(2,1)} %pad_maximum_fusion.24.refs_1_), channel_id=1, source_target_pairs={{0,4},{4,0},{8,12},{12,8},{16,20},{20,16},{24,28},{28,24},{1,5},{5... | collective-permute-start | bytes 10616840 | tf_op jit(solution)/shard_map/while/body/ppermute | solution.py:60
  209.9 80.6 %collective-permute-start.6 = (bf16[4,6,96,768]{3,2,1,0:T(8,128)(2,1)}, bf16[4,6,96,768]{3,2,1,0:T(8,128)(2,1)}, u32[]{:S(2)}, u32[]{:S(2)}) collective-permute-start(bf16[4,6,96,768]{3,2,1,0:T(8,128)(2,1)} %pad_maximum_fusion.25.refs_3_), channel_id=1, source_target_pairs={{0,4},{4,0},{8,12},{12,8},{16,20},{20,16},{24,28},{28,24},{1,5},{5... | collective-permute-start | bytes 10616840 | tf_op jit(solution)/shard_map/while/body/ppermute | solution.py:60
  215.0 208.7 %copy-start.26 = (s32[3]{0:T(128)}, s32[3]{0:T(128)S(1)}, u32[]{:S(2)}) copy-start(s32[3]{0:T(128)S(1)} %get-tuple-element.1900.refs_1_) | copy-start | bytes 40 | tf_op jit(solution)/shard_map/while
  215.1 208.7 %copy-start.27 = (s32[3]{0:T(128)}, s32[3]{0:T(128)S(1)}, u32[]{:S(2)}) copy-start(s32[3]{0:T(128)S(1)} %get-tuple-element.1899.refs_0_) | copy-start | bytes 40 | tf_op jit(solution)/shard_map/while
  215.1 222.4 %copy-start.24 = (s32[1,384]{1,0:T(1,128)}, s32[1,384]{1,0:T(1,128)S(1)}, u32[]{:S(2)}) copy-start(s32[1,384]{1,0:T(1,128)S(1)} %broadcast_in_dim.752.refs_5_.refs_7_) | copy-start | bytes 4612 | tf_op jit(solution)/shard_map/while
  220.4 202.6 %copy-start.121 = (f32[768]{0:T(1024)}, f32[768]{0:T(1024)S(1)}, u32[]{:S(2)}) copy-start(f32[768]{0:T(1024)S(1)} %get-tuple-element.1904) | copy-start | bytes 9220 | tf_op jit(solution)/shard_map/while
  221.1 216.4 %copy-start.30 = (s32[3]{0:T(128)}, s32[3]{0:T(128)S(1)}, u32[]{:S(2)}) copy-start(s32[3]{0:T(128)S(1)} %get-tuple-element.1893.refs_1_) | copy-start | bytes 40 | tf_op jit(solution)/shard_map/while
  221.1 216.4 %copy-start.31 = (s32[3]{0:T(128)}, s32[3]{0:T(128)S(1)}, u32[]{:S(2)}) copy-start(s32[3]{0:T(128)S(1)} %get-tuple-element.1892.refs_0_) | copy-start | bytes 40 | tf_op jit(solution)/shard_map/while
  223.4 57.1 %all-reduce.18.cloned.1.call-start = ((), (), s32[]{:S(2)}) async-start(), calls=%async_computation.1 | async-start | bytes 2359296 | tf_op jit(solution)/shard_map/while/body/cond/branch_1_fun/psum | solution.py:1144
  283.2 132.8 %all-reduce.24.cloned.1.call-start = ((), (), s32[]{:S(2)}) async-start(), calls=%async_computation.4 | async-start | bytes 1179648 | tf_op jit(solution)/shard_map/while/body/psum | solution.py:1169
  302.1 28.2 %collective-permute-start.10 = (bf16[1,8,96,768]{3,2,1,0:T(8,128)(2,1)}, bf16[1,8,96,768]{3,2,1,0:T(8,128)(2,1)}, u32[]{:S(2)}, u32[]{:S(2)}) collective-permute-start(bf16[1,8,96,768]{3,2,1,0:T(8,128)(2,1)} %get-tuple-element.1895), channel_id=1, source_target_pairs={{0,16},{4,20},{8,24},{12,28},{16,0},{20,4},{24,8},{28,12},{1,17},{... | collective-permute-start | bytes 3538952 | tf_op jit(solution)/shard_map/while/body/ppermute | solution.py:60
  303.6 30.1 %collective-permute-start.7 = (bf16[1,8,96,768]{3,2,1,0:T(8,128)(2,1)}, bf16[1,8,96,768]{3,2,1,0:T(8,128)(2,1)S(1)}, u32[]{:S(2)}, u32[]{:S(2)}) collective-permute-start(bf16[1,8,96,768]{3,2,1,0:T(8,128)(2,1)} %get-tuple-element.1894), channel_id=1, source_target_pairs={{0,8},{4,12},{8,0},{12,4},{16,24},{20,28},{24,16},{28,20},{1,9},{5... | collective-permute-start | bytes 3538952 | tf_op jit(solution)/shard_map/while/body/ppermute | solution.py:60
  332.2 52.4 %collective-permute-start.11 = (bf16[2,8,96,768]{3,2,1,0:T(8,128)(2,1)S(1)}, bf16[2,8,96,768]{3,2,1,0:T(8,128)(2,1)S(1)}, u32[]{:S(2)}, u32[]{:S(2)}) collective-permute-start(bf16[2,8,96,768]{3,2,1,0:T(8,128)(2,1)S(1)} %pad_maximum_fusion.28), channel_id=1, source_target_pairs={{0,8},{4,12},{8,0},{12,4},{16,24},{20,28},{24,16},{28,20},{1,9},{5... | collective-permute-start | bytes 7077896 | tf_op jit(solution)/shard_map/while/body/ppermute | solution.py:60
  334.0 52.3 %collective-permute-start.8 = (bf16[2,8,96,768]{3,2,1,0:T(8,128)(2,1)S(1)}, bf16[2,8,96,768]{3,2,1,0:T(8,128)(2,1)S(1)}, u32[]{:S(2)}, u32[]{:S(2)}) collective-permute-start(bf16[2,8,96,768]{3,2,1,0:T(8,128)(2,1)S(1)} %pad_maximum_fusion.27), channel_id=1, source_target_pairs={{0,16},{4,20},{8,24},{12,28},{16,0},{20,4},{24,8},{28,12},{1,17},{... | collective-permute-start | bytes 7077896 | tf_op jit(solution)/shard_map/while/body/ppermute | solution.py:60
  386.2 31.1 %collective-permute-start.12 = (bf16[4,8,96,768]{3,2,1,0:T(8,128)(2,1)}, bf16[4,8,96,768]{3,2,1,0:T(8,128)(2,1)}, u32[]{:S(2)}, u32[]{:S(2)}) collective-permute-start(bf16[4,8,96,768]{3,2,1,0:T(8,128)(2,1)} %constant_dynamic-update-slice_fusion.17.refs_3_), channel_id=1, source_target_pairs={{0,4},{4,0},{8,12},{12,8},{16,20},{20,16},{24,28},{28,24},{1,5},{5... | collective-permute-start | bytes 14155784 | tf_op jit(solution)/shard_map/while/body/ppermute | solution.py:60
  387.8 29.5 %collective-permute-start.9 = (bf16[4,8,96,768]{3,2,1,0:T(8,128)(2,1)}, bf16[4,8,96,768]{3,2,1,0:T(8,128)(2,1)}, u32[]{:S(2)}, u32[]{:S(2)}) collective-permute-start(bf16[4,8,96,768]{3,2,1,0:T(8,128)(2,1)} %constant_dynamic-update-slice_fusion.14.refs_1_), channel_id=1, source_target_pairs={{0,4},{4,0},{8,12},{12,8},{16,20},{20,16},{24,28},{28,24},{1,5},{5... | collective-permute-start | bytes 14155784 | tf_op jit(solution)/shard_map/while/body/ppermute | solution.py:60
  515.2 6.0 collective-permute-start.13
  516.9 12.3 %collective-permute-start.14 = (bf16[96,768]{1,0:T(8,128)(2,1)S(1)}, bf16[96,768]{1,0:T(8,128)(2,1)S(1)}, u32[]{:S(2)}, u32[]{:S(2)}) collective-permute-start(bf16[96,768]{1,0:T(8,128)(2,1)S(1)} %get-tuple-element.1934), channel_id=1, source_target_pairs={{0,2},{1,3},{2,0},{3,1},{4,6},{5,7},{6,4},{7,5},{8,10},{9,11},{10,... | collective-permute-start | bytes 442376 | tf_op jit(solution)/shard_map/while/body/ppermute | solution.py:65
  516.9 12.3 %collective-permute-start.15 = (bf16[96,768]{1,0:T(8,128)(2,1)S(1)}, bf16[96,768]{1,0:T(8,128)(2,1)S(1)}, u32[]{:S(2)}, u32[]{:S(2)}) collective-permute-start(bf16[96,768]{1,0:T(8,128)(2,1)S(1)} %get-tuple-element.1935), channel_id=1, source_target_pairs={{0,1},{1,2},{2,3},{3,0},{4,5},{5,6},{6,7},{7,4},{8,9},{9,10},{10,1... | collective-permute-start | bytes 442376 | tf_op jit(solution)/shard_map/while/body/ppermute | solution.py:65
  529.2 5.2 collective-permute-start.16
  529.3 9.9 collective-permute-start.17
  531.4 7.9 collective-permute-start.18
  830.3 24.7 %collective-permute-start.30 = (f32[128,768]{1,0:T(8,128)S(1)}, f32[128,768]{1,0:T(8,128)}, u32[]{:S(2)}, u32[]{:S(2)}) collective-permute-start(f32[128,768]{1,0:T(8,128)S(1)} %pad_dynamic-slice_fusion), channel_id=1, source_target_pairs={{0,4},{4,0},{8,12},{12,8},{16,20},{20,16},{24,28},{28,24},{1,5},{5... | collective-permute-start | bytes 1179656 | tf_op jit(solution)/shard_map/ppermute | solution.py:60
  856.9 7.5 collective-permute-start.31
  866.0 4.7 collective-permute-start.32
  887.5 4.8 collective-permute-start.33
  893.3 5.8 collective-permute-start.34
  900.5 7.4 collective-permute-start.35
  936.2 2.0 collective-permute-start.36
  938.3 7.3 collective-permute-start.37
  945.7 6.4 collective-permute-start.38
  (176 other events, 2569.9 us)
Sparse Core Ops, SparseCore 0:
  227.1 53.3 all-reduce.17
  303.8 37.9 all-reduce.23

commit v4 on v3

--- a/solution.py
+++ b/solution.py
@@ -131,15 +131,24 @@
     return [([0], part[None, begin:end]) for begin, end in zip(ends, ends[1:])]
 
 
-def spread_step(shares, step):
+def spread_send(shares, step):
+    ways = spread_ways()
+    return [
+        exchange(held, ways[(turn + step) % len(ways)]) for turn, (_, held) in enumerate(shares)
+    ]
+
+
+def spread_receive(shares, arriving, step):
     ways = spread_ways()
     after = []
-    for turn, (bits, held) in enumerate(shares):
+    for turn, ((bits, held), array) in enumerate(zip(shares, arriving)):
         mask = ways[(turn + step) % len(ways)]
-        after.append(
-            (bits + [bit ^ mask for bit in bits], jnp.concatenate([held, exchange(held, mask)]))
-        )
+        after.append((bits + [bit ^ mask for bit in bits], jnp.concatenate([held, array])))
     return after
+
+
+def spread_step(shares, step):
+    return spread_receive(shares, spread_send(shares, step), step)
 
 
 def spread_end(shares):
@@ -812,9 +821,9 @@
 
 
 def packed_gradients(
-    source_stream, target_stream, gain_rows, biases, weights, layout, head, column_start, column_width
+    source_stream, target_stream, gain_rows, biases, weights, later, layout, head, column_start, column_width
 ):
-    enc_attention, enc_feed, dec_self, dec_cross, dec_feed = weights
+    enc_attention, enc_feed = weights[:3], weights[3:]
     (
         source_span,
         target_span,
@@ -897,6 +906,7 @@
     x1, enc_saved = attention(
         source_stream, gain_rows[0], None, enc_attention, source_span, source_row, source_column, False, bias_source
     )
+    x1, dec_self, dec_cross, dec_feed = later(x1)
     x2, enc_feed_saved = feed(x1, gain_rows[1], enc_feed)
     encoded = root_norm(x2, gain_rows[2]).astype(jnp.bfloat16)
     encoded, target_stream = lax.optimization_barrier((encoded, target_stream))
@@ -1129,11 +1139,15 @@
             ]
         )
         rows = lookup_rows(local_ids, spans, vocab)
-        shares, rows = spread_tied(shares, rows)
+        shares, rows, rest_parts = spread_tied(shares, rows, rest_parts)
+        rest_columns = jnp.concatenate(in_order(rest_parts, fsdp_rank), axis=2)
+        rest_shares, rows = spread_tied(spread_begin(rest_columns), rows)
+        if steps:
+            rest_shares = spread_step(rest_shares, 0)
         first_placed = place_pieces(
             spread_end(shares), attention_groups(0) + feed_groups(4), cuts_rank
         )
-        sizes = [room_source * part // 5 for part in (2, 3, 4, 5)]
+        sizes = [room_source * part // 10 for part in (4, 5, 6, 7, 8, 10)]
         fullest_source = jnp.int32(room_source)
         for index in range(len(shares_of) - 1, -1, -1):
             fullest_source = jnp.where(share == shares_of[index], most[2 * index], fullest_source)
@@ -1147,25 +1161,22 @@
             ],
             rows[:room_source],
         )
-        source_rows, target_rows, rest_parts = lax.optimization_barrier(
-            (source_rows, rows[room_source : room_source + room_target], rest_parts)
-        )
-        rest_columns = jnp.concatenate(in_order(rest_parts, fsdp_rank), axis=2)
-        rest_shares, first_placed = spread_tied(spread_begin(rest_columns), first_placed)
-        for step in range(steps):
+        rest_shares, source_rows, target_rows = spread_tied(
+            rest_shares, source_rows, rows[room_source : room_source + room_target]
+        )
+        for step in range(1, steps - 1):
             rest_shares = spread_step(rest_shares, step)
-        rest_pieces = spread_end(rest_shares)
-        rest_attention = place_pieces(
-            rest_pieces, attention_groups(0) + attention_groups(4), cuts_rank
-        )
-        rest_feed = place_pieces(rest_pieces, feed_groups(8), cuts_rank)
-        weights = (
-            first_placed[:3],
-            first_placed[3:],
-            rest_attention[:3],
-            rest_attention[3:],
-            rest_feed,
-        )
+        rest_arriving = spread_send(rest_shares, steps - 1) if steps > 1 else []
+
+        def decoder_weights(stream):
+            shares, arriving, stream = spread_tied(rest_shares, rest_arriving, stream)
+            if steps > 1:
+                shares = spread_receive(shares, arriving, steps - 1)
+            pieces = spread_end(shares)
+            attentions = place_pieces(pieces, attention_groups(0) + attention_groups(4), cuts_rank)
+            feeds = place_pieces(pieces, feed_groups(8), cuts_rank)
+            return stream, attentions[:3], attentions[3:], feeds
+
         target_rows = lax.psum(target_rows, "fsdp")
         source_stream = source_rows.astype(jnp.float32)
         target_stream = target_rows
@@ -1204,7 +1215,8 @@
                 target_stream,
                 gain_rows,
                 biases,
-                weights,
+                first_placed,
+                decoder_weights,
                 layout,
                 head,
                 fsdp_rank * blocks.shape[2],

time: 1050 us -> 1040 us (level); the launches traced: 1030 us -> 1060 us
  starting transfers between devices: 69.9 us -> 131 us
  waiting for transfers between devices: 200 us -> 180 us
  Pallas kernels: 185 us -> 170 us
    ppermute x27, starting transfers between devices: 53.6 us -> 114 us  [exchange(): lax.ppermute(array, 'cuts', [(i, i ^ mask) for i in range(lax.axis_size('...]
    ppermute x27, waiting for transfers between devices: 96 us -> 62.1 us  [exchange(): lax.ppermute(array, 'cuts', [(i, i ^ mask) for i in range(lax.axis_size('...]
    psum x1, waiting for transfers between devices: 54.7 us -> 66.5 us  [one_round(): lax.psum(table[:size], 'fsdp')]
    while x319 -> x345, local copies, waits for them, and re-layouts: 41.7 us -> 38.9 us
  transfers between devices with their start and end apart: 41 -> 41, of which waited for: 18 -> 17; matrix products, arithmetic and copies ran while one was open for 13% -> 13% of each run, Pallas kernels for 4% -> 5%
where the time goes in v4:
time: 1040 us; the launch traced here: 1060 us
  matrix products  254 us (24%)
  waiting for transfers between devices  180 us (17%)
  Pallas kernels  170 us (16%)
  starting transfers between devices  131 us (13%)
  local copies, waits for them, and re-layouts  124 us (12%)
  other arithmetic  104 us (10%)
  blocking collectives  56.9 us (5%)
  between operations  21.5 us (2%)
  loops' own time  17.6 us (2%)
    ppermute x27, starting transfers between devices, exchange(): lax.ppermute(array, 'cuts', [(i, i ^ mask) for i in range(lax.axis_size('...  114 us
    dot_general x13, matrix products, dot_nt(): lax.dot_general(left, right, (((1,), (1,)), ((), ())), preferred_element_...  68.1 us
    psum x1, waiting for transfers between devices, one_round(): lax.psum(table[:size], 'fsdp')  66.5 us
    ppermute x27, waiting for transfers between devices, exchange(): lax.ppermute(array, 'cuts', [(i, i ^ mask) for i in range(lax.axis_size('...  62.1 us
    ppermute x12, waiting for transfers between devices, shifted(): lax.ppermute(array, 'fsdp', [(i, (i + distance) % count) for i in range(c...  51.8 us
    dot_general x13, matrix products, dot(): return jnp.dot(left, right, preferred_element_type=jnp.float32)  50.1 us
    dot_general x11, matrix products, dot_tn(): lax.dot_general(left, right, (((0,), (0,)), ((), ())), preferred_element_...  40.6 us
    pallas_call x3, Pallas kernels, packed_backward(): pl.pallas_call(lambda *refs: backward_kernel(causal, biased, *refs), grid...  40.5 us
  transfers between devices with their start and end apart: 41, of which 17 were waited for; matrix products, arithmetic and copies ran while one was open for 13% of the time, Pallas kernels for 5%

profile of v4, /device:TPU:0, one launch (start us, length us, event | category | flops | bytes accessed | tf_op | source)
XLA Modules:
  0.0 1059.5 jit_solution(4353657371599860210)
XLA Ops:
  14.3 13.3 %all-gather.4 = s32[4,2,642]{2,1,0:T(2,128)S(1)} all-gather(s32[1,2,642]{2,1,0:T(2,128)S(1)} %add_bitcast_fusion), channel_id=1, replica_groups=mesh['cuts'=8,'fsdp'=4] {'fsdp'}, dimensions={0}, use_global_device_ids=true | all-gather | bytes 25680 | tf_op jit(solution)/shard_map/all_gather | solution.py:1013
  29.2 6.4 all-reduce.11
  60.6 34.7 %collective-permute-done.24 = bf16[12,96,192]{2,1,0:T(8,128)(2,1)} collective-permute-done((bf16[12,96,192]{2,1,0:T(8,128)(2,1)}, bf16[12,96,192]{2,1,0:T(8,128)(2,1)}, u32[]{:S(2)}, u32[]{:S(2)}) %collective-permute-start.24) | collective-permute-done | bytes 442400 | tf_op jit(solution)/shard_map/ppermute | solution.py:65
  110.0 17.8 %collective-permute-done.29 = bf16[1,6,96,768]{3,2,1,0:T(8,128)(2,1)} collective-permute-done((bf16[1,6,96,768]{3,2,1,0:T(8,128)(2,1)}, bf16[1,6,96,768]{3,2,1,0:T(8,128)(2,1)}, u32[]{:S(2)}, u32[]{:S(2)}) %collective-permute-start.29) | collective-permute-done | bytes 884768 | tf_op jit(solution)/shard_map/ppermute | solution.py:60
  134.7 656.4 %while.29 = (pred[]{:T(512)}, s32[]{:T(128)}, f32[]{:T(128)}, f32[]{:T(128)}, f32[28,192,768]{2,1,0:T(8,128)}, /*index=5*/f32[8032,768]{1,0:T(8,128)}, f32[7,768...) while((pred[]{:T(512)}, s32[]{:T(128)}, f32[]{:T(128)}, ...), condition=%wide.region_67.69_spmd, body=%wide.region_5.68_spmd.sunk | while | flops 170000547840 | bytes 2112565632 | solution.py:1246
  155.0 7.1 gather_fusion.2
  165.8 5.2 place.25.refs_2_
  175.5 18.7 %lookup.8 = bf16[1792,768]{1,0:T(8,128)(2,1)S(1)} custom-call(s32[3]{0:T(128)S(1)} %pad_add_fusion.4.refs_0_, s32[1792,1]{1,0:T(8,128)S(1)} %copy-done.16, bf16[768,8032]{1,0:T(8,128)(2,1)} %copy-done.1), custom_call_target="tpu_custom_call" | custom-call | flops 22108176384 | bytes 94371840 | tf_op jit(solution)/shard_map/while/body/lookup/pallas_call | solution.py:579
  209.3 6.7 collective-permute-start.8
  221.4 11.4 %collective-permute-start.7 = (bf16[1,8,96,768]{3,2,1,0:T(8,128)(2,1)}, bf16[1,8,96,768]{3,2,1,0:T(8,128)(2,1)}, u32[]{:S(2)}, u32[]{:S(2)}) collective-permute-start(bf16[1,8,96,768]{3,2,1,0:T(8,128)(2,1)} %get-tuple-element.1872), channel_id=1, source_target_pairs={{0,8},{4,12},{8,0},{12,4},{16,24},{20,28},{24,16},{28,20},{1,9},{5... | collective-permute-start | bytes 3538952 | tf_op jit(solution)/shard_map/while/body/ppermute | solution.py:60
  237.2 72.0 %conditional.2 = (bf16[1280,768]{1,0:T(8,128)(2,1)}) conditional(s32[]{:T(128)} %clamp.20, bf16[1280,768]{1,0:T(8,128)(2,1)} %slice.672, bf16[1280,768]{1,0:T(8,128)(2,1)} %slice.672, bf16[1280,768]{1,0:T(8,128)(2,1)} %slice.672, bf16[1280,768]{1,0:T(8,128)(2,1)} %slice.672, bf16[1280,768]{1,0:T(8,128)(2,1)} %slice.672, ...), branch_computations={%region_23.25_spmd, %region_25.27_spmd, %region_27.29_spmd, %regio... | conditional | flops 983040 | bytes 16121906 | solution.py:1154
  239.9 66.5 %all-reduce.28.cloned.1.call-done = bf16[1024,768]{1,0:T(8,128)(2,1)} async-done(((bf16[1024,768]{1,0:T(8,128)(2,1)}), bf16[1024,768]{1,0:T(8,128)(2,1)}) %all-reduce.28.cloned.1.call-update) | async-done | bytes 1572880 | tf_op jit(solution)/shard_map/while/body/cond/branch_4_fun/psum | solution.py:1158
  319.4 9.7 place.26
  334.0 6.4 convolution_convert_fusion.21.refs_3_.refs_4_.refs_5_
  340.5 6.6 attend.24
  351.2 15.3 %collective-permute-done.10 = bf16[2,8,96,768]{3,2,1,0:T(8,128)(2,1)} collective-permute-done((bf16[2,8,96,768]{3,2,1,0:T(8,128)(2,1)}, bf16[2,8,96,768]{3,2,1,0:T(8,128)(2,1)}, u32[]{:S(2)}, u32[]{:S(2)}) %collective-permute-start.10) | collective-permute-done | bytes 2359328 | tf_op jit(solution)/shard_map/while/body/ppermute | solution.py:60
  380.2 9.4 fusion.478
  389.6 13.1 %multiply_reduce_fusion.26 = (f32[1280]{0:T(1024)S(1)}, f32[1280,768]{1,0:T(8,128)S(1)}) fusion(f32[1280,768]{1,0:T(8,128)S(1)} %convert_add_fusion.4, bf16[3072,768]{1,0:T(8,128)(2,1)S(1)} %bitcast.355, f32[1280,3072]{1,0:T(8,128)} %fusion.478), kind=kOutput, calls=%fused_computation.61.clone.1 | convolution fusion | flops 6078135296 | bytes 28316672 | tf_op jit(solution)/shard_map/while/body/dot_general | solution.py:48
  443.6 13.9 %logits.8 = (f32[384,8032]{1,0:T(8,128)S(1)}, f32[384,128]{1,0:T(8,128)S(1)}) custom-call(s32[1]{0:T(128)} %bitcast.330.refs_0_, bf16[384,768]{1,0:T(8,128)(2,1)S(1)} %multiply_convert_fusion.36.refs_1_.final_ref, bf16[768,8032]{1,0:T(8,128)(2,1)} %copy-done.1, s32[384,1]{1,0:T(8,128)S(1)} %broadcast_in_dim.754.refs_3_), custom_call_target="tpu_custom_call" | custom-call | flops 4737466368 | bytes 41943040 | tf_op jit(solution)/shard_map/while/body/logits/pallas_call | solution.py:703
  462.1 13.4 %all-gather.6 = f32[4,3,384]{2,1,0:T(4,128)S(1)} all-gather(f32[1,3,384]{2,1,0:T(4,128)S(1)} %copy.347), channel_id=2, replica_groups=mesh['cuts'=8,'fsdp'=4] {'fsdp'}, dimensions={0}, use_global_device_ids=true | all-gather | bytes 23040 | tf_op jit(solution)/shard_map/while/body/all_gather | solution.py:1200
  476.2 17.1 %logit_grads.8 = (bf16[384,8032]{1,0:T(8,128)(2,1)S(1)}, f32[384,768]{1,0:T(8,128)S(1)}) custom-call(s32[1]{0:T(128)} %bitcast.330.refs_0_, f32[384,8032]{1,0:T(8,128)} %copy-done.2, bf16[768,8032]{1,0:T(8,128)(2,1)} %copy-done.1, s32[384,1]{1,0:T(8,128)S(1)} %broadcast_in_dim.754.refs_3_, f32[384,1]{1,0:T(8,128)S(1)} %add.2203.refs_4_, ...), custom_call_target="tpu_custom_call" | custom-call | flops 4737466368 | bytes 41943040 | tf_op jit(solution)/shard_map/while/body/logit_grads/pallas_call | solution.py:760
  503.1 5.4 collective-permute-done.14
  514.2 8.4 collective-permute-done.17
  527.0 8.5 fusion.490
  541.1 10.3 attend_back.24
  565.3 18.1 %fusion.493 = bf16[1280,3072]{1,0:T(8,128)(2,1)S(1)} fusion(f32[1280,3072]{1,0:T(8,128)} %fusion.478, bf16[1280,768]{1,0:T(8,128)(2,1)S(1)} %fusion.492, bf16[3072,768]{1,0:T(8,128)(2,1)} %get-tuple-element.1887), kind=kOutput, calls=%fused_computation.12.clone.1 | convolution fusion | flops 6118440960 | bytes 30277632 | tf_op jit(solution)/shard_map/while/body/dot_general | solution.py:52
  583.5 9.5 multiply_reduce_fusion.32
  593.0 9.6 attend_back.26
  608.9 6.6 constant_dynamic-slice_fusion.30
  615.5 10.9 %fusion.495 = f32[192,3072]{1,0:T(8,128)} fusion(bf16[1280,768]{1,0:T(8,128)(2,1)S(1)} %fusion.492, s32[]{:T(128)} %get-tuple-element.2165, f32[1280,3072]{1,0:T(8,128)} %fusion.478), kind=kOutput, calls=%fused_computation.158.clone.1 | convolution fusion | flops 1545338880 | bytes 18743300 | tf_op jit(solution)/shard_map/while/body/dot_general | solution.py:56
  637.7 8.6 fusion.494
  649.3 20.6 %attend_back.25 = (bf16[1280,768]{1,0:T(8,128)(2,1)}, bf16[1280,1536]{1,0:T(8,128)(2,1)}, f32[5,6,128,256]{3,2,1,0:T(8,128)}) custom-call(s32[10]{0:T(128)} %copy-done.29, s32[10]{0:T(128)} %copy-done.28, bf16[1280,768]{1,0:T(8,128)(2,1)} %copy-done.47, bf16[1280,768]{1,0:T(8,128)(2,1)} %convolution_convert_fusion.27.refs_3_, bf16[1280,1536]{1,0:T(8,128)(2,1)} %copy-done.48, ...), custom_call_target="tpu_custom_call" | custom-call | flops 25165824000 | bytes 41943040 | tf_op jit(solution)/shard_map/while/body/attend_back/pallas_call | solution.py:500
  678.3 5.5 fusion.501
  686.6 6.1 fusion.502
  736.8 18.4 %select_add_fusion.2 = f32[28,192,768]{2,1,0:T(8,128)} fusion(f32[28,192,768]{2,1,0:T(8,128)} %bitcast.331, f32[28,192,768]{2,1,0:T(8,128)} %get-tuple-element.1984, f32[28,192,768]{2,1,0:T(8,128)} %get-tuple-element.2074, pred[]{:T(512)S(6)} %eq.814), kind=kLoop, calls=%fused_computation.5.clone.1 | loop fusion | flops 8257536 | bytes 66060288 | tf_op jit(solution)/shard_map/while/body/add | solution.py:1237
  755.3 30.6 %vocab_grad.8 = f32[8032,768]{1,0:T(8,128)} custom-call(s32[4]{0:T(128)S(1)} %pad_add_fusion.5.blocks_ref, s32[1,1792]{1,0:T(1,128)S(1)} %broadcast_in_dim.755.id_ref, bf16[1792,768]{1,0:T(8,128)(2,1)S(1)} %fusion.504.grad_ref, bf16[384,8032]{1,0:T(8,128)(2,1)S(1)} %bitcast.335, bf16[384,768]{1,0:T(8,128)(2,1)S(1)} %copy-done.22, ...), custom_call_target="tpu_custom_call", output_to_operand_aliasing={{}: (6, {})} | custom-call | flops 26845642752 | bytes 104857600 | tf_op jit(solution)/shard_map/while/body/vocab_grad/pallas_call | solution.py:620
  791.1 7.9 convolution_bitcast_fusion
  799.0 10.8 %convolution_bitcast_fusion.4 = f32[8,1,768]{2,0,1:T(8,128)S(1)} fusion(f32[8032,768]{1,0:T(8,128)} %get-tuple-element.2389, f32[8032,8]{0,1:T(8,128)S(1)} %copy-done), kind=kOutput, calls=%fused_computation.434 | convolution fusion | flops 296091648 | bytes 24955904 | tf_op jit(solution)/shard_map/vd,vr->rd/dot_general | solution.py:1264
  815.7 47.5 %collective-permute-start.31 = (f32[64,768]{1,0:T(8,128)}, f32[64,768]{1,0:T(8,128)}, u32[]{:S(2)}, u32[]{:S(2)}) collective-permute-start(f32[64,768]{1,0:T(8,128)} %constant_dynamic-slice_fusion.22), channel_id=1, source_target_pairs={{0,8},{4,12},{8,0},{12,4},{16,24},{20,28},{24,16},{28,20},{1,9},{5... | collective-permute-start | bytes 589832 | tf_op jit(solution)/shard_map/ppermute | solution.py:60
  863.2 5.5 collective-permute-done.31
  870.3 27.4 %collective-permute-start.32 = (f32[32,768]{1,0:T(8,128)S(1)}, f32[32,768]{1,0:T(8,128)S(1)}, u32[]{:S(2)}, u32[]{:S(2)}) collective-permute-start(f32[32,768]{1,0:T(8,128)S(1)} %constant_dynamic-slice_fusion.21), channel_id=1, source_target_pairs={{0,16},{4,20},{8,24},{12,28},{16,0},{20,4},{24,8},{28,12},{1,17},{... | collective-permute-start | bytes 294920 | tf_op jit(solution)/shard_map/ppermute | solution.py:60
  901.4 15.0 %all-gather.2 = f32[128,768]{1,0:T(8,128)S(1)} all-gather(f32[32,768]{1,0:T(8,128)S(1)} %dynamic-slice_add_fusion.1), channel_id=4, replica_groups=mesh['cuts'=8,'fsdp'=4] {'fsdp'}, dimensions={0}, use_global_device_ids=true | all-gather | bytes 491520 | tf_op jit(solution)/shard_map/all_gather | solution.py:105
  946.0 8.2 fusion.170
  954.4 11.4 %convolution_convert_fusion.9 = bf16[8,8032]{1,0:T(8,128)(2,1)S(1)} fusion(f32[8032,768]{1,0:T(8,128)} %get-tuple-element.2389, f32[8,1,768]{2,1,0:T(1,128)S(1)} %slice.538), kind=kOutput, calls=%fused_computation.414 | convolution fusion | flops 98697216 | bytes 24827392 | tf_op jit(solution)/shard_map/vd,rd->rv/dot_general | solution.py:1286
  981.7 16.4 %subtract_bitcast_fusion = f32[1,8032,768]{2,1,0:T(8,128)} fusion(f32[8032,768]{1,0:T(8,128)} %get-tuple-element.2389, f32[8,13408]{1,0:T(8,128)S(1)} %convert_add_fusion.2, f32[8,1,768]{2,1,0:T(1,128)S(1)} %slice.538), kind=kOutput, calls=%fused_computation.408 | convolution fusion | flops 104865792 | bytes 49502208 | tf_op jit(solution)/shard_map/rv,rd->vd/dot_general | solution.py:1298
  1002.2 14.6 %subtract_bitcast_fusion.1 = f32[1,768,28,192]{1,3,2,0:T(8,128)} fusion(f32[28,192,768]{2,1,0:T(8,128)} %get-tuple-element.2388, f32[8,28,768]{2,1,0:T(8,128)} %bitcast.341, f32[8,28,192]{2,1,0:T(8,128)S(1)} %reshape.832), kind=kOutput, calls=%fused_computation.409 | convolution fusion | flops 70189056 | bytes 33890304 | tf_op jit(solution)/shard_map/rki,rkj->kji/dot_general | solution.py:1297
  1016.8 8.8 psum.63
  1044.1 5.8 multiply_subtract_fusion
  (749 shorter events, 371.6 us)
Async XLA Ops:
  7.2 791.8 %copy-start = (f32[8032,8]{0,1:T(8,128)S(1)}, f32[8032,8]{0,1:T(8,128)}, u32[]{:S(2)}) copy-start(f32[8032,8]{0,1:T(8,128)} %param.43) | copy-start | bytes 771076
  9.5 26.2 %collective-permute-start.19 = (bf16[1,1,48,8032]{3,2,1,0:T(8,128)(2,1)S(1)}, bf16[1,1,48,8032]{3,2,1,0:T(8,128)(2,1)}, u32[]{:S(2)}, u32[]{:S(2)}) collective-permute-start(bf16[1,1,48,8032]{3,2,1,0:T(8,128)(2,1)S(1)} %get-tuple-element.1394), channel_id=1, source_target_pairs={{0,8},{4,12},{8,0},{12,4},{16,24},{20,28},{24,16},{28,20},{1,9},{5... | collective-permute-start | bytes 2313224 | tf_op jit(solution)/shard_map/ppermute | solution.py:60
  12.5 24.9 %collective-permute-start.20 = (bf16[1,1,48,8032]{3,2,1,0:T(8,128)(2,1)S(1)}, bf16[1,1,48,8032]{3,2,1,0:T(8,128)(2,1)}, u32[]{:S(2)}, u32[]{:S(2)}) collective-permute-start(bf16[1,1,48,8032]{3,2,1,0:T(8,128)(2,1)S(1)} %get-tuple-element.1393), channel_id=1, source_target_pairs={{0,16},{4,20},{8,24},{12,28},{16,0},{20,4},{24,8},{28,12},{1,17},{... | collective-permute-start | bytes 2313224 | tf_op jit(solution)/shard_map/ppermute | solution.py:60
  40.4 57.6 %collective-permute-start.21 = (bf16[2,1,48,8032]{3,2,1,0:T(8,128)(2,1)S(1)}, bf16[2,1,48,8032]{3,2,1,0:T(8,128)(2,1)}, u32[]{:S(2)}, u32[]{:S(2)}) collective-permute-start(bf16[2,1,48,8032]{3,2,1,0:T(8,128)(2,1)S(1)} %pad_maximum_fusion.13), channel_id=1, source_target_pairs={{0,16},{4,20},{8,24},{12,28},{16,0},{20,4},{24,8},{28,12},{1,17},{... | collective-permute-start | bytes 4626440 | tf_op jit(solution)/shard_map/ppermute | solution.py:60
  43.1 17.5 %collective-permute-start.23 = (bf16[12,96,192]{2,1,0:T(8,128)(2,1)}, bf16[12,96,192]{2,1,0:T(8,128)(2,1)}, u32[]{:S(2)}, u32[]{:S(2)}) collective-permute-start(bf16[12,96,192]{2,1,0:T(8,128)(2,1)} %slice.499), channel_id=1, source_target_pairs={{0,3},{1,0},{2,1},{3,2},{4,7},{5,4},{6,5},{7,6},{8,11},{9,8},{10,9... | collective-permute-start | bytes 1327112 | tf_op jit(solution)/shard_map/ppermute | solution.py:65
  46.5 48.8 %collective-permute-start.24 = (bf16[12,96,192]{2,1,0:T(8,128)(2,1)}, bf16[12,96,192]{2,1,0:T(8,128)(2,1)}, u32[]{:S(2)}, u32[]{:S(2)}) collective-permute-start(bf16[12,96,192]{2,1,0:T(8,128)(2,1)} %slice.499), channel_id=1, source_target_pairs={{0,2},{1,3},{2,0},{3,1},{4,6},{5,7},{6,4},{7,5},{8,10},{9,11},{10,... | collective-permute-start | bytes 1327112 | tf_op jit(solution)/shard_map/ppermute | solution.py:65
  46.5 48.8 %collective-permute-start.25 = (bf16[12,96,192]{2,1,0:T(8,128)(2,1)}, bf16[12,96,192]{2,1,0:T(8,128)(2,1)}, u32[]{:S(2)}, u32[]{:S(2)}) collective-permute-start(bf16[12,96,192]{2,1,0:T(8,128)(2,1)} %slice.499), channel_id=1, source_target_pairs={{0,1},{1,2},{2,3},{3,0},{4,5},{5,6},{6,7},{7,4},{8,9},{9,10},{10,1... | collective-permute-start | bytes 1327112 | tf_op jit(solution)/shard_map/ppermute | solution.py:65
  47.3 52.9 %collective-permute-start.22 = (bf16[2,1,48,8032]{3,2,1,0:T(8,128)(2,1)}, bf16[2,1,48,8032]{3,2,1,0:T(8,128)(2,1)}, u32[]{:S(2)}, u32[]{:S(2)}) collective-permute-start(bf16[2,1,48,8032]{3,2,1,0:T(8,128)(2,1)} %pad_maximum_fusion.14), channel_id=1, source_target_pairs={{0,8},{4,12},{8,0},{12,4},{16,24},{20,28},{24,16},{28,20},{1,9},{5... | collective-permute-start | bytes 4626440 | tf_op jit(solution)/shard_map/ppermute | solution.py:60
  104.1 29.4 %collective-permute-start.26 = (bf16[4,1,48,8032]{3,2,1,0:T(8,128)(2,1)S(1)}, bf16[4,1,48,8032]{3,2,1,0:T(8,128)(2,1)}, u32[]{:S(2)}, u32[]{:S(2)}) collective-permute-start(bf16[4,1,48,8032]{3,2,1,0:T(8,128)(2,1)S(1)} %pad_maximum_fusion.8), channel_id=1, source_target_pairs={{0,4},{4,0},{8,12},{12,8},{16,20},{20,16},{24,28},{28,24},{1,5},{5... | collective-permute-start | bytes 9252872 | tf_op jit(solution)/shard_map/ppermute | solution.py:60
  104.1 29.4 %collective-permute-start.27 = (bf16[4,1,48,8032]{3,2,1,0:T(8,128)(2,1)}, bf16[4,1,48,8032]{3,2,1,0:T(8,128)(2,1)}, u32[]{:S(2)}, u32[]{:S(2)}) collective-permute-start(bf16[4,1,48,8032]{3,2,1,0:T(8,128)(2,1)} %pad_maximum_fusion.9), channel_id=1, source_target_pairs={{0,4},{4,0},{8,12},{12,8},{16,20},{20,16},{24,28},{28,24},{1,5},{5... | collective-permute-start | bytes 9252872 | tf_op jit(solution)/shard_map/ppermute | solution.py:60
  105.9 21.9 %collective-permute-start.29 = (bf16[1,6,96,768]{3,2,1,0:T(8,128)(2,1)}, bf16[1,6,96,768]{3,2,1,0:T(8,128)(2,1)}, u32[]{:S(2)}, u32[]{:S(2)}) collective-permute-start(bf16[1,6,96,768]{3,2,1,0:T(8,128)(2,1)} %get-tuple-element.1391), channel_id=1, source_target_pairs={{0,16},{4,20},{8,24},{12,28},{16,0},{20,4},{24,8},{28,12},{1,17},{... | collective-permute-start | bytes 2654216 | tf_op jit(solution)/shard_map/ppermute | solution.py:60
  106.6 24.0 %collective-permute-start.28 = (bf16[1,6,96,768]{3,2,1,0:T(8,128)(2,1)}, bf16[1,6,96,768]{3,2,1,0:T(8,128)(2,1)}, u32[]{:S(2)}, u32[]{:S(2)}) collective-permute-start(bf16[1,6,96,768]{3,2,1,0:T(8,128)(2,1)} %get-tuple-element.1392), channel_id=1, source_target_pairs={{0,8},{4,12},{8,0},{12,4},{16,24},{20,28},{24,16},{28,20},{1,9},{5... | collective-permute-start | bytes 2654216 | tf_op jit(solution)/shard_map/ppermute | solution.py:60
  134.9 66.5 %collective-permute-start.2 = (bf16[16,96,192]{2,1,0:T(8,128)(2,1)}, bf16[16,96,192]{2,1,0:T(8,128)(2,1)}, u32[]{:S(2)}, u32[]{:S(2)}) collective-permute-start(bf16[16,96,192]{2,1,0:T(8,128)(2,1)} %get-tuple-element.1864), channel_id=1, source_target_pairs={{0,1},{1,2},{2,3},{3,0},{4,5},{5,6},{6,7},{7,4},{8,9},{9,10},{10,1... | collective-permute-start | bytes 1769480 | tf_op jit(solution)/shard_map/while/body/ppermute | solution.py:65
  135.5 66.0 %collective-permute-start.3 = (bf16[16,96,192]{2,1,0:T(8,128)(2,1)}, bf16[16,96,192]{2,1,0:T(8,128)(2,1)}, u32[]{:S(2)}, u32[]{:S(2)}) collective-permute-start(bf16[16,96,192]{2,1,0:T(8,128)(2,1)} %get-tuple-element.1864), channel_id=1, source_target_pairs={{0,2},{1,3},{2,0},{3,1},{4,6},{5,7},{6,4},{7,5},{8,10},{9,11},{10,... | collective-permute-start | bytes 1769480 | tf_op jit(solution)/shard_map/while/body/ppermute | solution.py:65
  137.5 64.0 %collective-permute-start.4 = (bf16[16,96,192]{2,1,0:T(8,128)(2,1)}, bf16[16,96,192]{2,1,0:T(8,128)(2,1)}, u32[]{:S(2)}, u32[]{:S(2)}) collective-permute-start(bf16[16,96,192]{2,1,0:T(8,128)(2,1)} %get-tuple-element.1864), channel_id=1, source_target_pairs={{0,3},{1,0},{2,1},{3,2},{4,7},{5,4},{6,5},{7,6},{8,11},{9,8},{10,9... | collective-permute-start | bytes 1769480 | tf_op jit(solution)/shard_map/while/body/ppermute | solution.py:65
  140.3 53.9 %collective-permute-start = (bf16[2,6,96,768]{3,2,1,0:T(8,128)(2,1)}, bf16[2,6,96,768]{3,2,1,0:T(8,128)(2,1)}, u32[]{:S(2)}, u32[]{:S(2)}) collective-permute-start(bf16[2,6,96,768]{3,2,1,0:T(8,128)(2,1)} %get-tuple-element.1843), channel_id=1, source_target_pairs={{0,16},{4,20},{8,24},{12,28},{16,0},{20,4},{24,8},{28,12},{1,17},{... | collective-permute-start | bytes 5308424 | tf_op jit(solution)/shard_map/while/body/ppermute | solution.py:60
  141.2 56.7 %collective-permute-start.1 = (bf16[2,6,96,768]{3,2,1,0:T(8,128)(2,1)}, bf16[2,6,96,768]{3,2,1,0:T(8,128)(2,1)}, u32[]{:S(2)}, u32[]{:S(2)}) collective-permute-start(bf16[2,6,96,768]{3,2,1,0:T(8,128)(2,1)} %get-tuple-element.1844), channel_id=1, source_target_pairs={{0,8},{4,12},{8,0},{12,4},{16,24},{20,28},{24,16},{28,20},{1,9},{5... | collective-permute-start | bytes 5308424 | tf_op jit(solution)/shard_map/while/body/ppermute | solution.py:60
  201.5 117.9 %collective-permute-start.5 = (bf16[4,6,96,768]{3,2,1,0:T(8,128)(2,1)}, bf16[4,6,96,768]{3,2,1,0:T(8,128)(2,1)}, u32[]{:S(2)}, u32[]{:S(2)}) collective-permute-start(bf16[4,6,96,768]{3,2,1,0:T(8,128)(2,1)} %pad_maximum_fusion.24.refs_1_), channel_id=1, source_target_pairs={{0,4},{4,0},{8,12},{12,8},{16,20},{20,16},{24,28},{28,24},{1,5},{5... | collective-permute-start | bytes 10616840 | tf_op jit(solution)/shard_map/while/body/ppermute | solution.py:60
  201.6 117.8 %collective-permute-start.6 = (bf16[4,6,96,768]{3,2,1,0:T(8,128)(2,1)}, bf16[4,6,96,768]{3,2,1,0:T(8,128)(2,1)}, u32[]{:S(2)}, u32[]{:S(2)}) collective-permute-start(bf16[4,6,96,768]{3,2,1,0:T(8,128)(2,1)} %pad_maximum_fusion.25.refs_3_), channel_id=1, source_target_pairs={{0,4},{4,0},{8,12},{12,8},{16,20},{20,16},{24,28},{28,24},{1,5},{5... | collective-permute-start | bytes 10616840 | tf_op jit(solution)/shard_map/while/body/ppermute | solution.py:60
  209.3 99.9 %collective-permute-start.8 = (bf16[1,8,96,768]{3,2,1,0:T(8,128)(2,1)}, bf16[1,8,96,768]{3,2,1,0:T(8,128)(2,1)}, u32[]{:S(2)}, u32[]{:S(2)}) collective-permute-start(bf16[1,8,96,768]{3,2,1,0:T(8,128)(2,1)} %get-tuple-element.1873), channel_id=1, source_target_pairs={{0,16},{4,20},{8,24},{12,28},{16,0},{20,4},{24,8},{28,12},{1,17},{... | collective-permute-start | bytes 3538952 | tf_op jit(solution)/shard_map/while/body/ppermute | solution.py:60
  216.1 209.3 %copy-start.24 = (s32[1,384]{1,0:T(1,128)}, s32[1,384]{1,0:T(1,128)S(1)}, u32[]{:S(2)}) copy-start(s32[1,384]{1,0:T(1,128)S(1)} %broadcast_in_dim.752.refs_5_.refs_7_) | copy-start | bytes 4612 | tf_op jit(solution)/shard_map/while
  221.4 191.7 %copy-start.124 = (f32[768]{0:T(1024)}, f32[768]{0:T(1024)S(1)}, u32[]{:S(2)}) copy-start(f32[768]{0:T(1024)S(1)} %get-tuple-element.1911) | copy-start | bytes 9220 | tf_op jit(solution)/shard_map/while
  221.4 91.0 %collective-permute-start.7 = (bf16[1,8,96,768]{3,2,1,0:T(8,128)(2,1)}, bf16[1,8,96,768]{3,2,1,0:T(8,128)(2,1)}, u32[]{:S(2)}, u32[]{:S(2)}) collective-permute-start(bf16[1,8,96,768]{3,2,1,0:T(8,128)(2,1)} %get-tuple-element.1872), channel_id=1, source_target_pairs={{0,8},{4,12},{8,0},{12,4},{16,24},{20,28},{24,16},{28,20},{1,9},{5... | collective-permute-start | bytes 3538952 | tf_op jit(solution)/shard_map/while/body/ppermute | solution.py:60
  234.2 179.7 %copy-start.26 = (s32[3]{0:T(128)}, s32[3]{0:T(128)S(1)}, u32[]{:S(2)}) copy-start(s32[3]{0:T(128)S(1)} %get-tuple-element.1907.refs_1_) | copy-start | bytes 40 | tf_op jit(solution)/shard_map/while
  234.2 179.7 %copy-start.27 = (s32[3]{0:T(128)}, s32[3]{0:T(128)S(1)}, u32[]{:S(2)}) copy-start(s32[3]{0:T(128)S(1)} %get-tuple-element.1906.refs_0_) | copy-start | bytes 40 | tf_op jit(solution)/shard_map/while
  234.9 190.5 %copy-start.30 = (s32[3]{0:T(128)}, s32[3]{0:T(128)S(1)}, u32[]{:S(2)}) copy-start(s32[3]{0:T(128)S(1)} %get-tuple-element.1898.refs_1_) | copy-start | bytes 40 | tf_op jit(solution)/shard_map/while
  234.9 190.5 %copy-start.31 = (s32[3]{0:T(128)}, s32[3]{0:T(128)S(1)}, u32[]{:S(2)}) copy-start(s32[3]{0:T(128)S(1)} %get-tuple-element.1897.refs_0_) | copy-start | bytes 40 | tf_op jit(solution)/shard_map/while
  237.2 69.2 %all-reduce.28.cloned.1.call-start = ((), (), s32[]{:S(2)}) async-start(), calls=%async_computation.4 | async-start | bytes 3145728 | tf_op jit(solution)/shard_map/while/body/cond/branch_4_fun/psum | solution.py:1158
  309.2 97.0 %all-reduce.32.cloned.1.call-start = ((), (), s32[]{:S(2)}) async-start(), calls=%async_computation.6 | async-start | bytes 1179648 | tf_op jit(solution)/shard_map/while/body/psum | solution.py:1180
  314.3 52.2 %collective-permute-start.10 = (bf16[2,8,96,768]{3,2,1,0:T(8,128)(2,1)}, bf16[2,8,96,768]{3,2,1,0:T(8,128)(2,1)}, u32[]{:S(2)}, u32[]{:S(2)}) collective-permute-start(bf16[2,8,96,768]{3,2,1,0:T(8,128)(2,1)} %pad_maximum_fusion.28), channel_id=1, source_target_pairs={{0,8},{4,12},{8,0},{12,4},{16,24},{20,28},{24,16},{28,20},{1,9},{5... | collective-permute-start | bytes 7077896 | tf_op jit(solution)/shard_map/while/body/ppermute | solution.py:60
  315.9 51.7 %collective-permute-start.9 = (bf16[2,8,96,768]{3,2,1,0:T(8,128)(2,1)S(1)}, bf16[2,8,96,768]{3,2,1,0:T(8,128)(2,1)}, u32[]{:S(2)}, u32[]{:S(2)}) collective-permute-start(bf16[2,8,96,768]{3,2,1,0:T(8,128)(2,1)S(1)} %pad_maximum_fusion.27), channel_id=1, source_target_pairs={{0,16},{4,20},{8,24},{12,28},{16,0},{20,4},{24,8},{28,12},{1,17},{... | collective-permute-start | bytes 7077896 | tf_op jit(solution)/shard_map/while/body/ppermute | solution.py:60
  373.9 33.5 %collective-permute-start.12 = (bf16[4,8,96,768]{3,2,1,0:T(8,128)(2,1)}, bf16[4,8,96,768]{3,2,1,0:T(8,128)(2,1)}, u32[]{:S(2)}, u32[]{:S(2)}) collective-permute-start(bf16[4,8,96,768]{3,2,1,0:T(8,128)(2,1)} %constant_dynamic-update-slice_fusion.11.refs_3_), channel_id=1, source_target_pairs={{0,4},{4,0},{8,12},{12,8},{16,20},{20,16},{24,28},{28,24},{1,5},{5... | collective-permute-start | bytes 14155784 | tf_op jit(solution)/shard_map/while/body/ppermute | solution.py:60
  379.3 28.2 %collective-permute-start.11 = (bf16[4,8,96,768]{3,2,1,0:T(8,128)(2,1)}, bf16[4,8,96,768]{3,2,1,0:T(8,128)(2,1)}, u32[]{:S(2)}, u32[]{:S(2)}) collective-permute-start(bf16[4,8,96,768]{3,2,1,0:T(8,128)(2,1)} %constant_dynamic-update-slice_fusion.9.refs_1_), channel_id=1, source_target_pairs={{0,4},{4,0},{8,12},{12,8},{16,20},{20,16},{24,28},{28,24},{1,5},{5... | collective-permute-start | bytes 14155784 | tf_op jit(solution)/shard_map/while/body/ppermute | solution.py:60
  496.1 7.0 collective-permute-start.13
  498.7 9.8 collective-permute-start.14
  498.7 9.8 collective-permute-start.15
  508.6 5.6 collective-permute-start.16
  509.7 12.8 %collective-permute-start.17 = (bf16[96,768]{1,0:T(8,128)(2,1)S(1)}, bf16[96,768]{1,0:T(8,128)(2,1)S(1)}, u32[]{:S(2)}, u32[]{:S(2)}) collective-permute-start(bf16[96,768]{1,0:T(8,128)(2,1)S(1)} %add_convert_fusion.4), channel_id=1, source_target_pairs={{0,2},{1,3},{2,0},{3,1},{4,6},{5,7},{6,4},{7,5},{8,10},{9,11},{10,... | collective-permute-start | bytes 442376 | tf_op jit(solution)/shard_map/while/body/ppermute | solution.py:65
  510.5 12.0 %collective-permute-start.18 = (bf16[96,768]{1,0:T(8,128)(2,1)S(1)}, bf16[96,768]{1,0:T(8,128)(2,1)}, u32[]{:S(2)}, u32[]{:S(2)}) collective-permute-start(bf16[96,768]{1,0:T(8,128)(2,1)S(1)} %add_convert_fusion.4), channel_id=1, source_target_pairs={{0,1},{1,2},{2,3},{3,0},{4,5},{5,6},{6,7},{7,4},{8,9},{9,10},{10,1... | collective-permute-start | bytes 442376 | tf_op jit(solution)/shard_map/while/body/ppermute | solution.py:65
  811.9 1.9 collective-permute-start.30
  815.7 53.0 %collective-permute-start.31 = (f32[64,768]{1,0:T(8,128)}, f32[64,768]{1,0:T(8,128)}, u32[]{:S(2)}, u32[]{:S(2)}) collective-permute-start(f32[64,768]{1,0:T(8,128)} %constant_dynamic-slice_fusion.22), channel_id=1, source_target_pairs={{0,8},{4,12},{8,0},{12,4},{16,24},{20,28},{24,16},{28,20},{1,9},{5... | collective-permute-start | bytes 589832 | tf_op jit(solution)/shard_map/ppermute | solution.py:60
  870.3 30.2 %collective-permute-start.32 = (f32[32,768]{1,0:T(8,128)S(1)}, f32[32,768]{1,0:T(8,128)S(1)}, u32[]{:S(2)}, u32[]{:S(2)}) collective-permute-start(f32[32,768]{1,0:T(8,128)S(1)} %constant_dynamic-slice_fusion.21), channel_id=1, source_target_pairs={{0,16},{4,20},{8,24},{12,28},{16,0},{20,4},{24,8},{28,12},{1,17},{... | collective-permute-start | bytes 294920 | tf_op jit(solution)/shard_map/ppermute | solution.py:60
  917.0 4.8 collective-permute-start.33
  922.9 5.8 collective-permute-start.34
  930.0 7.4 collective-permute-start.35
  965.8 2.0 collective-permute-start.36
  967.9 7.3 collective-permute-start.37
  975.2 6.4 collective-permute-start.38
  (190 other events, 2619.2 us)
Sparse Core Ops, SparseCore 0:
  241.0 65.3 all-reduce.27
  317.5 36.1 all-reduce.31
